TPU v7x, 128 devices: a whole 4x4x4 slice. The times are simulated.
128 devices in a mesh: dp: 32 (over x, y, core), tensor: 4 (over z).
Axes of the slice: x: 4, y: 4, z: 4, core: 2. Of those that a mesh axis runs over, the one named last changes fastest.
Arguments:
- hidden: bfloat16 [16384, 8192], P('dp', 'tensor'), may hold values from -6 to 6
- key_weight_frozen: bfloat16 [8192, 1024], P(None, 'tensor'), may hold values from -0.0625 to 0.0625
- value_weight_frozen: bfloat16 [8192, 1024], P(None, 'tensor'), may hold values from -0.0625 to 0.0625
- adapter_down_maps: bfloat16 [64, 2, 16, 8192], P('dp', None, None, 'tensor'), may hold values from -0.0625 to 0.0625
- adapter_up_maps: bfloat16 [64, 2, 16, 1024], P('dp', None, None, 'tensor'), may hold values from -0.375 to 0.375
- block_adapter_index: int32 [128], P('dp'), may hold values from 0 to 63
- segment_document_index: int32 [32, 512], P('dp'), may hold values from 0 to 15, never falling along the last dimension, each value on 1 to 256 neighbouring positions
- adapter_position: int32 [64], replicated, may hold values from 0 to 63, each once
- key_gradient: bfloat16 [16384, 1024], P('dp', 'tensor'), may hold values from -1.5 to 1.5
- value_gradient: bfloat16 [16384, 1024], P('dp', 'tensor'), may hold values from -1.5 to 1.5
Outputs:
- key_out: bfloat16 [16384, 1024], P('dp', 'tensor')
- value_output: bfloat16 [16384, 1024], P('dp', 'tensor')
- hidden_gradient: bfloat16 [16384, 8192], P('dp', 'tensor')
- grad_down: float32 [64, 2, 16, 8192], P('dp', None, None, 'tensor')
- grad_up: float32 [64, 2, 16, 1024], P('dp', None, None, 'tensor')
Inputs may be any that keep to these rules, and one draw needn't show every extreme that they name: `block_adapter_index`: adapter of each block of 128 tokens. `segment_document_index`: in each row, document numbers never fall, each document has 1 to 256 tokens and one has exactly 256. A permutation: adapter a's weights and gradients sit at index adapter_position[a] of adapter_down_maps, adapter_up_maps, grad_down and grad_up.
All inputs are finite; a program needn't handle non-finite values.
Results may differ from a plain program's by a relative error of at most 0.022.
Values may be sent and summed in bfloat16 or wider, within the bound.
No kernel may reach another device: no remote copies, remote signals or barrier semaphores. Data moves between devices by JAX's collectives and lax.ppermute only.
A program may use at most 192 MiB of HBM per device.

v0:
```python
import math

import jax
import jax.numpy as jnp
from jax import lax
from jax.sharding import PartitionSpec as P

HEAD = 128


adapter_scale = 0.5
rope_theta = 500000.0


def rope_tables(segments):
    places = jnp.arange(segments.shape[1], dtype=jnp.int32)
    earlier = jnp.concatenate([segments[:, :1] - 1, segments[:, :-1]], axis=1)
    starts = lax.cummax(jnp.where(segments != earlier, places[None, :], 0), axis=1)
    position = (places[None, :] - starts).astype(jnp.float32).reshape(-1)
    halves = jnp.arange(HEAD // 2, dtype=jnp.float32)
    inverse = jnp.exp(halves * (-2.0 * math.log(rope_theta) / HEAD))
    angles = position[:, None] * inverse[None, :]
    return (jnp.cos(angles), jnp.sin(angles))


def rotate(values, cosine, sine):
    leading = values[..., : HEAD // 2]
    trailing = values[..., HEAD // 2 :]
    cosine = cosine[:, None, :]
    sine = sine[:, None, :]
    return jnp.concatenate(
        [leading * cosine - trailing * sine, trailing * cosine + leading * sine], axis=-1
    )


def unrotate(values, cosine, sine):
    leading = values[..., : HEAD // 2]
    trailing = values[..., HEAD // 2 :]
    cosine = cosine[:, None, :]
    sine = sine[:, None, :]
    return jnp.concatenate(
        [leading * cosine + trailing * sine, trailing * cosine - leading * sine], axis=-1
    )


def per_device(
    hidden,
    key_weight_frozen,
    value_weight_frozen,
    adapter_down_maps,
    adapter_up_maps,
    block_adapter_index,
    segment_document_index,
    adapter_position,
    key_gradient,
    value_gradient,
):
    rows_here = hidden.shape[0]
    width_here = hidden.shape[1]
    kv_here = key_weight_frozen.shape[1]
    heads_here = kv_here // HEAD
    blocks_here = block_adapter_index.shape[0]
    block_rows = rows_here // blocks_here
    cosine, sine = rope_tables(segment_document_index)
    columns = lax.all_gather(hidden, "tensor", axis=1, tiled=True)
    key_baseline = jnp.dot(columns, key_weight_frozen, preferred_element_type=jnp.float32)
    value_baseline = jnp.dot(columns, value_weight_frozen, preferred_element_type=jnp.float32)
    all_down, all_up = (
        lax.all_gather(adapter_down_maps, "dp", axis=0, tiled=True),
        lax.all_gather(adapter_up_maps, "dp", axis=0, tiled=True),
    )
    slot_index_list = jnp.take(adapter_position, block_adapter_index, axis=0)
    block_down_maps = jnp.take(all_down, slot_index_list, axis=0)
    block_up_maps = jnp.take(all_up, slot_index_list, axis=0)
    blocked_tokens = hidden.reshape(blocks_here, block_rows, width_here)
    in_part = jnp.einsum(
        "qli,qogi->qlog", blocked_tokens, block_down_maps, preferred_element_type=jnp.float32
    )
    key_back = (
        unrotate(
            key_gradient.astype(jnp.float32).reshape(rows_here, heads_here, HEAD), cosine, sine
        )
        .reshape(rows_here, kv_here)
        .astype(jnp.bfloat16)
    )
    backward_terms = jnp.stack([key_back, value_gradient], axis=1).reshape(
        blocks_here, block_rows, 2, kv_here
    )
    inner_part = jnp.einsum(
        "oezl,ozal->oeza", backward_terms, block_up_maps, preferred_element_type=jnp.float32
    )
    input_sum_total, inner_total_sum = (
        lax.psum(in_part.astype(jnp.bfloat16), "tensor").astype(jnp.float32),
        lax.psum(inner_part.astype(jnp.bfloat16), "tensor").astype(jnp.float32),
    )
    adapter_input = input_sum_total.astype(jnp.bfloat16)
    inner_gradient = (inner_total_sum * adapter_scale).astype(jnp.bfloat16)
    adapter_added_output = (
        jnp.einsum(
            "ezwp,ewpu->ezwu", adapter_input, block_up_maps, preferred_element_type=jnp.float32
        ).reshape(rows_here, 2, kv_here)
        * adapter_scale
    )
    key_before_adapter = key_baseline + adapter_added_output[:, 0]
    key_out = (
        rotate(key_before_adapter.reshape(rows_here, heads_here, HEAD), cosine, sine)
        .reshape(rows_here, kv_here)
        .astype(jnp.bfloat16)
    )
    value_output = (value_baseline + adapter_added_output[:, 1]).astype(jnp.bfloat16)
    adapter_backward = jnp.einsum(
        "qvtx,qtxm->qvm", inner_gradient, block_down_maps, preferred_element_type=jnp.float32
    ).reshape(rows_here, width_here)
    dims = (((1,), (1,)), ((), ()))
    partial_terms = lax.dot_general(
        key_back, key_weight_frozen, dims, preferred_element_type=jnp.float32
    )
    partial_terms = partial_terms + lax.dot_general(
        value_gradient, value_weight_frozen, dims, preferred_element_type=jnp.float32
    )
    frozen_output = lax.psum_scatter(
        partial_terms.astype(jnp.bfloat16), "tensor", scatter_dimension=1, tiled=True
    ).astype(jnp.float32)
    hidden_gradient = (frozen_output + adapter_backward).astype(jnp.bfloat16)
    part_down = jnp.einsum(
        "nbjr,nbd->njrd", inner_gradient, blocked_tokens, preferred_element_type=jnp.float32
    )
    partial_up_map = (
        jnp.einsum(
            "qwth,qwtm->qthm", adapter_input, backward_terms, preferred_element_type=jnp.float32
        )
        * adapter_scale
    )
    adapter_count = all_down.shape[0]
    onehot = (
        slot_index_list[:, None] == jnp.arange(adapter_count, dtype=jnp.int32)[None, :]
    ).astype(jnp.float32)
    dense_down = jnp.einsum("na,njrd->ajrd", onehot, part_down, precision=lax.Precision.HIGHEST)
    dense_up = jnp.einsum("na,njrk->ajrk", onehot, partial_up_map, precision=lax.Precision.HIGHEST)
    grad_down, grad_up = (
        lax.psum_scatter(
            dense_down.astype(jnp.bfloat16), "dp", scatter_dimension=0, tiled=True
        ).astype(jnp.float32),
        lax.psum_scatter(
            dense_up.astype(jnp.bfloat16), "dp", scatter_dimension=0, tiled=True
        ).astype(jnp.float32),
    )
    return (key_out, value_output, hidden_gradient, grad_down, grad_up)


def solution(mesh):
    return jax.shard_map(
        per_device,
        mesh=mesh,
        in_specs=(
            P("dp", "tensor"),
            P(None, "tensor"),
            P(None, "tensor"),
            P("dp", None, None, "tensor"),
            P("dp", None, None, "tensor"),
            P("dp"),
            P("dp", None),
            P(),
            P("dp", "tensor"),
            P("dp", "tensor"),
        ),
        out_specs=(
            P("dp", "tensor"),
            P("dp", "tensor"),
            P("dp", "tensor"),
            P("dp", None, None, "tensor"),
            P("dp", None, None, "tensor"),
        ),
        check_vma=False,
    )
```

profile of v0, /device:TPU:1, one launch (start us, length us, event | category | flops | bytes accessed | tf_op | source)
XLA Modules:
  0.0 509.8 jit_solution(17744577238729689642)
XLA Ops:
  8.7 1.1 copy.50
  9.8 1.2 slice.32
  15.6 41.1 %all-gather.6.cloned.1.call-done = bf16[64,2,16,256]{3,2,1,0:T(8,128)(2,1)} async-done(((bf16[2,2,16,256]{3,2,1,0:T(8,128)(2,1)}), bf16[64,2,16,256]{3,2,1,0:T(8,128)(2,1)}) %all-gather.6.cloned.1.call-update) | async-done | bytes 1048592 | tf_op jit(solution)/shard_map/all_gather | solution.py:70
  56.6 1.8 gather_fusion.1
  59.3 51.7 %all-gather.8.cloned.1.call-done = bf16[64,2,16,2048]{3,2,1,0:T(8,128)(2,1)} async-done(((bf16[2,2,16,2048]{3,2,1,0:T(8,128)(2,1)}), bf16[64,2,16,2048]{3,2,1,0:T(8,128)(2,1)}) %all-gather.8.cloned.1.call-update) | async-done | bytes 8388624 | tf_op jit(solution)/shard_map/all_gather | solution.py:69
  111.0 4.0 gather_fusion.2
  115.0 1.5 fusion.3
  117.1 10.3 %fusion.24 = f32[512,8192]{1,0:T(8,128)} fusion(bf16[512,256]{0,1:T(8,128)(2,1)S(1)} %bitcast.67, bf16[8192,256]{1,0:T(8,128)(2,1)} %param.11), kind=kOutput, calls=%fused_computation.61 | convolution fusion | flops 2147483648 | bytes 21233664 | tf_op jit(solution)/shard_map/dot_general | solution.py:115
  127.5 12.8 %add_convert_fusion = bf16[512,8192]{1,0:T(8,128)(2,1)} fusion(f32[512,8192]{1,0:T(8,128)} %fusion.24, bf16[512,256]{1,0:T(8,128)(2,1)S(1)} %copy-done.4, bf16[8192,256]{1,0:T(8,128)(2,1)} %param.12), kind=kOutput, calls=%fused_computation.3 | convolution fusion | flops 2155872256 | bytes 29622272 | tf_op jit(solution)/shard_map/dot_general | solution.py:118
  140.4 14.7 %all-reduce.3.cloned.1.call-done = (bf16[4,128,2,16]{1,3,2,0:T(8,128)(2,1)}, bf16[4,128,2,16]{1,3,2,0:T(8,128)(2,1)}) async-done(((bf16[4,128,2,16]{1,3,2,0:T(8,128)(2,1)}, bf16[4,128,2,16]{1,3,2,0:T(8,128)(2,1)}), (bf16[4,128,2,16]{1,3,2,0:T(8,128)(2,1)}, bf16[4,128,2,16]{1,3,2,0:T(8,128)(2,1)})) %all-reduce.3.cloned.1.call-update) | async-done | bytes 65552 | tf_op jit(solution)/shard_map/psum | solution.py:93
  156.1 1.1 convolution_convert_fusion.1
  157.2 1.6 copy.42
  159.4 9.3 %convolution_convert_fusion = bf16[64,2,16,2048]{3,0,2,1:T(8,128)(2,1)} fusion(f32[4,2,16,2048]{3,2,1,0:T(8,128)S(1)} %fusion.8, s32[4]{0:T(128)S(1)} %get-tuple-element.23), kind=kOutput, calls=%fused_computation.4 | convolution fusion | flops 205521152 | bytes 9437200 | tf_op jit(solution)/shard_map/na,njrd->ajrd/dot_general | solution.py:138
  168.7 12.2 %copy.40 = bf16[64,2,16,2048]{3,2,1,0:T(8,128)(2,1)} copy(bf16[64,2,16,2048]{3,0,2,1:T(8,128)(2,1)} %convolution_convert_fusion) | data formatting | bytes 16777216 | tf_op jit(solution)/shard_map/convert_element_type | solution.py:142
  182.8 59.6 %all-gather.4.cloned.1.call-done = bf16[512,8192]{1,0:T(8,128)(2,1)} async-done(((bf16[512,2048]{1,0:T(8,128)(2,1)}), bf16[512,8192]{1,0:T(8,128)(2,1)}) %all-gather.4.cloned.1.call-update) | async-done | bytes 8388624 | tf_op jit(solution)/shard_map/all_gather | solution.py:65
  242.3 6.9 %convolution_add_fusion.1 = f32[512,256]{0,1:T(8,128)S(1)} fusion(bf16[512,8192]{1,0:T(8,128)(2,1)} %all-gather.4.cloned.1.call-done, bf16[8192,256]{1,0:T(8,128)(2,1)} %param.11, f32[512,2,256]{0,2,1:T(8,128)S(1)} %mul.109), kind=kOutput, calls=%fused_computation.11 | convolution fusion | flops 2147614720 | bytes 13631488 | tf_op jit(solution)/shard_map/dot_general | solution.py:66
  250.3 7.1 %fusion.2 = bf16[512,256]{0,1:T(8,128)(2,1)S(1)} fusion(bf16[512,8192]{1,0:T(8,128)(2,1)} %all-gather.4.cloned.1.call-done, bf16[8192,256]{1,0:T(8,128)(2,1)} %param.12, f32[512,2,256]{0,2,1:T(8,128)S(1)} %mul.109), kind=kOutput, calls=%fused_computation.12 | convolution fusion | flops 2147745792 | bytes 13369344 | tf_op jit(solution)/shard_map/dot_general | solution.py:67
  258.2 2.7 fusion.6
  261.0 65.5 %reduce-scatter.4.cloned.1.call-done = bf16[512,2048]{1,0:T(8,128)(2,1)} async-done(((bf16[512,8192]{1,0:T(8,128)(2,1)}), bf16[512,2048]{1,0:T(8,128)(2,1)}) %reduce-scatter.4.cloned.1.call-update) | async-done | bytes 2097168 | tf_op jit(solution)/shard_map/reduce_scatter | solution.py:121
  326.5 4.9 fusion
  331.4 74.2 %reduce-scatter.8.cloned.1.call-done = bf16[2,2,16,256]{3,2,1,0:T(8,128)(2,1)} async-done(((bf16[64,2,16,256]{3,2,1,0:T(8,128)(2,1)}), bf16[2,2,16,256]{3,2,1,0:T(8,128)(2,1)}) %reduce-scatter.8.cloned.1.call-update) | async-done | bytes 32784 | tf_op jit(solution)/shard_map/reduce_scatter | solution.py:144
  405.5 1.4 convert_element_type.94
  406.9 94.3 %reduce-scatter.6.cloned.1.call-done = bf16[2,2,16,2048]{3,2,1,0:T(8,128)(2,1)} async-done(((bf16[64,2,16,2048]{3,2,1,0:T(8,128)(2,1)}), bf16[2,2,16,2048]{3,2,1,0:T(8,128)(2,1)}) %reduce-scatter.6.cloned.1.call-update) | async-done | bytes 262160 | tf_op jit(solution)/shard_map/reduce_scatter | solution.py:141
  501.2 1.8 convert_element_type.92
  (63 shorter events, 12.3 us)
Async XLA Ops:
  7.2 7.7 %copy-start = (s32[64]{0:T(128)S(1)}, s32[64]{0:T(128)}, u32[]{:S(2)}) copy-start(s32[64]{0:T(128)} %param.17) | copy-start | bytes 772
  7.2 8.4 %copy-start.9 = (s32[4]{0:T(128)S(1)}, s32[4]{0:T(128)}, u32[]{:S(2)}) copy-start(s32[4]{0:T(128)} %param.15) | copy-start | bytes 52
  7.2 51.2 %copy-start.4 = (bf16[512,256]{1,0:T(8,128)(2,1)S(1)}, bf16[512,256]{1,0:T(8,128)(2,1)}, u32[]{:S(2)}) copy-start(bf16[512,256]{1,0:T(8,128)(2,1)} %param.19) | copy-start | bytes 786436
  7.2 107.8 %copy-start.2 = (bf16[512,2048]{1,0:T(8,128)(2,1)S(1)}, bf16[512,2048]{1,0:T(8,128)(2,1)}, u32[]{:S(2)}) copy-start(bf16[512,2048]{1,0:T(8,128)(2,1)} %param.10) | copy-start | bytes 6291460
  7.2 49.4 %all-gather.6.cloned.1.call-start = ((), (), s32[]{:S(2)}) async-start(), calls=%async_computation.4 | async-start | bytes 1081344 | tf_op jit(solution)/shard_map/all_gather | solution.py:70
  8.0 103.1 %all-gather.8.cloned.1.call-start = ((), (), s32[]{:S(2)}) async-start(), calls=%async_computation.5 | async-start | bytes 8650752 | tf_op jit(solution)/shard_map/all_gather | solution.py:69
  8.7 146.4 %all-reduce.3.cloned.1.call-start = ((), (), s32[]{:S(2)}) async-start(), calls=%async_computation.9 | async-start | bytes 131072 | tf_op jit(solution)/shard_map/psum | solution.py:93
  14.2 45.1 %copy-start.5 = (bf16[4,128,1,256]{3,1,2,0:T(8,128)(2,1)}, bf16[4,128,1,256]{3,1,2,0:T(8,128)(2,1)S(1)}, u32[]{:S(2)}) copy-start(bf16[4,128,1,256]{3,1,2,0:T(8,128)(2,1)S(1)} %copy.49) | copy-start | bytes 786436
  116.5 125.8 %all-gather.4.cloned.1.call-start = ((), (), s32[]{:S(2)}) async-start(), calls=%async_computation.3 | async-start | bytes 10485760 | tf_op jit(solution)/shard_map/all_gather | solution.py:65
  117.1 209.4 %reduce-scatter.4.cloned.1.call-start = ((), (), s32[]{:S(2)}) async-start(), calls=%async_computation.6 | async-start | bytes 10485760 | tf_op jit(solution)/shard_map/reduce_scatter | solution.py:121
  140.3 14.8 %copy-start.6 = (bf16[4,128,1,256]{3,1,2,0:T(8,128)(2,1)S(1)}, bf16[4,128,1,256]{3,1,2,0:T(8,128)(2,1)}, u32[]{:S(2)}) copy-start(bf16[4,128,1,256]{3,1,2,0:T(8,128)(2,1)} %copy-done.5) | copy-start | bytes 786436
  140.3 18.6 %copy-start.3 = (bf16[512,2048]{1,0:T(8,128)(2,1)S(1)}, bf16[512,2048]{1,0:T(8,128)(2,1)}, u32[]{:S(2)}) copy-start(bf16[512,2048]{1,0:T(8,128)(2,1)} %param.10) | copy-start | bytes 6291460
  140.4 265.2 %reduce-scatter.8.cloned.1.call-start = ((), (), s32[]{:S(2)}) async-start(), calls=%async_computation.8 | async-start | bytes 1081344 | tf_op jit(solution)/shard_map/reduce_scatter | solution.py:144
  155.1 3.9 copy-start.7
  158.7 342.5 %reduce-scatter.6.cloned.1.call-start = ((), (), s32[]{:S(2)}) async-start(), calls=%async_computation.7 | async-start | bytes 8650752 | tf_op jit(solution)/shard_map/reduce_scatter | solution.py:141
  180.8 0.8 copy-start.8
  258.2 244.8 %copy-start.1 = (s32[64]{0:T(128)S(1)}, s32[64]{0:T(128)}, u32[]{:S(2)}) copy-start(s32[64]{0:T(128)} %param.17) | copy-start | bytes 772
Sparse Core Ops, SparseCore 0:
  10.3 46.2 all-gather.5
  58.9 52.0 all-gather.7
  116.6 38.4 all-reduce.2
  156.7 85.5 all-gather.3
  244.8 81.6 reduce-scatter.3
  330.2 75.2 reduce-scatter.7
  409.3 91.9 reduce-scatter.5
where the time goes:
time: 511 us; the launch traced here: 510 us
  waiting for transfers between devices  403 us (79%)
  matrix products  54.4 us (11%)
  local copies, waits for them, and re-layouts  26.1 us (5%)
  between operations  15 us (3%)
  other arithmetic  10.9 us (2%)
    reduce_scatter x1, waiting for transfers between devices, per_device(): lax.psum_scatter(dense_down.astype(jnp.bfloat16), 'dp', scatter_dimension...  94.3 us
    reduce_scatter x1, waiting for transfers between devices, per_device(): lax.psum_scatter(dense_up.astype(jnp.bfloat16), 'dp', scatter_dimension=0...  74.2 us
    reduce_scatter x1, waiting for transfers between devices, per_device(): lax.psum_scatter(partial_terms.astype(jnp.bfloat16), 'tensor', scatter_di...  65.5 us
    all_gather x1, waiting for transfers between devices, per_device(): columns = lax.all_gather(hidden, 'tensor', axis=1, tiled=True)  59.6 us
    all_gather x1, waiting for transfers between devices, per_device(): lax.all_gather(adapter_down_maps, 'dp', axis=0, tiled=True)  51.7 us
    all_gather x1, waiting for transfers between devices, per_device(): lax.all_gather(adapter_up_maps, 'dp', axis=0, tiled=True)  41.1 us
    psum x1, waiting for transfers between devices, per_device(): lax.psum(in_part.astype(jnp.bfloat16), 'tensor').astype(jnp.float32)  14.7 us
    dot_general x1, matrix products, per_device(): lax.dot_general(value_gradient, value_weight_frozen, dims, preferred_elem...  12.8 us
  transfers between devices with their start and end apart: 7, of which 7 were waited for; matrix products, arithmetic and copies ran while one was open for 16% of the time, Pallas kernels for 0%

commit v1 on v0

v1 whole, which is shorter than its diff:
```python
import math

import jax
import jax.numpy as jnp
from jax import lax
from jax.experimental import pallas as pl
from jax.experimental.pallas import tpu as pltpu
from jax.sharding import PartitionSpec as P

HEAD = 128
SIDE = 4
SHIFTS = (1, -1, 2)

adapter_scale = 0.5
rope_theta = 500000.0
bf16 = jnp.bfloat16
f32 = jnp.float32
ANY = pl.BlockSpec(memory_space=pl.ANY)
VMEM = pl.BlockSpec(memory_space=pltpu.VMEM)
SMEM = pl.BlockSpec(memory_space=pltpu.SMEM)
NT = (((1,), (1,)), ((), ()))
TN = (((0,), (0,)), ((), ()))


def exchange(array, move):
    pairs = []
    for x in range(SIDE):
        for y in range(SIDE):
            for c in range(2):
                for z in range(SIDE):
                    x2, y2, c2, z2 = move(x, y, c, z)
                    target = (((x2 % SIDE) * SIDE + y2 % SIDE) * 2 + c2) * SIDE + z2 % SIDE
                    pairs.append((((x * SIDE + y) * 2 + c) * SIDE + z, target))
    return lax.ppermute(array, ("dp", "tensor"), pairs)


def along_z(array, shift):
    return exchange(array, lambda x, y, c, z: (x, y, c, z + shift))


def to_other_core(array):
    return exchange(array, lambda x, y, c, z: (x, y, 1 - c, z))


def along_line(array, shift):
    return exchange(
        array, lambda x, y, c, z: (x + shift, y, c, z) if c == 0 else (x, y + shift, c, z)
    )


def along_cross(array, shift):
    return exchange(
        array, lambda x, y, c, z: (x, y + shift, c, z) if c == 0 else (x + shift, y, c, z)
    )


def params(megabytes):
    return pltpu.CompilerParams(vmem_limit_bytes=megabytes << 20)


def cost(flops, moved):
    return pl.CostEstimate(flops=flops, bytes_accessed=moved, transcendentals=0)


def rope_tables(segments):
    places = jnp.arange(segments.shape[1], dtype=jnp.int32)
    earlier = jnp.concatenate([segments[:, :1] - 1, segments[:, :-1]], axis=1)
    starts = lax.cummax(jnp.where(segments != earlier, places[None, :], 0), axis=1)
    position = (places[None, :] - starts).astype(jnp.float32).reshape(-1)
    halves = jnp.arange(HEAD // 2, dtype=jnp.float32)
    inverse = jnp.exp(halves * (-2.0 * math.log(rope_theta) / HEAD))
    angles = position[:, None] * inverse[None, :]
    return (jnp.cos(angles), jnp.sin(angles))


def rotate(values, cosine, sine):
    leading = values[..., : HEAD // 2]
    trailing = values[..., HEAD // 2 :]
    cosine = cosine[:, None, :]
    sine = sine[:, None, :]
    return jnp.concatenate(
        [leading * cosine - trailing * sine, trailing * cosine + leading * sine], axis=-1
    )


def unrotate(values, cosine, sine):
    leading = values[..., : HEAD // 2]
    trailing = values[..., HEAD // 2 :]
    cosine = cosine[:, None, :]
    sine = sine[:, None, :]
    return jnp.concatenate(
        [leading * cosine + trailing * sine, trailing * cosine - leading * sine], axis=-1
    )


def pick_kernel(index, place, own, one, minus, two, *rest):
    outs, line, load, save = rest[:4], rest[4], rest[5], rest[6]
    n = own.shape[0]
    loads = []
    for i, source in enumerate((own, one, minus, two)):
        copy = pltpu.make_async_copy(source, line.at[pl.ds(place[i] * n, n)], load.at[i])
        copy.start()
        loads.append(copy)
    for copy in loads:
        copy.wait()
    saves = []
    for i in range(4):
        for b in range(n):
            copy = pltpu.make_async_copy(
                line.at[index[i * n + b]], outs[i].at[b], save.at[i * n + b]
            )
            copy.start()
            saves.append(copy)
    for copy in saves:
        copy.wait()


def pick(index, place, pieces):
    shape = pieces[0].shape
    return pl.pallas_call(
        pick_kernel,
        out_shape=[jax.ShapeDtypeStruct(shape, bf16)] * 4,
        in_specs=[SMEM, SMEM] + [ANY] * 4,
        out_specs=[ANY] * 4,
        scratch_shapes=[
            pltpu.VMEM((4 * shape[0],) + shape[1:], bf16),
            pltpu.SemaphoreType.DMA((4,)),
            pltpu.SemaphoreType.DMA((4 * shape[0],)),
        ],
        compiler_params=params(16),
        cost_estimate=cost(0, 16 * pieces[0].size),
    )(index, place, *pieces)


def lora_kernel(origin, hidden, key_back, value_back, s0, s1, s2, s3, out, maps, sems):
    blocks, both, wide = maps.shape
    width = hidden.shape[1]
    tokens = hidden.shape[0] // blocks
    for b in range(blocks):
        for i, source in enumerate((s0, s1, s2, s3)):

            @pl.when(origin[b] == i)
            def _():
                pltpu.make_async_copy(source.at[b], maps.at[b], sems.at[b]).start()

    half = lax.broadcasted_iota(jnp.int32, (both, tokens), 0) < both // 2
    for b in range(blocks):
        pltpu.make_async_copy(s0.at[b], maps.at[b], sems.at[b]).wait()
        rows = pl.ds(b * tokens, tokens)
        down = maps[b, :, :width]
        up = maps[b, :, width:]
        into = lax.dot_general(down, hidden[rows, :], NT, preferred_element_type=f32)
        keys = lax.dot_general(up, key_back[rows, :], NT, preferred_element_type=f32)
        values = lax.dot_general(up, value_back[rows, :], NT, preferred_element_type=f32)
        out[:both, rows] = into.astype(bf16)
        out[both:, rows] = jnp.where(half, keys, values).astype(bf16)


def lora(origin, hidden, key_back, value_back, sources):
    shape = sources[0].shape
    return pl.pallas_call(
        lora_kernel,
        out_shape=[
            jax.ShapeDtypeStruct((2 * shape[1], hidden.shape[0]), bf16),
            jax.ShapeDtypeStruct(shape, bf16),
        ],
        in_specs=[SMEM, VMEM, VMEM, VMEM] + [ANY] * 4,
        out_specs=[VMEM, VMEM],
        scratch_shapes=[pltpu.SemaphoreType.DMA((shape[0],))],
        compiler_params=params(24),
        cost_estimate=cost(2 * shape[1] * hidden.size, 2 * hidden.size + 4 * sources[0].size),
    )(origin, hidden, key_back, value_back, *sources)


def parts_kernel(hidden, key_back, value_back, t0, t1, t2, t3, part, sums):
    blocks, both, wide = part.shape
    width = hidden.shape[1]
    tokens = hidden.shape[0] // blocks
    rank = both // 2
    total = t0[...].astype(f32) + t1[...].astype(f32) + t2[...].astype(f32) + t3[...].astype(f32)
    sums[:both, :] = total[:both].astype(bf16)
    sums[both:, :] = (total[both:] * adapter_scale).astype(bf16)
    for b in range(blocks):
        rows = pl.ds(b * tokens, tokens)
        inner = sums[both:, rows]
        into = sums[:both, rows]
        down = jnp.dot(inner, hidden[rows, :], preferred_element_type=f32)
        part[b, :, :width] = down.astype(bf16)
        keys = jnp.dot(into[:rank], key_back[rows, :], preferred_element_type=f32)
        values = jnp.dot(into[rank:], value_back[rows, :], preferred_element_type=f32)
        part[b, :rank, width:] = (keys * adapter_scale).astype(bf16)
        part[b, rank:, width:] = (values * adapter_scale).astype(bf16)


def parts(hidden, key_back, value_back, pieces, blocks):
    both = pieces[0].shape[0] // 2
    shape = (blocks, both, hidden.shape[1] + key_back.shape[1])
    return pl.pallas_call(
        parts_kernel,
        out_shape=[
            jax.ShapeDtypeStruct(shape, bf16),
            jax.ShapeDtypeStruct(pieces[0].shape, bf16),
        ],
        in_specs=[VMEM] * 7,
        out_specs=[VMEM] * 2,
        compiler_params=params(24),
        cost_estimate=cost(2 * both * hidden.size, 4 * hidden.size),
    )(hidden, key_back, value_back, *pieces)


def collect_kernel(here, index, place, p0, p1, p2, p3, o0, o1, o2, o3, total):
    blocks = p0.shape[0]
    total[...] = jnp.zeros_like(total)
    for i, piece in enumerate((p0, p1, p2, p3)):
        for b in range(blocks):

            @pl.when(here[i * blocks + b] == 1)
            def _():
                slot = index[i * blocks + b]
                total[slot] = total[slot] + piece[b].astype(f32)

    for i, out in enumerate((o0, o1, o2, o3)):
        out[...] = total[pl.ds(place[i] * blocks, blocks)].astype(bf16)


def collect(here, index, place, pieces):
    shape = pieces[0].shape
    return pl.pallas_call(
        collect_kernel,
        out_shape=[jax.ShapeDtypeStruct(shape, bf16)] * 4,
        in_specs=[SMEM] * 3 + [VMEM] * 4,
        out_specs=[VMEM] * 4,
        scratch_shapes=[pltpu.VMEM((4 * shape[0],) + shape[1:], f32)],
        compiler_params=params(24),
        cost_estimate=cost(8 * pieces[0].size, 16 * pieces[0].size),
    )(here, index, place, *pieces)


def forward_kernel(place, mine, theirs, own, p0, p1, p2, p3, o0, o1, o2, o3, weights, sems):
    quarter = weights.shape[2]
    rows = mine.shape[0]
    loads = []
    for i, piece in enumerate((p0, p1, p2, p3)):
        copy = pltpu.make_async_copy(piece, weights.at[place[i]], sems.at[i])
        copy.start()
        loads.append(copy)
    for i, tokens in enumerate((mine, theirs)):
        o0[pl.ds(i * rows, rows), :] = jnp.dot(
            tokens[...], own[...], preferred_element_type=f32
        ).astype(bf16)
    for copy in loads:
        copy.wait()
    for k, out in enumerate((o1, o2, o3)):
        for i, tokens in enumerate((mine, theirs)):
            total = jnp.dot(tokens[:, :quarter], weights[0, k], preferred_element_type=f32)
            for j in range(1, 4):
                total = total + jnp.dot(
                    tokens[:, j * quarter : (j + 1) * quarter],
                    weights[j, k],
                    preferred_element_type=f32,
                )
            out[pl.ds(i * rows, rows), :] = total.astype(bf16)


def forward(place, mine, theirs, own, pieces):
    out = jax.ShapeDtypeStruct((2 * mine.shape[0], own.shape[1]), bf16)
    return pl.pallas_call(
        forward_kernel,
        out_shape=[out] * 4,
        in_specs=[SMEM] + [VMEM] * 3 + [ANY] * 4,
        out_specs=[VMEM] * 4,
        scratch_shapes=[
            pltpu.VMEM((4,) + pieces[0].shape, bf16),
            pltpu.SemaphoreType.DMA((4,)),
        ],
        compiler_params=params(40),
        cost_estimate=cost(4 * mine.size * own.shape[1] * 4, 16 * own.size),
    )(place, mine, theirs, own, *pieces)


def backward_kernel(
    place, other_place, sums, maps, b0, b1, b2, b3, own, w0, w1, w2, w3,
    other, v0, v1, v2, v3, out, weights, others, total, sems,
):
    both = maps.shape[1]
    quarter = weights.shape[2]
    blocks = maps.shape[0]
    tokens = sums.shape[1] // blocks
    loads = []
    for i, (one, two) in enumerate(((w0, v0), (w1, v1), (w2, v2), (w3, v3))):
        for k, (piece, store, at) in enumerate(
            ((one, weights, place), (two, others, other_place))
        ):
            copy = pltpu.make_async_copy(piece, store.at[at[i]], sems.at[2 * i + k])
            copy.start()
            loads.append(copy)
    for copy in loads:
        copy.wait()
    for j in range(4):
        columns = slice(j * quarter, (j + 1) * quarter)
        total[...] = lax.dot_general(
            b0[0], own[columns, :], NT, preferred_element_type=f32
        ) + lax.dot_general(b0[1], other[columns, :], NT, preferred_element_type=f32)
        for k, back in enumerate((b1, b2, b3)):
            total[...] += lax.dot_general(
                back[0], weights[j, k], NT, preferred_element_type=f32
            ) + lax.dot_general(back[1], others[j, k], NT, preferred_element_type=f32)
        for b in range(blocks):
            rows = pl.ds(b * tokens, tokens)
            out[rows, columns] = (
                total[rows, :]
                + lax.dot_general(
                    sums[both:, rows], maps[b, :, columns], TN, preferred_element_type=f32
                )
            ).astype(bf16)


def backward(place, other_place, sums, maps, backs, own, pieces, other, other_pieces):
    rows, quarter = backs[0].shape[1], pieces[0].shape[1]
    return pl.pallas_call(
        backward_kernel,
        out_shape=jax.ShapeDtypeStruct((rows, own.shape[0]), bf16),
        in_specs=[SMEM] * 2 + [VMEM] * 7 + [ANY] * 4 + [VMEM] + [ANY] * 4,
        out_specs=VMEM,
        scratch_shapes=[
            pltpu.VMEM((4,) + pieces[0].shape, bf16),
            pltpu.VMEM((4,) + pieces[0].shape, bf16),
            pltpu.VMEM((rows, quarter), f32),
            pltpu.SemaphoreType.DMA((8,)),
        ],
        compiler_params=params(48),
        cost_estimate=cost(16 * rows * own.size, 24 * own.size),
    )(place, other_place, sums, maps, *backs, own, *pieces, other, *other_pieces)


def per_device(
    hidden,
    key_weight_frozen,
    value_weight_frozen,
    adapter_down_maps,
    adapter_up_maps,
    block_adapter_index,
    segment_document_index,
    adapter_position,
    key_gradient,
    value_gradient,
):
    rows, width = hidden.shape
    kv_here = key_weight_frozen.shape[1]
    heads_here = kv_here // HEAD
    blocks = block_adapter_index.shape[0]
    block_rows = rows // blocks
    slots_here, _, rank, _ = adapter_down_maps.shape
    both = 2 * rank
    quarter = width // SIDE
    dp = lax.axis_index("dp")
    z = lax.axis_index("tensor")
    core = dp % 2
    x, y = dp // 8, (dp // 2) % 4
    line = jnp.where(core == 0, x, y)
    cross = jnp.where(core == 0, y, x)
    first = core == 0
    line_place = jnp.stack([(line - d) % SIDE for d in (0,) + SHIFTS])
    cross_place = jnp.stack([(cross - d) % SIDE for d in (0,) + SHIFTS])

    slots = jnp.take(adapter_position, block_adapter_index, axis=0)
    slots_at = [slots] + [along_cross(slots, -d) for d in SHIFTS]

    def split(slot):
        slot_x, slot_y, within = slot // 16, (slot // 4) % 4, slot % 4
        slot_line = jnp.where(first, slot_x, slot_y)
        slot_cross = jnp.where(first, slot_y, slot_x)
        local = ((within // 2 + core) % 2) * 2 + within % 2
        return slot_cross, slot_line * (2 * slots_here) + local

    maps_here = jnp.concatenate(
        [
            adapter_down_maps.reshape(slots_here, both, width),
            adapter_up_maps.reshape(slots_here, both, kv_here),
        ],
        axis=2,
    )
    maps_chip = jnp.concatenate([maps_here, to_other_core(maps_here)], axis=0)
    maps_line = [maps_chip] + [along_line(maps_chip, d) for d in SHIFTS]
    index = jnp.concatenate([split(s)[1] for s in slots_at])
    picked = pick(index, line_place, maps_line)
    maps_from = [picked[0]] + [along_cross(picked[i + 1], d) for i, d in enumerate(SHIFTS)]
    apart = (cross - split(slots)[0]) % SIDE
    origin = jnp.where(apart == 3, 2, jnp.where(apart == 2, 3, apart))

    def own_kind(start, size):
        return jnp.where(
            first,
            lax.dynamic_slice_in_dim(key_weight_frozen, start, size, 0),
            lax.dynamic_slice_in_dim(value_weight_frozen, start, size, 0),
        )

    def other_kind(start, size):
        return jnp.where(
            first,
            lax.dynamic_slice_in_dim(value_weight_frozen, start, size, 0),
            lax.dynamic_slice_in_dim(key_weight_frozen, start, size, 0),
        )

    quarters = jnp.stack(
        [
            along_z(own_kind(((z + d) % SIDE) * width + line * quarter, quarter), d)
            for d in SHIFTS
        ]
    )
    pieces = [quarters] + [along_line(quarters, d) for d in SHIFTS]
    theirs = to_other_core(hidden)
    own = own_kind(z * width, width)
    other = other_kind(z * width, width)
    partial = forward(line_place, hidden, theirs, own, pieces)
    other_pieces = [to_other_core(piece) for piece in pieces]

    cosine, sine = rope_tables(segment_document_index)
    key_back = (
        unrotate(
            key_gradient.astype(jnp.float32).reshape(rows, heads_here, HEAD), cosine, sine
        )
        .reshape(rows, kv_here)
        .astype(bf16)
    )
    back = jnp.where(
        first,
        jnp.stack([key_back, value_gradient]),
        jnp.stack([value_gradient, key_back]),
    )
    backs = [back] + [along_z(back, d) for d in SHIFTS]

    into, maps = lora(origin, hidden, key_back, value_gradient, maps_from)
    terms = [into] + [along_z(into, d) for d in SHIFTS]
    part, sums = parts(hidden, key_back, value_gradient, terms, blocks)

    hidden_gradient = backward(
        line_place, cross_place, sums, maps, backs, own, pieces, other, other_pieces
    )

    part_from = [part] + [along_cross(part, d) for d in SHIFTS]
    slots_from = [slots_at[0], slots_at[2], slots_at[1], slots_at[3]]
    found = [split(s) for s in slots_from]
    here = jnp.concatenate([(f[0] == cross).astype(jnp.int32) for f in found])
    where_to = jnp.concatenate([f[1] for f in found])
    target = jnp.stack([(line + d) % SIDE for d in (0,) + SHIFTS])
    line_sums = collect(here, where_to, target, part_from)
    arrived = [line_sums[0]] + [along_line(line_sums[i + 1], d) for i, d in enumerate(SHIFTS)]
    chip_sum = sum(a.astype(f32) for a in arrived)
    mine_sum = chip_sum[:slots_here] + to_other_core(
        chip_sum[slots_here:].astype(bf16)
    ).astype(f32)
    grad_down = mine_sum[:, :, :width].reshape(adapter_down_maps.shape)
    grad_up = mine_sum[:, :, width:].reshape(adapter_up_maps.shape)

    frozen = partial[0].astype(f32)
    for i, d in enumerate(SHIFTS):
        frozen = frozen + along_z(partial[i + 1], -d).astype(f32)
    crossed = to_other_core(frozen[rows:].astype(bf16)).astype(f32)
    adapter_input = sums[:both].reshape(2, rank, blocks, block_rows)
    added = (
        jnp.einsum(
            "jrqw,qjru->qwju",
            adapter_input,
            maps[:, :, width:].reshape(blocks, 2, rank, kv_here),
            preferred_element_type=f32,
        ).reshape(rows, 2, kv_here)
        * adapter_scale
    )
    key_pre = jnp.where(first, frozen[:rows], crossed) + added[:, 0]
    value_pre = jnp.where(first, crossed, frozen[:rows]) + added[:, 1]
    key_out = (
        rotate(key_pre.reshape(rows, heads_here, HEAD), cosine, sine)
        .reshape(rows, kv_here)
        .astype(bf16)
    )
    return key_out, value_pre.astype(bf16), hidden_gradient, grad_down, grad_up


def solution(mesh):
    return jax.shard_map(
        per_device,
        mesh=mesh,
        in_specs=(
            P("dp", "tensor"),
            P(None, "tensor"),
            P(None, "tensor"),
            P("dp", None, None, "tensor"),
            P("dp", None, None, "tensor"),
            P("dp"),
            P("dp", None),
            P(),
            P("dp", "tensor"),
            P("dp", "tensor"),
        ),
        out_specs=(
            P("dp", "tensor"),
            P("dp", "tensor"),
            P("dp", "tensor"),
            P("dp", None, None, "tensor"),
            P("dp", None, None, "tensor"),
        ),
        check_vma=False,
    )
```

time: 511 us -> 161 us (0.32)
  waiting for transfers between devices: 403 us -> 32.6 us
  starting transfers between devices: 0.46 us -> 64.6 us
  matrix products: 54.4 us -> 0.34 us
  Pallas kernels: 0 us -> 29.6 us
  local copies, waits for them, and re-layouts: 26.1 us -> 12.6 us
  between operations: 15 us -> 1.85 us
  other arithmetic: 10.9 us -> 19.4 us
    reduce_scatter x3 -> x0, waiting for transfers between devices: 234 us -> none  [the longest x1 94.3 us: per_device(): lax.psum_scatter(dense_down.astype(jnp.bfloat16), 'dp', scatter_dimension...]
    all_gather x3 -> x0, waiting for transfers between devices: 152 us -> none  [the longest x1 59.6 us: per_device(): columns = lax.all_gather(hidden, 'tensor', axis=1, tiled=True)]
    ppermute x0 -> x38, starting transfers between devices: none -> 64.6 us  [exchange(): return lax.ppermute(array, ('dp', 'tensor'), pairs)]
    dot_general x12 -> x1, matrix products: 54.4 us -> 0.34 us  [per_device(): jnp.einsum('jrqw,qjru->qwju', adapter_input, maps[:, :, width:].reshape(b...]
    ppermute x0 -> x38, waiting for transfers between devices: none -> 32.6 us  [exchange(): return lax.ppermute(array, ('dp', 'tensor'), pairs)]
    pallas_call x0 -> x6, Pallas kernels: none -> 29.6 us  [the longest x1 11 us: backward(): pl.pallas_call(backward_kernel, out_shape=jax.ShapeDtypeStruct((rows, own...]
    psum x1 -> x0, waiting for transfers between devices: 14.7 us -> none  [per_device(): lax.psum(in_part.astype(jnp.bfloat16), 'tensor').astype(jnp.float32)]
    convert_element_type x5 -> x1, local copies, waits for them, and re-layouts: 14.8 us -> 0.17 us  [per_device(): key_back = unrotate(key_gradient.astype(jnp.float32).reshape(rows, heads_...]
  transfers between devices with their start and end apart: 7 -> 38, of which waited for: 7 -> 7; matrix products, arithmetic and copies ran while one was open for 16% -> 12% of each run, Pallas kernels for 0% -> 18%
where the time goes in v1:
time: 161 us
  starting transfers between devices  64.6 us (40%)
  waiting for transfers between devices  32.6 us (20%)
  Pallas kernels  29.6 us (18%)
  other arithmetic  19.4 us (12%)
  local copies, waits for them, and re-layouts  12.6 us (8%)
  between operations  1.85 us (1%)
    ppermute x38, starting transfers between devices, exchange(): return lax.ppermute(array, ('dp', 'tensor'), pairs)  64.6 us
    ppermute x38, waiting for transfers between devices, exchange(): return lax.ppermute(array, ('dp', 'tensor'), pairs)  32.6 us
    pallas_call x1, Pallas kernels, backward(): pl.pallas_call(backward_kernel, out_shape=jax.ShapeDtypeStruct((rows, own...  11 us
    unnamed x66, local copies, waits for them, and re-layouts  8.17 us
    pallas_call x1, Pallas kernels, forward(): pl.pallas_call(forward_kernel, out_shape=[out] * 4, in_specs=[SMEM] + [VM...  7.45 us
    pallas_call x1, Pallas kernels, pick(): pl.pallas_call(pick_kernel, out_shape=[jax.ShapeDtypeStruct(shape, bf16)]...  4.35 us
    pallas_call x1, Pallas kernels, lora(): pl.pallas_call(lora_kernel, out_shape=[jax.ShapeDtypeStruct((2 * shape[1]...  3.23 us
  transfers between devices with their start and end apart: 38, of which 7 were waited for; matrix products, arithmetic and copies ran while one was open for 12% of the time, Pallas kernels for 18%

profile of v1, /device:TPU:1, one launch (start us, length us, event | category | flops | bytes accessed | tf_op | source)
XLA Modules:
  0.0 161.0 jit_solution(5624349402871671002)
XLA Ops:
  3.3 3.6 %collective-permute-start.13 = (s32[4]{0:T(128)S(1)}, s32[4]{0:T(128)S(1)}, u32[]{:S(2)}, u32[]{:S(2)}) collective-permute-start(s32[4]{0:T(128)S(1)} %get-tuple-element.40), channel_id=1, source_target_pairs={{0,16},{1,17},{2,18},{3,19},{4,68},{5,69},{6,70},{7,71},{8,24},{9,... | collective-permute-start | bytes 56 | tf_op jit(solution)/shard_map/ppermute | solution.py:34
  7.1 2.4 %collective-permute-start.11 = (s32[4]{0:T(128)S(1)}, s32[4]{0:T(128)S(1)}, u32[]{:S(2)}, u32[]{:S(2)}) collective-permute-start(s32[4]{0:T(128)S(1)} %get-tuple-element.40), channel_id=1, source_target_pairs={{0,24},{1,25},{2,26},{3,27},{4,100},{5,101},{6,102},{7,103},{8,0},... | collective-permute-start | bytes 56 | tf_op jit(solution)/shard_map/ppermute | solution.py:34
  12.3 2.4 %dynamic-slice_select_fusion.2 = (bf16[512,256]{1,0:T(8,128)(2,1)}, bf16[512,256]{1,0:T(8,128)(2,1)}, bf16[512,256]{1,0:T(8,128)(2,1)}) fusion(bf16[8192,256]{1,0:T(8,128)(2,1)} %param.12, s32[]{:T(128)S(6)} %select_n.377, bf16[8192,256]{1,0:T(8,128)(2,1)} %param.11, pred[]{:T(512)S(6)} %eq.80, s32[]{:T(128)S(6)} %select_n.383, s32[]{:T(128)S(6)} %select_n.380), kind=kLoop, calls=%fused_computation.33 | loop fusion | flops 393216 | bytes 2359309 | tf_op jit(solution)/shard_map/jit(_where)/select_n | solution.py:392
  25.7 2.7 %collective-permute-start.16 = (bf16[4,32,2304]{2,1,0:T(8,128)(2,1)S(1)}, bf16[4,32,2304]{2,1,0:T(8,128)(2,1)S(1)}, u32[]{:S(2)}, u32[]{:S(2)}) collective-permute-start(bf16[4,32,2304]{2,1,0:T(8,128)(2,1)S(1)} %pad_maximum_fusion.1.own), channel_id=1, source_target_pairs={{0,96},{1,97},{2,98},{3,99},{4,28},{5,29},{6,30},{7,31},{8,104},{9... | collective-permute-start | bytes 1769480 | tf_op jit(solution)/shard_map/ppermute | solution.py:34
  29.0 13.2 %collective-permute-done.15.one = bf16[4,32,2304]{2,1,0:T(8,128)(2,1)S(1)} collective-permute-done((bf16[4,32,2304]{2,1,0:T(8,128)(2,1)S(1)}, bf16[4,32,2304]{2,1,0:T(8,128)(2,1)S(1)}, u32[]{:S(2)}, u32[]{:S(2)}) %collective-permute-start.15) | collective-permute-done | bytes 589856 | tf_op jit(solution)/shard_map/ppermute | solution.py:34
  45.1 4.3 %shard_map.138 = (bf16[4,32,2304]{2,1,0:T(8,128)(2,1)S(1)}, bf16[4,32,2304]{2,1,0:T(8,128)(2,1)S(1)}, bf16[4,32,2304]{2,1,0:T(8,128)(2,1)S(1)}, bf16[4,32,2304]{2,1,0:T(8,128)(2,1)S(1)}) custom-call(s32[16]{0:T(128)S(1)} %get-tuple-element.64.index, s32[4]{0:T(128)S(1)} %pad_add_fusion.place, bf16[4,32,2304]{2,1,0:T(8,128)(2,1)S(1)} %pad_maximum_fusion.1.own, ...), custom_call_target="tpu_custom_call" | custom-call | bytes 4718592 | tf_op jit(solution)/shard_map/pallas_call | solution.py:120
  52.7 5.6 %collective-permute-done.3 = bf16[512,256]{1,0:T(8,128)(2,1)S(1)} collective-permute-done((bf16[512,256]{1,0:T(8,128)(2,1)}, bf16[512,256]{1,0:T(8,128)(2,1)S(1)}, u32[]{:S(2)}, u32[]{:S(2)}) %collective-permute-start.3) | collective-permute-done | bytes 262176 | tf_op jit(solution)/shard_map/ppermute | solution.py:34
  62.7 8.9 %collective-permute-done.20.s3 = bf16[4,32,2304]{2,1,0:T(8,128)(2,1)S(1)} collective-permute-done((bf16[4,32,2304]{2,1,0:T(8,128)(2,1)S(1)}, bf16[4,32,2304]{2,1,0:T(8,128)(2,1)S(1)}, u32[]{:S(2)}, u32[]{:S(2)}) %collective-permute-start.20) | collective-permute-done | bytes 589856 | tf_op jit(solution)/shard_map/ppermute | solution.py:34
  71.7 3.2 %shard_map.139 = (bf16[64,512]{1,0:T(8,128)(2,1)S(1)}, bf16[4,32,2304]{2,1,0:T(8,128)(2,1)S(1)}) custom-call(s32[4]{0:T(128)S(1)} %get-tuple-element.66.origin, bf16[512,2048]{1,0:T(8,128)(2,1)S(1)} %copy-done.1, bf16[512,256]{1,0:T(8,128)(2,1)S(1)} %bitcast.50, bf16[512,256]{1,0:T(8,128)(2,1)S(1)} %copy-done.2, ...), custom_call_target="tpu_custom_call" | custom-call | flops 67108864 | bytes 3276800 | tf_op jit(solution)/shard_map/pallas_call | solution.py:161
  75.7 3.4 %collective-permute-start.21 = (bf16[64,512]{1,0:T(8,128)(2,1)S(1)}, bf16[64,512]{1,0:T(8,128)(2,1)S(1)}, u32[]{:S(2)}, u32[]{:S(2)}) collective-permute-start(bf16[64,512]{1,0:T(8,128)(2,1)S(1)} %get-tuple-element.30.t0), channel_id=1, source_target_pairs={{0,1},{1,2},{2,3},{3,0},{4,5},{5,6},{6,7},{7,4},{8,9},{9,10},{10,1... | collective-permute-start | bytes 196616 | tf_op jit(solution)/shard_map/ppermute | solution.py:34
  80.0 8.0 %collective-permute-start.22 = (bf16[64,512]{1,0:T(8,128)(2,1)S(1)}, bf16[64,512]{1,0:T(8,128)(2,1)S(1)}, u32[]{:S(2)}, u32[]{:S(2)}) collective-permute-start(bf16[64,512]{1,0:T(8,128)(2,1)S(1)} %get-tuple-element.30.t0), channel_id=1, source_target_pairs={{0,3},{1,0},{2,1},{3,2},{4,7},{5,4},{6,5},{7,6},{8,11},{9,8},{10,9... | collective-permute-start | bytes 196616 | tf_op jit(solution)/shard_map/ppermute | solution.py:34
  88.0 5.7 %collective-permute-start.6 = (bf16[3,512,256]{2,1,0:T(8,128)(2,1)}, bf16[3,512,256]{2,1,0:T(8,128)(2,1)}, u32[]{:S(2)}, u32[]{:S(2)}) collective-permute-start(bf16[3,512,256]{2,1,0:T(8,128)(2,1)} %pad_maximum_fusion.p0.w0), channel_id=1, source_target_pairs={{0,64},{1,65},{2,66},{3,67},{4,20},{5,21},{6,22},{7,23},{8,72},{9,... | collective-permute-start | bytes 2359304 | tf_op jit(solution)/shard_map/ppermute | solution.py:34
  94.2 3.3 %collective-permute-start.28 = (bf16[3,512,256]{2,1,0:T(8,128)(2,1)}, bf16[3,512,256]{2,1,0:T(8,128)(2,1)}, u32[]{:S(2)}, u32[]{:S(2)}) collective-permute-start(bf16[3,512,256]{2,1,0:T(8,128)(2,1)} %collective-permute-done.4.p1.w1), channel_id=1, source_target_pairs={{0,4},{1,5},{2,6},{3,7},{4,0},{5,1},{6,2},{7,3},{8,12},{9,13},{10,... | collective-permute-start | bytes 2359304 | tf_op jit(solution)/shard_map/ppermute | solution.py:34
  99.8 2.9 %broadcast_select_fusion = (bf16[2048,256]{1,0:T(8,128)(2,1)}, bf16[2048,256]{1,0:T(8,128)(2,1)S(1)}) fusion(pred[]{:T(512)S(6)} %eq.80, bf16[8192,256]{1,0:T(8,128)(2,1)} %param.12, s32[]{:T(128)S(6)} %select_n.374, bf16[8192,256]{1,0:T(8,128)(2,1)} %param.11), kind=kLoop, calls=%fused_computation.5 | loop fusion | flops 1048576 | bytes 4194309 | tf_op jit(solution)/shard_map/jit(_where)/select_n | solution.py:399
  102.7 3.3 %collective-permute-done.6.p3.w3 = bf16[3,512,256]{2,1,0:T(8,128)(2,1)} collective-permute-done((bf16[3,512,256]{2,1,0:T(8,128)(2,1)}, bf16[3,512,256]{2,1,0:T(8,128)(2,1)}, u32[]{:S(2)}, u32[]{:S(2)}) %collective-permute-start.6) | collective-permute-done | bytes 786464 | tf_op jit(solution)/shard_map/ppermute | solution.py:34
  106.0 2.8 %collective-permute-start.29 = (bf16[3,512,256]{2,1,0:T(8,128)(2,1)}, bf16[3,512,256]{2,1,0:T(8,128)(2,1)}, u32[]{:S(2)}, u32[]{:S(2)}) collective-permute-start(bf16[3,512,256]{2,1,0:T(8,128)(2,1)} %collective-permute-done.5.p2.w2), channel_id=1, source_target_pairs={{0,4},{1,5},{2,6},{3,7},{4,0},{5,1},{6,2},{7,3},{8,12},{9,13},{10,... | collective-permute-start | bytes 2359304 | tf_op jit(solution)/shard_map/ppermute | solution.py:34
  109.3 7.5 %shard_map.137 = (bf16[1024,256]{1,0:T(8,128)(2,1)S(1)}, bf16[1024,256]{1,0:T(8,128)(2,1)}, bf16[1024,256]{1,0:T(8,128)(2,1)S(1)}, bf16[1024,256]{1,0:T(8,128)(2,1)S(1)}) custom-call(s32[4]{0:T(128)S(1)} %pad_add_fusion.place, bf16[512,2048]{1,0:T(8,128)(2,1)S(1)} %copy-done.1, bf16[512,2048]{1,0:T(8,128)(2,1)} %collective-permute-done.theirs, ...), custom_call_target="tpu_custom_call" | custom-call | flops 4294967296 | bytes 8388608 | tf_op jit(solution)/shard_map/pallas_call | solution.py:267
  120.1 3.7 %collective-permute-start.7 = (bf16[1024,256]{1,0:T(8,128)(2,1)}, bf16[1024,256]{1,0:T(8,128)(2,1)S(1)}, u32[]{:S(2)}, u32[]{:S(2)}) collective-permute-start(bf16[1024,256]{1,0:T(8,128)(2,1)} %get-tuple-element.22), channel_id=1, source_target_pairs={{0,3},{1,0},{2,1},{3,2},{4,7},{5,4},{6,5},{7,6},{8,11},{9,8},{10,9... | collective-permute-start | bytes 1572872 | tf_op jit(solution)/shard_map/ppermute | solution.py:34
  124.1 4.4 %collective-permute-start.9 = (bf16[1024,256]{1,0:T(8,128)(2,1)}, bf16[1024,256]{1,0:T(8,128)(2,1)S(1)}, u32[]{:S(2)}, u32[]{:S(2)}) collective-permute-start(bf16[1024,256]{1,0:T(8,128)(2,1)} %copy-done.16), channel_id=1, source_target_pairs={{0,2},{1,3},{2,0},{3,1},{4,6},{5,7},{6,4},{7,5},{8,10},{9,11},{10,... | collective-permute-start | bytes 1572872 | tf_op jit(solution)/shard_map/ppermute | solution.py:34
  129.9 2.2 %shard_map.142 = (bf16[4,32,2304]{2,1,0:T(8,128)(2,1)S(1)}, bf16[4,32,2304]{2,1,0:T(8,128)(2,1)S(1)}, bf16[4,32,2304]{2,1,0:T(8,128)(2,1)S(1)}, bf16[4,32,2304]{2,1,0:T(8,128)(2,1)S(1)}) custom-call(s32[16]{0:T(128)S(1)} %add_convert_fusion.1.here, s32[16]{0:T(128)S(1)} %get-tuple-element.63.index, s32[4]{0:T(128)S(1)} %pad_add_fusion.2.place, ...), custom_call_target="tpu_custom_call" | custom-call | flops 2359296 | bytes 4718592 | tf_op jit(solution)/shard_map/pallas_call | solution.py:228
  132.3 2.7 %collective-permute-start.35 = (bf16[4,32,2304]{2,1,0:T(8,128)(2,1)S(1)}, bf16[4,32,2304]{2,1,0:T(8,128)(2,1)S(1)}, u32[]{:S(2)}, u32[]{:S(2)}) collective-permute-start(bf16[4,32,2304]{2,1,0:T(8,128)(2,1)S(1)} %get-tuple-element.35), channel_id=1, source_target_pairs={{0,96},{1,97},{2,98},{3,99},{4,28},{5,29},{6,30},{7,31},{8,104},{9... | collective-permute-start | bytes 1769480 | tf_op jit(solution)/shard_map/ppermute | solution.py:34
  135.2 2.6 %collective-permute-start.36 = (bf16[4,32,2304]{2,1,0:T(8,128)(2,1)S(1)}, bf16[4,32,2304]{2,1,0:T(8,128)(2,1)S(1)}, u32[]{:S(2)}, u32[]{:S(2)}) collective-permute-start(bf16[4,32,2304]{2,1,0:T(8,128)(2,1)S(1)} %get-tuple-element.36), channel_id=1, source_target_pairs={{0,64},{1,65},{2,66},{3,67},{4,20},{5,21},{6,22},{7,23},{8,72},{9,... | collective-permute-start | bytes 1769480 | tf_op jit(solution)/shard_map/ppermute | solution.py:34
  137.8 11.0 %shard_map.141 = bf16[512,2048]{1,0:T(8,128)(2,1)} custom-call(s32[4]{0:T(128)S(1)} %pad_add_fusion.place, s32[4]{0:T(128)S(1)} %pad_add_fusion.1.other_place, bf16[64,512]{1,0:T(8,128)(2,1)S(1)} %get-tuple-element.31.sums, bf16[4,32,2304]{2,1,0:T(8,128)(2,1)S(1)} %get-tuple-element.29.maps, bf16[2,512,256]{2,1,0:T(8,128)(2,1)S(1)} %copy-done.7, ...), custom_call_target="tpu_custom_call" | custom-call | flops 4294967296 | bytes 12582912 | tf_op jit(solution)/shard_map/pallas_call | solution.py:320
  150.2 2.9 %collective-permute-start.10 = (bf16[512,256]{1,0:T(8,128)(2,1)S(1)}, bf16[512,256]{1,0:T(8,128)(2,1)S(1)}, u32[]{:S(2)}, u32[]{:S(2)}) collective-permute-start(bf16[512,256]{1,0:T(8,128)(2,1)S(1)} %slice.111), channel_id=1, source_target_pairs={{0,4},{1,5},{2,6},{3,7},{4,0},{5,1},{6,2},{7,3},{8,12},{9,13},{10,... | collective-permute-start | bytes 786440 | tf_op jit(solution)/shard_map/ppermute | solution.py:34
  (176 shorter events, 46.6 us)
Async XLA Ops:
  3.3 19.5 %collective-permute-start.13 = (s32[4]{0:T(128)S(1)}, s32[4]{0:T(128)S(1)}, u32[]{:S(2)}, u32[]{:S(2)}) collective-permute-start(s32[4]{0:T(128)S(1)} %get-tuple-element.40), channel_id=1, source_target_pairs={{0,16},{1,17},{2,18},{3,19},{4,68},{5,69},{6,70},{7,71},{8,24},{9,... | collective-permute-start | bytes 56 | tf_op jit(solution)/shard_map/ppermute | solution.py:34
  6.8 18.1 %collective-permute-start.12 = (s32[4]{0:T(128)S(1)}, s32[4]{0:T(128)S(1)}, u32[]{:S(2)}, u32[]{:S(2)}) collective-permute-start(s32[4]{0:T(128)S(1)} %get-tuple-element.40), channel_id=1, source_target_pairs={{0,8},{1,9},{2,10},{3,11},{4,36},{5,37},{6,38},{7,39},{8,16},{9,17... | collective-permute-start | bytes 56 | tf_op jit(solution)/shard_map/ppermute | solution.py:34
  7.1 21.2 %collective-permute-start.11 = (s32[4]{0:T(128)S(1)}, s32[4]{0:T(128)S(1)}, u32[]{:S(2)}, u32[]{:S(2)}) collective-permute-start(s32[4]{0:T(128)S(1)} %get-tuple-element.40), channel_id=1, source_target_pairs={{0,24},{1,25},{2,26},{3,27},{4,100},{5,101},{6,102},{7,103},{8,0},... | collective-permute-start | bytes 56 | tf_op jit(solution)/shard_map/ppermute | solution.py:34
  14.6 34.8 %collective-permute-start.1 = (bf16[512,256]{1,0:T(8,128)(2,1)}, bf16[512,256]{1,0:T(8,128)(2,1)}, u32[]{:S(2)}, u32[]{:S(2)}) collective-permute-start(bf16[512,256]{1,0:T(8,128)(2,1)} %get-tuple-element.52), channel_id=1, source_target_pairs={{0,1},{1,2},{2,3},{3,0},{4,5},{5,6},{6,7},{7,4},{8,9},{9,10},{10,1... | collective-permute-start | bytes 786440 | tf_op jit(solution)/shard_map/ppermute | solution.py:34
  22.8 27.8 %collective-permute-start.2 = (bf16[512,256]{1,0:T(8,128)(2,1)}, bf16[512,256]{1,0:T(8,128)(2,1)S(1)}, u32[]{:S(2)}, u32[]{:S(2)}) collective-permute-start(bf16[512,256]{1,0:T(8,128)(2,1)} %get-tuple-element.54), channel_id=1, source_target_pairs={{0,3},{1,0},{2,1},{3,2},{4,7},{5,4},{6,5},{7,6},{8,11},{9,8},{10,9... | collective-permute-start | bytes 786440 | tf_op jit(solution)/shard_map/ppermute | solution.py:34
  25.6 16.6 %collective-permute-start.15 = (bf16[4,32,2304]{2,1,0:T(8,128)(2,1)S(1)}, bf16[4,32,2304]{2,1,0:T(8,128)(2,1)S(1)}, u32[]{:S(2)}, u32[]{:S(2)}) collective-permute-start(bf16[4,32,2304]{2,1,0:T(8,128)(2,1)S(1)} %pad_maximum_fusion.1.own), channel_id=1, source_target_pairs={{0,32},{1,33},{2,34},{3,35},{4,12},{5,13},{6,14},{7,15},{8,40},{9,... | collective-permute-start | bytes 1769480 | tf_op jit(solution)/shard_map/ppermute | solution.py:34
  25.7 16.6 %collective-permute-start.16 = (bf16[4,32,2304]{2,1,0:T(8,128)(2,1)S(1)}, bf16[4,32,2304]{2,1,0:T(8,128)(2,1)S(1)}, u32[]{:S(2)}, u32[]{:S(2)}) collective-permute-start(bf16[4,32,2304]{2,1,0:T(8,128)(2,1)S(1)} %pad_maximum_fusion.1.own), channel_id=1, source_target_pairs={{0,96},{1,97},{2,98},{3,99},{4,28},{5,29},{6,30},{7,31},{8,104},{9... | collective-permute-start | bytes 1769480 | tf_op jit(solution)/shard_map/ppermute | solution.py:34
  42.2 19.6 %collective-permute-start.24 = (bf16[2,512,256]{2,1,0:T(8,128)(2,1)S(1)}, bf16[2,512,256]{2,1,0:T(8,128)(2,1)S(1)}, u32[]{:S(2)}, u32[]{:S(2)}) collective-permute-start(bf16[2,512,256]{2,1,0:T(8,128)(2,1)S(1)} %maximum_select_fusion.b0), channel_id=1, source_target_pairs={{0,1},{1,2},{2,3},{3,0},{4,5},{5,6},{6,7},{7,4},{8,9},{9,10},{10,1... | collective-permute-start | bytes 1572872 | tf_op jit(solution)/shard_map/ppermute | solution.py:34
  42.2 66.7 %collective-permute-start = (bf16[512,2048]{1,0:T(8,128)(2,1)S(1)}, bf16[512,2048]{1,0:T(8,128)(2,1)}, u32[]{:S(2)}, u32[]{:S(2)}) collective-permute-start(bf16[512,2048]{1,0:T(8,128)(2,1)S(1)} %copy-done.1), channel_id=1, source_target_pairs={{0,4},{1,5},{2,6},{3,7},{4,0},{5,1},{6,2},{7,3},{8,12},{9,13},{10,... | collective-permute-start | bytes 6291464 | tf_op jit(solution)/shard_map/ppermute | solution.py:34
  43.0 15.3 %collective-permute-start.3 = (bf16[512,256]{1,0:T(8,128)(2,1)}, bf16[512,256]{1,0:T(8,128)(2,1)S(1)}, u32[]{:S(2)}, u32[]{:S(2)}) collective-permute-start(bf16[512,256]{1,0:T(8,128)(2,1)} %get-tuple-element.53), channel_id=1, source_target_pairs={{0,2},{1,3},{2,0},{3,1},{4,6},{5,7},{6,4},{7,5},{8,10},{9,11},{10,... | collective-permute-start | bytes 786440 | tf_op jit(solution)/shard_map/ppermute | solution.py:34
  61.8 26.2 %collective-permute-start.4 = (bf16[3,512,256]{2,1,0:T(8,128)(2,1)}, bf16[3,512,256]{2,1,0:T(8,128)(2,1)}, u32[]{:S(2)}, u32[]{:S(2)}) collective-permute-start(bf16[3,512,256]{2,1,0:T(8,128)(2,1)} %pad_maximum_fusion.p0.w0), channel_id=1, source_target_pairs={{0,32},{1,33},{2,34},{3,35},{4,12},{5,13},{6,14},{7,15},{8,40},{9,... | collective-permute-start | bytes 2359304 | tf_op jit(solution)/shard_map/ppermute | solution.py:34
  61.9 17.2 %collective-permute-start.26 = (bf16[2,512,256]{2,1,0:T(8,128)(2,1)S(1)}, bf16[2,512,256]{2,1,0:T(8,128)(2,1)S(1)}, u32[]{:S(2)}, u32[]{:S(2)}) collective-permute-start(bf16[2,512,256]{2,1,0:T(8,128)(2,1)S(1)} %maximum_select_fusion.b0), channel_id=1, source_target_pairs={{0,2},{1,3},{2,0},{3,1},{4,6},{5,7},{6,4},{7,5},{8,10},{9,11},{10,... | collective-permute-start | bytes 1572872 | tf_op jit(solution)/shard_map/ppermute | solution.py:34
  71.6 27.1 %collective-permute-start.5 = (bf16[3,512,256]{2,1,0:T(8,128)(2,1)}, bf16[3,512,256]{2,1,0:T(8,128)(2,1)}, u32[]{:S(2)}, u32[]{:S(2)}) collective-permute-start(bf16[3,512,256]{2,1,0:T(8,128)(2,1)} %pad_maximum_fusion.p0.w0), channel_id=1, source_target_pairs={{0,96},{1,97},{2,98},{3,99},{4,28},{5,29},{6,30},{7,31},{8,104},{9... | collective-permute-start | bytes 2359304 | tf_op jit(solution)/shard_map/ppermute | solution.py:34
  88.0 18.1 %collective-permute-start.6 = (bf16[3,512,256]{2,1,0:T(8,128)(2,1)}, bf16[3,512,256]{2,1,0:T(8,128)(2,1)}, u32[]{:S(2)}, u32[]{:S(2)}) collective-permute-start(bf16[3,512,256]{2,1,0:T(8,128)(2,1)} %pad_maximum_fusion.p0.w0), channel_id=1, source_target_pairs={{0,64},{1,65},{2,66},{3,67},{4,20},{5,21},{6,22},{7,23},{8,72},{9,... | collective-permute-start | bytes 2359304 | tf_op jit(solution)/shard_map/ppermute | solution.py:34
  93.7 15.2 %collective-permute-start.27 = (bf16[3,512,256]{2,1,0:T(8,128)(2,1)}, bf16[3,512,256]{2,1,0:T(8,128)(2,1)}, u32[]{:S(2)}, u32[]{:S(2)}) collective-permute-start(bf16[3,512,256]{2,1,0:T(8,128)(2,1)} %pad_maximum_fusion.p0.w0), channel_id=1, source_target_pairs={{0,4},{1,5},{2,6},{3,7},{4,0},{5,1},{6,2},{7,3},{8,12},{9,13},{10,... | collective-permute-start | bytes 2359304 | tf_op jit(solution)/shard_map/ppermute | solution.py:34
  98.7 20.5 %collective-permute-start.31 = (bf16[4,32,2304]{2,1,0:T(8,128)(2,1)}, bf16[4,32,2304]{2,1,0:T(8,128)(2,1)S(1)}, u32[]{:S(2)}, u32[]{:S(2)}) collective-permute-start(bf16[4,32,2304]{2,1,0:T(8,128)(2,1)} %get-tuple-element.32.p0), channel_id=1, source_target_pairs={{0,8},{1,9},{2,10},{3,11},{4,36},{5,37},{6,38},{7,39},{8,16},{9,17... | collective-permute-start | bytes 1769480 | tf_op jit(solution)/shard_map/ppermute | solution.py:34
  106.0 26.1 %collective-permute-start.29 = (bf16[3,512,256]{2,1,0:T(8,128)(2,1)}, bf16[3,512,256]{2,1,0:T(8,128)(2,1)}, u32[]{:S(2)}, u32[]{:S(2)}) collective-permute-start(bf16[3,512,256]{2,1,0:T(8,128)(2,1)} %collective-permute-done.5.p2.w2), channel_id=1, source_target_pairs={{0,4},{1,5},{2,6},{3,7},{4,0},{5,1},{6,2},{7,3},{8,12},{9,13},{10,... | collective-permute-start | bytes 2359304 | tf_op jit(solution)/shard_map/ppermute | solution.py:34
  108.8 23.4 %collective-permute-start.30 = (bf16[3,512,256]{2,1,0:T(8,128)(2,1)}, bf16[3,512,256]{2,1,0:T(8,128)(2,1)}, u32[]{:S(2)}, u32[]{:S(2)}) collective-permute-start(bf16[3,512,256]{2,1,0:T(8,128)(2,1)} %collective-permute-done.6.p3.w3), channel_id=1, source_target_pairs={{0,4},{1,5},{2,6},{3,7},{4,0},{5,1},{6,2},{7,3},{8,12},{9,13},{10,... | collective-permute-start | bytes 2359304 | tf_op jit(solution)/shard_map/ppermute | solution.py:34
  120.1 15.2 %collective-permute-start.7 = (bf16[1024,256]{1,0:T(8,128)(2,1)}, bf16[1024,256]{1,0:T(8,128)(2,1)S(1)}, u32[]{:S(2)}, u32[]{:S(2)}) collective-permute-start(bf16[1024,256]{1,0:T(8,128)(2,1)} %get-tuple-element.22), channel_id=1, source_target_pairs={{0,3},{1,0},{2,1},{3,2},{4,7},{5,4},{6,5},{7,6},{8,11},{9,8},{10,9... | collective-permute-start | bytes 1572872 | tf_op jit(solution)/shard_map/ppermute | solution.py:34
  124.0 24.8 %collective-permute-start.8 = (bf16[1024,256]{1,0:T(8,128)(2,1)}, bf16[1024,256]{1,0:T(8,128)(2,1)S(1)}, u32[]{:S(2)}, u32[]{:S(2)}) collective-permute-start(bf16[1024,256]{1,0:T(8,128)(2,1)} %copy-done.17), channel_id=1, source_target_pairs={{0,1},{1,2},{2,3},{3,0},{4,5},{5,6},{6,7},{7,4},{8,9},{9,10},{10,1... | collective-permute-start | bytes 1572872 | tf_op jit(solution)/shard_map/ppermute | solution.py:34
  124.1 25.8 %collective-permute-start.9 = (bf16[1024,256]{1,0:T(8,128)(2,1)}, bf16[1024,256]{1,0:T(8,128)(2,1)S(1)}, u32[]{:S(2)}, u32[]{:S(2)}) collective-permute-start(bf16[1024,256]{1,0:T(8,128)(2,1)} %copy-done.16), channel_id=1, source_target_pairs={{0,2},{1,3},{2,0},{3,1},{4,6},{5,7},{6,4},{7,5},{8,10},{9,11},{10,... | collective-permute-start | bytes 1572872 | tf_op jit(solution)/shard_map/ppermute | solution.py:34
  132.2 21.0 %collective-permute-start.34 = (bf16[4,32,2304]{2,1,0:T(8,128)(2,1)S(1)}, bf16[4,32,2304]{2,1,0:T(8,128)(2,1)S(1)}, u32[]{:S(2)}, u32[]{:S(2)}) collective-permute-start(bf16[4,32,2304]{2,1,0:T(8,128)(2,1)S(1)} %get-tuple-element.34), channel_id=1, source_target_pairs={{0,32},{1,33},{2,34},{3,35},{4,12},{5,13},{6,14},{7,15},{8,40},{9,... | collective-permute-start | bytes 1769480 | tf_op jit(solution)/shard_map/ppermute | solution.py:34
  132.3 20.9 %collective-permute-start.35 = (bf16[4,32,2304]{2,1,0:T(8,128)(2,1)S(1)}, bf16[4,32,2304]{2,1,0:T(8,128)(2,1)S(1)}, u32[]{:S(2)}, u32[]{:S(2)}) collective-permute-start(bf16[4,32,2304]{2,1,0:T(8,128)(2,1)S(1)} %get-tuple-element.35), channel_id=1, source_target_pairs={{0,96},{1,97},{2,98},{3,99},{4,28},{5,29},{6,30},{7,31},{8,104},{9... | collective-permute-start | bytes 1769480 | tf_op jit(solution)/shard_map/ppermute | solution.py:34
  135.2 18.0 %collective-permute-start.36 = (bf16[4,32,2304]{2,1,0:T(8,128)(2,1)S(1)}, bf16[4,32,2304]{2,1,0:T(8,128)(2,1)S(1)}, u32[]{:S(2)}, u32[]{:S(2)}) collective-permute-start(bf16[4,32,2304]{2,1,0:T(8,128)(2,1)S(1)} %get-tuple-element.36), channel_id=1, source_target_pairs={{0,64},{1,65},{2,66},{3,67},{4,20},{5,21},{6,22},{7,23},{8,72},{9,... | collective-permute-start | bytes 1769480 | tf_op jit(solution)/shard_map/ppermute | solution.py:34
  (46 other events, 413.8 us)

commit v2 on v0

v2 whole, which is shorter than its diff:
```python
import math

import jax
import jax.numpy as jnp
from jax import lax
from jax.experimental import pallas as pl
from jax.experimental.pallas import tpu as pltpu
from jax.sharding import PartitionSpec as P

HEAD = 128
SIDE = 4
SHIFTS = (1, -1, 2)
SCALE = 1000
TOKEN = jax.ShapeDtypeStruct((8, HEAD), jnp.float32)

adapter_scale = 0.5
rope_theta = 500000.0
bf16 = jnp.bfloat16
f32 = jnp.float32
ANY = pl.BlockSpec(memory_space=pl.ANY)
VMEM = pl.BlockSpec(memory_space=pltpu.VMEM)
SMEM = pl.BlockSpec(memory_space=pltpu.SMEM)
NT = (((1,), (1,)), ((), ()))
TN = (((0,), (0,)), ((), ()))


def exchange(array, move):
    pairs = []
    for x in range(SIDE):
        for y in range(SIDE):
            for c in range(2):
                for z in range(SIDE):
                    x2, y2, c2, z2 = move(x, y, c, z)
                    target = (((x2 % SIDE) * SIDE + y2 % SIDE) * 2 + c2) * SIDE + z2 % SIDE
                    pairs.append((((x * SIDE + y) * 2 + c) * SIDE + z, target))
    return lax.ppermute(array, ("dp", "tensor"), pairs)


def along_z(array, shift):
    return exchange(array, lambda x, y, c, z: (x, y, c, z + shift))


def to_other_core(array):
    return exchange(array, lambda x, y, c, z: (x, y, 1 - c, z))


def along_z_apart(array, shift):
    return exchange(array, lambda x, y, c, z: (x, y, c, z + (shift if c == 0 else -shift)))


def along_line(array, shift):
    return exchange(
        array, lambda x, y, c, z: (x + shift, y, c, z) if c == 0 else (x, y + shift, c, z)
    )


def along_cross(array, shift):
    return exchange(
        array, lambda x, y, c, z: (x, y + shift, c, z) if c == 0 else (x + shift, y, c, z)
    )


def params(megabytes):
    return pltpu.CompilerParams(vmem_limit_bytes=megabytes << 20)


def cost(flops, moved):
    return pl.CostEstimate(flops=flops // SCALE, bytes_accessed=moved // SCALE, transcendentals=0)


def rope_tables(segments):
    places = jnp.arange(segments.shape[1], dtype=jnp.int32)
    earlier = jnp.concatenate([segments[:, :1] - 1, segments[:, :-1]], axis=1)
    starts = lax.cummax(jnp.where(segments != earlier, places[None, :], 0), axis=1)
    position = (places[None, :] - starts).astype(jnp.float32).reshape(-1)
    halves = jnp.arange(HEAD // 2, dtype=jnp.float32)
    inverse = jnp.exp(halves * (-2.0 * math.log(rope_theta) / HEAD))
    angles = position[:, None] * jnp.concatenate([inverse, inverse])[None, :]
    sign = jnp.where(jnp.arange(HEAD) < HEAD // 2, 1.0, -1.0)
    return jnp.stack([jnp.cos(angles), jnp.sin(angles) * sign[None, :]])


def unrotated(values, cosine, signed):
    return values * cosine + pltpu.roll(values, HEAD // 2, 1) * signed


def rotated(values, cosine, signed):
    return values * cosine - pltpu.roll(values, HEAD // 2, 1) * signed


def placed(slot, core):
    slot_x, slot_y = slot >> 4, (slot >> 2) & 3
    on_line = jnp.where(core == 0, slot_x, slot_y)
    on_cross = jnp.where(core == 0, slot_y, slot_x)
    row = ((slot & 3) + 2 * core) & 3
    return on_line, on_cross, row


def piece_from(here, there):
    apart = (here - there) & 3
    return jnp.where(apart == 3, 2, jnp.where(apart == 2, 3, apart))


def pack_kernel(count, *refs):
    out, sems = refs[-2], refs[-1]
    copies = []
    start = 0
    for i, piece in enumerate(refs[:count]):
        if piece.ndim < out.ndim:
            copies.append(pltpu.make_async_copy(piece, out.at[start], sems.at[i]))
            start += 1
        else:
            size = piece.shape[0]
            copies.append(pltpu.make_async_copy(piece, out.at[pl.ds(start, size)], sems.at[i]))
            start += size
    for copy in copies:
        copy.start()
    for copy in copies:
        copy.wait()


def pack(pieces, after=(), new_axis=False):
    if new_axis:
        shape = (len(pieces),) + pieces[0].shape
    else:
        shape = (sum(p.shape[0] for p in pieces),) + pieces[0].shape[1:]

    def kernel(*refs):
        pack_kernel(len(pieces), *refs)

    return pl.pallas_call(
        kernel,
        out_shape=jax.ShapeDtypeStruct(shape, pieces[0].dtype),
        in_specs=[ANY] * (len(pieces) + len(after)),
        out_specs=VMEM,
        scratch_shapes=[pltpu.SemaphoreType.DMA((len(pieces),))],
        compiler_params=params(16),
        cost_estimate=cost(0, 4 * math.prod(shape)),
    )(*pieces, *after)


def halves_kernel(index, at, down, up, _, mine, give, riding, sems):
    core = at[2]
    slots, both, width = down.shape
    wide = mine.shape[2] - HEAD
    lane = lax.broadcasted_iota(jnp.int32, riding.shape, 2)
    value = jnp.zeros(riding.shape, f32)
    for b in range(index.shape[0]):
        value = jnp.where(lane == b, index[b].astype(f32), value)
    riding[...] = value.astype(bf16)
    ends = [
        pltpu.make_async_copy(riding, out.at[:, :, pl.ds(wide, HEAD)], sems.at[i])
        for i, out in enumerate((mine, give))
    ]
    for copy in ends:
        copy.start()

    def halves(first, second):
        copies = [
            pltpu.make_async_copy(
                down.at[:, :, pl.ds(0, wide)], first.at[:, :, pl.ds(0, wide)], sems.at[2]
            ),
            pltpu.make_async_copy(
                down.at[:, :, pl.ds(wide, width - wide)],
                second.at[:, :, pl.ds(0, width - wide)],
                sems.at[3],
            ),
            pltpu.make_async_copy(
                up, second.at[:, :, pl.ds(width - wide, 2 * wide - width)], sems.at[4]
            ),
        ]
        for copy in copies:
            copy.start()
        for copy in copies:
            copy.wait()

    pl.when(core == 0)(lambda: halves(mine, give))
    pl.when(core == 1)(lambda: halves(give, mine))
    for copy in ends:
        copy.wait()


def split_maps(index, at, down, up, after):
    slots, both, width = down.shape
    wide = (width + up.shape[2]) // 2
    out = jax.ShapeDtypeStruct((slots, both, wide + HEAD), bf16)
    return pl.pallas_call(
        halves_kernel,
        out_shape=[out] * 2,
        in_specs=[SMEM] * 2 + [ANY] * 3,
        out_specs=[VMEM] * 2,
        scratch_shapes=[pltpu.VMEM((slots, both, HEAD), bf16), pltpu.SemaphoreType.DMA((5,))],
        compiler_params=params(16),
        cost_estimate=cost(0, 4 * down.size),
    )(index, at, down, up, after)


def lists_kernel(m0, m1, m2, m3, out, rows, sems):
    slots = m0.shape[0] // 2
    wide = m0.shape[2] - HEAD
    copies = [
        pltpu.make_async_copy(
            piece.at[k * slots, pl.ds(0, 16), pl.ds(wide, HEAD)], rows.at[2 * i + k], sems.at[2 * i + k]
        )
        for i, piece in enumerate((m0, m1, m2, m3))
        for k in range(2)
    ]
    for copy in copies:
        copy.start()
    for copy in copies:
        copy.wait()
    out[...] = rows[:, 0, :].astype(f32).astype(jnp.int32)


def riding_lists(pieces):
    return pl.pallas_call(
        lists_kernel,
        out_shape=jax.ShapeDtypeStruct((8, HEAD), jnp.int32),
        in_specs=[ANY] * 4,
        out_specs=VMEM,
        scratch_shapes=[pltpu.VMEM((8, 16, HEAD), bf16), pltpu.SemaphoreType.DMA((8,))],
        compiler_params=params(16),
        cost_estimate=cost(0, 1 << 16),
    )(*pieces)


def listed(lists, piece, b):
    return lists[2 * piece + b // 4, b % 4]


def pick_kernel(lists, positions, at, m0, m1, m2, m3, *rest):
    o1, o2, o3, sems = rest[-4:]
    line, cross, core = at[0], at[1], at[2]
    count, _, wide = o1.shape
    found = []
    for i, (row, out) in enumerate(((2, o1), (1, o2), (3, o3))):
        for b in range(count):
            on_line, on_cross, local = placed(positions[listed(lists, row, b)], core)
            piece = jnp.where(on_cross == cross, piece_from(line, on_line), SIDE)
            found.append((piece, out.at[b], sems.at[i * count + b]))
            for k, source in enumerate((m0, m1, m2, m3)):

                @pl.when(piece == k)
                def _():
                    pltpu.make_async_copy(
                        source.at[local, :, pl.ds(0, wide)], out.at[b], sems.at[i * count + b]
                    ).start()

    for piece, target, sem in found:

        @pl.when(piece < SIDE)
        def _():
            pltpu.make_async_copy(m0.at[0, :, pl.ds(0, wide)], target, sem).wait()


def pick(lists, positions, at, pieces, wide, blocks, after):
    count = 2 * blocks
    out = jax.ShapeDtypeStruct((count, pieces[0].shape[1], wide), bf16)
    return pl.pallas_call(
        pick_kernel,
        out_shape=[out] * 3,
        in_specs=[SMEM] * 3 + [ANY] * (4 + len(after)),
        out_specs=[VMEM] * 3,
        scratch_shapes=[pltpu.SemaphoreType.DMA((3 * count,))],
        compiler_params=params(60),
        cost_estimate=cost(0, 8 * pieces[0].size),
    )(lists, positions, at, *pieces, *after)


def start_block(lists, positions, at, line_pieces, cross_pieces, b, target, sem):
    line, cross, core = at[0], at[1], at[2]
    wide = cross_pieces[0].shape[2]
    on_line, on_cross, local = placed(positions[listed(lists, 0, b)], core)
    piece = piece_from(line, on_line)
    sender = piece_from(cross, on_cross)
    for k, source in enumerate(line_pieces):

        @pl.when((sender == 0) & (piece == k))
        def _():
            pltpu.make_async_copy(source.at[local, :, pl.ds(0, wide)], target, sem).start()

    for k, source in enumerate(cross_pieces):

        @pl.when(sender == k + 1)
        def _():
            pltpu.make_async_copy(source.at[b], target, sem).start()


def resolve_kernel(lists, positions, at, m0, m1, m2, m3, r1, r2, r3, mine, give, sems):
    blocks = mine.shape[0]
    targets = [give.at[b] for b in range(blocks)] + [mine.at[b] for b in range(blocks)]
    for b, target in enumerate(targets):
        start_block(lists, positions, at, (m0, m1, m2, m3), (r1, r2, r3), b, target, sems.at[b])
    for b, target in enumerate(targets):
        pltpu.make_async_copy(r1.at[0], target, sems.at[b]).wait()


def resolve(lists, positions, at, pieces, received):
    count, both, wide = received[0].shape
    out = jax.ShapeDtypeStruct((count // 2, both, wide), bf16)
    return pl.pallas_call(
        resolve_kernel,
        out_shape=[out] * 2,
        in_specs=[SMEM] * 3 + [ANY] * 7,
        out_specs=[VMEM] * 2,
        scratch_shapes=[pltpu.SemaphoreType.DMA((count,))],
        compiler_params=params(60),
        cost_estimate=cost(0, 2 * received[0].size),
    )(lists, positions, at, *pieces, *received)


def lora_kernel(at, hidden, back, mine, other, out, maps):
    core = at[2]
    blocks, both, _ = maps.shape
    wide = other.shape[2]
    width = hidden.shape[1]
    tokens = hidden.shape[0] // blocks

    @pl.when(core == 0)
    def _():
        maps[:, :, :wide] = mine[...]
        maps[:, :, wide:] = other[...]

    @pl.when(core == 1)
    def _():
        maps[:, :, :wide] = other[...]
        maps[:, :, wide:] = mine[...]

    half = lax.broadcasted_iota(jnp.int32, (both, tokens), 0) < both // 2
    for b in range(blocks):
        rows = pl.ds(b * tokens, tokens)
        down = maps[b, :, :width]
        up = maps[b, :, width:]
        into = lax.dot_general(down, hidden[rows, :], NT, preferred_element_type=f32)
        keys = lax.dot_general(up, back[0, rows, :], NT, preferred_element_type=f32)
        values = lax.dot_general(up, back[1, rows, :], NT, preferred_element_type=f32)
        out[:both, rows] = into.astype(bf16)
        out[both:, rows] = jnp.where(half, keys, values).astype(bf16)


def lora(at, hidden, back, mine, other):
    blocks, both, wide = other.shape
    return pl.pallas_call(
        lora_kernel,
        out_shape=[
            jax.ShapeDtypeStruct((2 * both, hidden.shape[0]), bf16),
            jax.ShapeDtypeStruct((blocks, both, 2 * wide), bf16),
        ],
        in_specs=[SMEM] + [VMEM] * 4,
        out_specs=[VMEM] * 2,
        compiler_params=params(24),
        cost_estimate=cost(2 * both * hidden.size, 2 * hidden.size + 4 * other.size),
    )(at, hidden, back, mine, other)


def parts_kernel(at, hidden, back, t0, t1, t2, t3, _1, _2, mine, give, sums, again, part):
    again[...] = back[...]
    core = at[2]
    blocks, both, _ = part.shape
    wide = mine.shape[2]
    width = hidden.shape[1]
    tokens = hidden.shape[0] // blocks
    rank = both // 2
    total = t0[...].astype(f32) + t1[...].astype(f32) + t2[...].astype(f32) + t3[...].astype(f32)
    sums[:both, :] = total[:both].astype(bf16)
    sums[both:, :] = (total[both:] * adapter_scale).astype(bf16)
    for b in range(blocks):
        rows = pl.ds(b * tokens, tokens)
        inner = sums[both:, rows]
        into = sums[:both, rows]
        down = jnp.dot(inner, hidden[rows, :], preferred_element_type=f32)
        part[b, :, :width] = down.astype(bf16)
        keys = jnp.dot(into[:rank], back[0, rows, :], preferred_element_type=f32)
        values = jnp.dot(into[rank:], back[1, rows, :], preferred_element_type=f32)
        part[b, :rank, width:] = (keys * adapter_scale).astype(bf16)
        part[b, rank:, width:] = (values * adapter_scale).astype(bf16)

    @pl.when(core == 0)
    def _():
        mine[...] = part[:, :, :wide]
        give[...] = part[:, :, wide:]

    @pl.when(core == 1)
    def _():
        mine[...] = part[:, :, wide:]
        give[...] = part[:, :, :wide]


def parts(at, hidden, back, pieces, blocks, after):
    both = pieces[0].shape[0] // 2
    wide = (hidden.shape[1] + back.shape[2]) // 2
    return pl.pallas_call(
        parts_kernel,
        out_shape=[
            jax.ShapeDtypeStruct((blocks, both, wide), bf16),
            jax.ShapeDtypeStruct((blocks, both, wide), bf16),
            jax.ShapeDtypeStruct(pieces[0].shape, bf16),
            jax.ShapeDtypeStruct(back.shape, bf16),
        ],
        in_specs=[SMEM] + [VMEM] * 6 + [ANY] * 2,
        out_specs=[VMEM] * 4,
        scratch_shapes=[pltpu.VMEM((blocks, both, 2 * wide), bf16)],
        compiler_params=params(24),
        cost_estimate=cost(2 * both * hidden.size, 4 * hidden.size),
    )(at, hidden, back, *pieces, *after)


def collect_kernel(lists, positions, at, p0, p1, p2, p3, *rest):
    o0, o1, o2, o3, total = rest[-5:]
    line, cross, core = at[0], at[1], at[2]
    slots = o0.shape[0]
    total[...] = jnp.zeros_like(total)
    for i, piece in enumerate((p0, p1, p2, p3)):
        for b in range(piece.shape[0]):
            on_line, on_cross, local = placed(positions[listed(lists, i, b)], core)

            @pl.when(on_cross == cross)
            def _():
                slot = on_line * slots + local
                total[slot] = total[slot] + piece[b].astype(f32)

    for shift, out in zip((0,) + SHIFTS, (o0, o1, o2, o3)):
        target = (line + shift + SIDE) % SIDE
        out[...] = total[pl.ds(target * slots, slots)].astype(bf16)


def collect(lists, positions, at, pieces, slots, after):
    _, both, wide = pieces[0].shape
    return pl.pallas_call(
        collect_kernel,
        out_shape=[jax.ShapeDtypeStruct((slots, both, wide), bf16)] * 4,
        in_specs=[SMEM] * 3 + [VMEM] * 4 + [ANY] * len(after),
        out_specs=[VMEM] * 4,
        scratch_shapes=[pltpu.VMEM((4 * slots, both, wide), f32)],
        compiler_params=params(60),
        cost_estimate=cost(8 * pieces[0].size, 16 * pieces[0].size),
    )(lists, positions, at, *pieces, *after)


def turn_kernel(tables, key_grad, value_grad, back):
    for h in range(key_grad.shape[1] // HEAD):
        lanes = slice(h * HEAD, (h + 1) * HEAD)
        back[0, :, lanes] = unrotated(
            key_grad[:, lanes].astype(f32), tables[0], tables[1]
        ).astype(bf16)
    back[1] = value_grad[...]


def turn(tables, key_grad, value_grad):
    return pl.pallas_call(
        turn_kernel,
        out_shape=jax.ShapeDtypeStruct((2,) + key_grad.shape, bf16),
        in_specs=[VMEM] * 3,
        out_specs=VMEM,
        compiler_params=params(16),
        cost_estimate=cost(0, 10 * key_grad.size),
    )(tables, key_grad, value_grad)


def send_kernel(at, keys, values, near, far, sems):
    core, z = at[2], at[3]
    width = far.shape[0]

    def copies(mine, theirs, shift):
        rows = pl.ds(pl.multiple_of(((z + shift + SIDE) % SIDE) * width, 256), width)
        across = pl.ds(pl.multiple_of(((z + 2) % SIDE) * width, 256), width)
        found = [
            pltpu.make_async_copy(mine.at[rows], near.at[0], sems.at[0]),
            pltpu.make_async_copy(theirs.at[rows], near.at[1], sems.at[1]),
            pltpu.make_async_copy(mine.at[across], far, sems.at[2]),
        ]
        for copy in found:
            copy.start()
        for copy in found:
            copy.wait()

    pl.when(core == 0)(lambda: copies(keys, values, 1))
    pl.when(core == 1)(lambda: copies(values, keys, -1))


def to_send(at, keys, values):
    rows, kv = keys.shape[0] // SIDE, keys.shape[1]
    return pl.pallas_call(
        send_kernel,
        out_shape=[
            jax.ShapeDtypeStruct((2, rows, kv), bf16),
            jax.ShapeDtypeStruct((rows, kv), bf16),
        ],
        in_specs=[SMEM] + [ANY] * 2,
        out_specs=[VMEM] * 2,
        scratch_shapes=[pltpu.SemaphoreType.DMA((3,))],
        compiler_params=params(60),
        cost_estimate=cost(0, 12 * rows * kv),
    )(at, keys, values)


def weight_sources(at, keys, values, near, near_theirs, far, far_theirs):
    core = at[2]
    found = []
    for kind in range(2):
        own = ((keys, (core + kind) % 2 == 0), (values, (core + kind) % 2 == 1))
        found.append(own)
        for piece in (near.at[kind], near_theirs.at[1 - kind], (far, far_theirs)[kind]):
            found.append(((piece, None),))
    return found


def start_weights(sources, own_rows, rows, target, sem):
    for source, condition in sources:
        if condition is None:
            pltpu.make_async_copy(source.at[rows], target, sem).start()
        else:

            @pl.when(condition)
            def _():
                pltpu.make_async_copy(source.at[own_rows], target, sem).start()


def forward_kernel(
    at, hidden, keys, values, near, near_theirs, far, far_theirs, _, o0, o1, o2, o3, done, weights, sems
):
    width = weights.shape[1]
    sources = weight_sources(at, keys, values, near, near_theirs, far, far_theirs)
    own_rows = pl.ds(pl.multiple_of(at[3] * width, 256), width)
    order = [4 * kind + k for k in range(4) for kind in range(2)]

    def start(step):
        i = order[step]
        start_weights(sources[i], own_rows, pl.ds(0, width), weights.at[i], sems.at[i])

    for step in range(3):
        start(step)
    done[...] = jnp.zeros_like(done)
    for step, i in enumerate(order):
        if step + 3 < len(order):
            start(step + 3)
        pltpu.make_async_copy(far, weights.at[i], sems.at[i]).wait()
        (o0, o1, o2, o3)[i % 4][i // 4] = jnp.dot(
            hidden[...], weights[i], preferred_element_type=f32
        ).astype(bf16)


def forward(at, hidden, keys, values, pieces, after):
    rows, width = hidden.shape
    kv = keys.shape[1]
    out = jax.ShapeDtypeStruct((2, rows, kv), bf16)
    return pl.pallas_call(
        forward_kernel,
        out_shape=[out] * 4 + [TOKEN],
        in_specs=[SMEM, VMEM] + [ANY] * 7,
        out_specs=[VMEM] * 5,
        scratch_shapes=[pltpu.VMEM((8, width, kv), bf16), pltpu.SemaphoreType.DMA((8,))],
        compiler_params=params(40),
        cost_estimate=cost(SCALE * 32 * hidden.size * kv, SCALE * 32 * width * kv),
    )(at, hidden, keys, values, *pieces, after)


def backward_kernel(
    at, b0, b1, b2, b3, keys, values, near, near_theirs, far, far_theirs, sums, maps, *rest
):
    out, done, weights, back, sems = rest[-5:]
    core, z = at[2], at[3]
    kv = b0.shape[2]
    width = weights.shape[1]
    quarter = width // SIDE
    blocks, both, _ = maps.shape
    sources = weight_sources(at, keys, values, near, near_theirs, far, far_theirs)

    def load(j):
        rows = pl.ds(j * quarter, quarter)
        own_rows = pl.ds(pl.multiple_of(z * width + j * quarter, 256), quarter)
        for i in range(8):
            start_weights(sources[i], own_rows, rows, weights.at[i, rows], sems.at[8 * j + i])

    load(0)
    load(1)
    done[...] = jnp.zeros_like(done)
    for kind in range(2):
        for k, part in enumerate((b0, b1, b2, b3)):
            start = (4 * kind + k) * kv
            back[:, start : start + kv] = part[(core + kind) % 2]
    for j in range(SIDE):
        rows = pl.ds(j * quarter, quarter)
        if j + 2 < SIDE:
            load(j + 2)
        for i in range(8):
            pltpu.make_async_copy(far.at[rows], weights.at[i, rows], sems.at[8 * j + i]).wait()
        columns = slice(j * quarter, (j + 1) * quarter)
        wide = jnp.concatenate([weights[i, columns, :] for i in range(8)], axis=1)
        total = lax.dot_general(back[...], wide, NT, preferred_element_type=f32)
        tokens = total.shape[0] // blocks
        for b in range(blocks):
            block = slice(b * tokens, (b + 1) * tokens)
            out[block, columns] = (
                total[block, :]
                + lax.dot_general(
                    sums[both:, block], maps[b, :, columns], TN, preferred_element_type=f32
                )
            ).astype(bf16)


def backward(at, backs, keys, values, pieces, sums, maps, after):
    _, rows, kv = backs[0].shape
    width = keys.shape[0] // SIDE
    return pl.pallas_call(
        backward_kernel,
        out_shape=[jax.ShapeDtypeStruct((rows, width), bf16), TOKEN],
        in_specs=[SMEM] + [VMEM] * 4 + [ANY] * 6 + [VMEM] * 2 + [ANY] * len(after),
        out_specs=[VMEM] * 2,
        scratch_shapes=[
            pltpu.VMEM((8, width, kv), bf16),
            pltpu.VMEM((rows, 8 * kv), bf16),
            pltpu.SemaphoreType.DMA((32,)),
        ],
        compiler_params=params(60),
        cost_estimate=cost(SCALE * 48 * rows * width * kv, SCALE * 32 * width * kv),
    )(at, *backs, keys, values, *pieces, sums, maps, *after)


def finish_kernel(at, sums, maps, tables, t0, t1, t2, t3, _, key_out, value_out):
    core = at[2]
    blocks, both, wide = maps.shape
    rank = both // 2
    rows, kv = key_out.shape
    tokens = rows // blocks
    for b in range(blocks):
        block = slice(b * tokens, (b + 1) * tokens)
        for kind, out in enumerate((key_out, value_out)):
            first = kind * rank
            total = sum(t[(core + kind) % 2, block].astype(f32) for t in (t0, t1, t2, t3))
            total = total + adapter_scale * lax.dot_general(
                sums[first : first + rank, block],
                maps[b, first : first + rank, wide - kv :],
                TN,
                preferred_element_type=f32,
            )
            if kind == 1:
                out[block, :] = total.astype(bf16)
            else:
                for h in range(kv // HEAD):
                    lanes = slice(h * HEAD, (h + 1) * HEAD)
                    out[block, lanes] = rotated(
                        total[:, lanes], tables[0, block, :], tables[1, block, :]
                    ).astype(bf16)


def finish(at, sums, maps, tables, terms, after):
    _, rows, kv = terms[0].shape
    return pl.pallas_call(
        finish_kernel,
        out_shape=[jax.ShapeDtypeStruct((rows, kv), bf16)] * 2,
        in_specs=[SMEM] + [VMEM] * 7 + [ANY],
        out_specs=[VMEM] * 2,
        compiler_params=params(24),
        cost_estimate=cost(0, 16 * terms[0].size),
    )(at, sums, maps, tables, *terms, after)


def give_kernel(a0, a1, a2, a3, *rest):
    out = rest[-1]
    n = out.shape[0]
    out[...] = sum(a[n:].astype(f32) for a in (a0, a1, a2, a3))


def sums_kernel(at, a0, a1, a2, a3, crossed, down, up):
    core = at[2]
    n, _, width = down.shape
    wide = crossed.shape[2]
    mine = sum(a[:n].astype(f32) for a in (a0, a1, a2, a3))

    def store(first, second):
        down[:, :, :wide] = first
        down[:, :, wide:] = second[:, :, : width - wide]
        up[...] = second[:, :, width - wide :]

    pl.when(core == 0)(lambda: store(mine, crossed[...]))
    pl.when(core == 1)(lambda: store(crossed[...], mine))


def gather_sums(at, arrived, slots_here, width, after):
    _, both, wide = arrived[0].shape
    give = pl.pallas_call(
        give_kernel,
        out_shape=jax.ShapeDtypeStruct((slots_here, both, wide), f32),
        in_specs=[VMEM] * 4 + [ANY] * len(after),
        out_specs=VMEM,
        compiler_params=params(16),
        cost_estimate=cost(0, 8 * arrived[0].size),
    )(*arrived, *after)
    return pl.pallas_call(
        sums_kernel,
        out_shape=[
            jax.ShapeDtypeStruct((slots_here, both, width), f32),
            jax.ShapeDtypeStruct((slots_here, both, 2 * wide - width), f32),
        ],
        in_specs=[SMEM] + [VMEM] * 5,
        out_specs=[VMEM] * 2,
        compiler_params=params(16),
        cost_estimate=cost(0, 8 * arrived[0].size),
    )(at, *arrived, to_other_core(give))


def per_device(
    hidden,
    key_weight_frozen,
    value_weight_frozen,
    adapter_down_maps,
    adapter_up_maps,
    block_adapter_index,
    segment_document_index,
    adapter_position,
    key_gradient,
    value_gradient,
):
    width = hidden.shape[1]
    kv_here = key_weight_frozen.shape[1]
    blocks = block_adapter_index.shape[0]
    slots_here, _, rank, _ = adapter_down_maps.shape
    both = 2 * rank
    wide = width + kv_here
    quarter = width // SIDE
    dp = lax.axis_index("dp")
    z = lax.axis_index("tensor")
    core = dp % 2
    x, y = dp // 8, (dp // 2) % 4
    first = core == 0
    line = jnp.where(first, x, y)
    cross = jnp.where(first, y, x)
    at = jnp.stack([line, cross, core, z])

    half = wide // 2
    sent_near, sent_far = to_send(at, key_weight_frozen, value_weight_frozen)
    mine_half, give_half = split_maps(
        block_adapter_index,
        at,
        adapter_down_maps.reshape(slots_here, both, width),
        adapter_up_maps.reshape(slots_here, both, kv_here),
        sent_near,
    )
    maps_chip = pack([mine_half, to_other_core(give_half)])
    maps_line = [maps_chip] + [along_line(maps_chip, d) for d in SHIFTS]
    lists_here = riding_lists(maps_line)
    lists = to_other_core(lists_here)
    sent_far, _ = lax.optimization_barrier((sent_far, lists_here))
    segments, _ = lax.optimization_barrier((segment_document_index, maps_chip))
    tables = rope_tables(segments)
    back = turn(tables, key_gradient, value_gradient)
    picked = pick(lists, adapter_position, at, maps_line, half, blocks, (back,))
    received = [along_cross(p, d) for p, d in zip(picked, SHIFTS)]

    near = along_z_apart(sent_near, 1)
    far = along_z(sent_far, 2)
    mine_maps, give_maps = resolve(lists, adapter_position, at, maps_line, received)
    into, maps = lora(at, hidden, back, mine_maps, to_other_core(give_maps))
    near, far, _ = lax.optimization_barrier((near, far, into))
    pieces = [near, to_other_core(near), far, to_other_core(far)]
    terms = [into] + [along_z(into, d) for d in SHIFTS]
    part_mine, part_give, sums, back = parts(
        at, hidden, back, terms, blocks, (pieces[1], pieces[3])
    )
    part = pack([to_other_core(part_give), part_mine])
    *partial, forward_done = forward(
        at, hidden, key_weight_frozen, value_weight_frozen, pieces, part
    )

    part_from = [part] + [along_cross(part, d) for d in SHIFTS]
    back_later, _ = lax.optimization_barrier((back, forward_done))
    backs = [back, along_z_apart(back, 1), along_z_apart(back, -1), along_z(back_later, 2)]
    line_sums = collect(
        lists, adapter_position, at, part_from, 2 * slots_here, [forward_done] + backs[1:3]
    )
    arrived = [line_sums[0]] + [along_line(s, d) for s, d in zip(line_sums[1:], SHIFTS)]
    key_terms = [
        partial[0],
        along_z_apart(partial[1], -1),
        along_z_apart(partial[2], 1),
        along_z(partial[3], 2),
    ]
    hidden_gradient, backward_done = backward(
        at, backs, key_weight_frozen, value_weight_frozen, pieces, sums, maps, line_sums[:1]
    )
    grad_down, grad_up = gather_sums(at, arrived, slots_here, width, (backward_done,))
    key_out, value_out = finish(at, sums, maps, tables, key_terms, backward_done)
    return (
        key_out,
        value_out,
        hidden_gradient,
        grad_down.reshape(adapter_down_maps.shape),
        grad_up.reshape(adapter_up_maps.shape),
    )


def solution(mesh):
    return jax.shard_map(
        per_device,
        mesh=mesh,
        in_specs=(
            P("dp", "tensor"),
            P(None, "tensor"),
            P(None, "tensor"),
            P("dp", None, None, "tensor"),
            P("dp", None, None, "tensor"),
            P("dp"),
            P("dp", None),
            P(),
            P("dp", "tensor"),
            P("dp", "tensor"),
        ),
        out_specs=(
            P("dp", "tensor"),
            P("dp", "tensor"),
            P("dp", "tensor"),
            P("dp", None, None, "tensor"),
            P("dp", None, None, "tensor"),
        ),
        check_vma=False,
    )
```

time: 511 us -> 134 us (0.26)
  waiting for transfers between devices: 403 us -> 36.6 us
  matrix products: 54.4 us -> 0 us
  Pallas kernels: 0 us -> 46.4 us
  starting transfers between devices: 0.46 us -> 38.7 us
  local copies, waits for them, and re-layouts: 26.1 us -> 8.31 us
  between operations: 15 us -> 1.74 us
  other arithmetic: 10.9 us -> 2.28 us
    reduce_scatter x3 -> x0, waiting for transfers between devices: 234 us -> none  [the longest x1 94.3 us: per_device(): lax.psum_scatter(dense_down.astype(jnp.bfloat16), 'dp', scatter_dimension...]
    all_gather x3 -> x0, waiting for transfers between devices: 152 us -> none  [the longest x1 59.6 us: per_device(): columns = lax.all_gather(hidden, 'tensor', axis=1, tiled=True)]
    dot_general x12 -> x0, matrix products: 54.4 us -> none  [the longest x1 12.8 us: per_device(): lax.dot_general(value_gradient, value_weight_frozen, dims, preferred_elem...]
    pallas_call x0 -> x16, Pallas kernels: none -> 46.4 us  [the longest x1 12.7 us: forward(): pl.pallas_call(forward_kernel, out_shape=[out] * 4 + [TOKEN], in_specs=[S...]
    ppermute x0 -> x30, starting transfers between devices: none -> 38.7 us  [exchange(): return lax.ppermute(array, ('dp', 'tensor'), pairs)]
    ppermute x0 -> x30, waiting for transfers between devices: none -> 36.6 us  [exchange(): return lax.ppermute(array, ('dp', 'tensor'), pairs)]
    convert_element_type x5 -> x0, local copies, waits for them, and re-layouts: 14.8 us -> none  [the longest x1 12.2 us: per_device(): dense_down.astype(jnp.bfloat16)]
    psum x1 -> x0, waiting for transfers between devices: 14.7 us -> none  [per_device(): lax.psum(in_part.astype(jnp.bfloat16), 'tensor').astype(jnp.float32)]
  transfers between devices with their start and end apart: 7 -> 30, of which waited for: 7 -> 11; matrix products, arithmetic and copies ran while one was open for 16% -> 2% of each run, Pallas kernels for 0% -> 29%
where the time goes in v2:
time: 134 us
  Pallas kernels  46.4 us (35%)
  starting transfers between devices  38.7 us (29%)
  waiting for transfers between devices  36.6 us (27%)
  local copies, waits for them, and re-layouts  8.31 us (6%)
  other arithmetic  2.28 us (2%)
  between operations  1.74 us (1%)
    ppermute x30, starting transfers between devices, exchange(): return lax.ppermute(array, ('dp', 'tensor'), pairs)  38.7 us
    ppermute x30, waiting for transfers between devices, exchange(): return lax.ppermute(array, ('dp', 'tensor'), pairs)  36.6 us
    pallas_call x1, Pallas kernels, forward(): pl.pallas_call(forward_kernel, out_shape=[out] * 4 + [TOKEN], in_specs=[S...  12.7 us
    pallas_call x1, Pallas kernels, backward(): pl.pallas_call(backward_kernel, out_shape=[jax.ShapeDtypeStruct((rows, wi...  10.6 us
    unnamed x68, local copies, waits for them, and re-layouts  7.53 us
    pallas_call x1, Pallas kernels, to_send(): pl.pallas_call(send_kernel, out_shape=[jax.ShapeDtypeStruct((2, rows, kv)...  4.37 us
    pallas_call x1, Pallas kernels, pick(): pl.pallas_call(pick_kernel, out_shape=[out] * 3, in_specs=[SMEM] * 3 + [A...  3.53 us
    pallas_call x1, Pallas kernels, collect(): pl.pallas_call(collect_kernel, out_shape=[jax.ShapeDtypeStruct((slots, bo...  3.5 us
  transfers between devices with their start and end apart: 30, of which 11 were waited for; matrix products, arithmetic and copies ran while one was open for 2% of the time, Pallas kernels for 29%

profile of v2, /device:TPU:1, one launch (start us, length us, event | category | flops | bytes accessed | tf_op | source)
XLA Modules:
  0.0 134.0 jit_solution(95484326622325154)
XLA Ops:
  1.3 4.4 %shard_map.137 = (bf16[2,2048,256]{2,1,0:T(8,128)(2,1)}, bf16[2048,256]{1,0:T(8,128)(2,1)}) custom-call(s32[4]{0:T(128)} %pad_add_fusion.at, bf16[8192,256]{1,0:T(8,128)(2,1)} %keys.5, bf16[8192,256]{1,0:T(8,128)(2,1)} %values.5), custom_call_target="tpu_custom_call" | custom-call | bytes 6291 | tf_op jit(solution)/shard_map/pallas_call | solution.py:483
  5.7 4.7 %collective-permute-start.12 = (bf16[2,2048,256]{2,1,0:T(8,128)(2,1)}, bf16[2,2048,256]{2,1,0:T(8,128)(2,1)}, u32[]{:S(2)}, u32[]{:S(2)}) collective-permute-start(bf16[2,2048,256]{2,1,0:T(8,128)(2,1)} %get-tuple-element.40._), channel_id=1, source_target_pairs={{0,1},{1,2},{2,3},{3,0},{4,7},{5,4},{6,5},{7,6},{8,9},{9,10},{10,1... | collective-permute-start | bytes 6291464 | tf_op jit(solution)/shard_map/ppermute | solution.py:36
  14.6 3.0 %collective-permute-start.3 = (bf16[4,32,1280]{2,1,0:T(8,128)(2,1)S(1)}, bf16[4,32,1280]{2,1,0:T(8,128)(2,1)S(1)}, u32[]{:S(2)}, u32[]{:S(2)}) collective-permute-start(bf16[4,32,1280]{2,1,0:T(8,128)(2,1)S(1)} %shard_map.139.m0), channel_id=1, source_target_pairs={{0,64},{1,65},{2,66},{3,67},{4,20},{5,21},{6,22},{7,23},{8,72},{9,... | collective-permute-start | bytes 983048 | tf_op jit(solution)/shard_map/ppermute | solution.py:36
  22.4 4.0 %collective-permute-done.2.m2 = bf16[4,32,1280]{2,1,0:T(8,128)(2,1)S(1)} collective-permute-done((bf16[4,32,1280]{2,1,0:T(8,128)(2,1)S(1)}, bf16[4,32,1280]{2,1,0:T(8,128)(2,1)S(1)}, u32[]{:S(2)}, u32[]{:S(2)}) %collective-permute-start.2) | collective-permute-done | bytes 327712 | tf_op jit(solution)/shard_map/ppermute | solution.py:36
  26.5 1.8 %collective-permute-start.13 = (bf16[2048,256]{1,0:T(8,128)(2,1)}, bf16[2048,256]{1,0:T(8,128)(2,1)}, u32[]{:S(2)}, u32[]{:S(2)}) collective-permute-start(bf16[2048,256]{1,0:T(8,128)(2,1)} %get-tuple-element.51), channel_id=1, source_target_pairs={{0,2},{1,3},{2,0},{3,1},{4,6},{5,7},{6,4},{7,5},{8,10},{9,11},{10,... | collective-permute-start | bytes 3145736 | tf_op jit(solution)/shard_map/ppermute | solution.py:36
  31.9 3.5 %shard_map.142 = (bf16[8,32,1152]{2,1,0:T(8,128)(2,1)}, bf16[8,32,1152]{2,1,0:T(8,128)(2,1)}, bf16[8,32,1152]{2,1,0:T(8,128)(2,1)}) custom-call(s32[8,128]{1,0:T(8,128)} %collective-permute-done.4.lists, s32[64]{0:T(128)} %positions.5, s32[4]{0:T(128)} %pad_add_fusion.at, bf16[4,32,1280]{2,1,0:T(8,128)(2,1)} %copy-done.3, bf16[4,32,1280]{2,1,0:T(8,128)(2,1)} %copy-done.6, ...), custom_call_target="tpu_custom_call" | custom-call | bytes 1310 | tf_op jit(solution)/shard_map/pallas_call | solution.py:259
  36.4 1.8 %collective-permute-start.6 = (bf16[8,32,1152]{2,1,0:T(8,128)(2,1)}, bf16[8,32,1152]{2,1,0:T(8,128)(2,1)}, u32[]{:S(2)}, u32[]{:S(2)}) collective-permute-start(bf16[8,32,1152]{2,1,0:T(8,128)(2,1)} %get-tuple-element.45), channel_id=1, source_target_pairs={{0,24},{1,25},{2,26},{3,27},{4,100},{5,101},{6,102},{7,103},{8,0},... | collective-permute-start | bytes 1769480 | tf_op jit(solution)/shard_map/ppermute | solution.py:36
  39.3 6.8 %collective-permute-done.5.r1 = bf16[8,32,1152]{2,1,0:T(8,128)(2,1)S(1)} collective-permute-done((bf16[8,32,1152]{2,1,0:T(8,128)(2,1)}, bf16[8,32,1152]{2,1,0:T(8,128)(2,1)S(1)}, u32[]{:S(2)}, u32[]{:S(2)}) %collective-permute-start.5) | collective-permute-done | bytes 589856 | tf_op jit(solution)/shard_map/ppermute | solution.py:36
  46.0 5.6 %collective-permute-done.6.r2 = bf16[8,32,1152]{2,1,0:T(8,128)(2,1)} collective-permute-done((bf16[8,32,1152]{2,1,0:T(8,128)(2,1)}, bf16[8,32,1152]{2,1,0:T(8,128)(2,1)}, u32[]{:S(2)}, u32[]{:S(2)}) %collective-permute-start.6) | collective-permute-done | bytes 589856 | tf_op jit(solution)/shard_map/ppermute | solution.py:36
  53.1 2.8 %shard_map.143 = (bf16[4,32,1152]{2,1,0:T(8,128)(2,1)}, bf16[4,32,1152]{2,1,0:T(8,128)(2,1)}) custom-call(s32[8,128]{1,0:T(8,128)} %collective-permute-done.4.lists, s32[64]{0:T(128)} %positions.5, s32[4]{0:T(128)} %pad_add_fusion.at, bf16[4,32,1280]{2,1,0:T(8,128)(2,1)} %copy-done.3, bf16[4,32,1280]{2,1,0:T(8,128)(2,1)} %copy-done.6, ...), custom_call_target="tpu_custom_call" | custom-call | bytes 589 | tf_op jit(solution)/shard_map/pallas_call | solution.py:301
  64.6 2.2 %collective-permute-done.11.t3 = bf16[64,512]{1,0:T(8,128)(2,1)S(1)} collective-permute-done((bf16[64,512]{1,0:T(8,128)(2,1)S(1)}, bf16[64,512]{1,0:T(8,128)(2,1)S(1)}, u32[]{:S(2)}, u32[]{:S(2)}) %collective-permute-start.11) | collective-permute-done | bytes 65568 | tf_op jit(solution)/shard_map/ppermute | solution.py:36
  68.3 1.9 %shard_map.145 = (bf16[4,32,1152]{2,1,0:T(8,128)(2,1)S(1)}, bf16[4,32,1152]{2,1,0:T(8,128)(2,1)S(1)}, bf16[64,512]{1,0:T(8,128)(2,1)S(1)}, bf16[2,512,256]{2,1,0:T(8,128)(2,1)}) custom-call(s32[4]{0:T(128)S(1)} %copy-done.21, bf16[512,2048]{1,0:T(8,128)(2,1)S(1)} %copy-done, bf16[2,512,256]{2,1,0:T(8,128)(2,1)S(1)} %copy-done.2, ...), custom_call_target="tpu_custom_call" | custom-call | flops 67108 | bytes 4194 | tf_op jit(solution)/shard_map/pallas_call | solution.py:392
  70.2 1.8 %collective-permute-start.16 = (bf16[4,32,1152]{2,1,0:T(8,128)(2,1)S(1)}, bf16[4,32,1152]{2,1,0:T(8,128)(2,1)S(1)}, u32[]{:S(2)}, u32[]{:S(2)}) collective-permute-start(bf16[4,32,1152]{2,1,0:T(8,128)(2,1)S(1)} %get-tuple-element.56), channel_id=1, source_target_pairs={{0,4},{1,5},{2,6},{3,7},{4,0},{5,1},{6,2},{7,3},{8,12},{9,13},{10,... | collective-permute-start | bytes 884744 | tf_op jit(solution)/shard_map/ppermute | solution.py:36
  72.0 2.7 %collective-permute-start.20 = (bf16[2,512,256]{2,1,0:T(8,128)(2,1)}, bf16[2,512,256]{2,1,0:T(8,128)(2,1)S(1)}, u32[]{:S(2)}, u32[]{:S(2)}) collective-permute-start(bf16[2,512,256]{2,1,0:T(8,128)(2,1)} %get-tuple-element.64.b0), channel_id=1, source_target_pairs={{0,1},{1,2},{2,3},{3,0},{4,7},{5,4},{6,5},{7,6},{8,9},{9,10},{10,1... | collective-permute-start | bytes 1572872 | tf_op jit(solution)/shard_map/ppermute | solution.py:36
  74.8 2.4 %collective-permute-start.25 = (bf16[8,32,1152]{2,1,0:T(8,128)(2,1)S(1)}, bf16[8,32,1152]{2,1,0:T(8,128)(2,1)S(1)}, u32[]{:S(2)}, u32[]{:S(2)}) collective-permute-start(bf16[8,32,1152]{2,1,0:T(8,128)(2,1)S(1)} %shard_map.146._.p0), channel_id=1, source_target_pairs={{0,16},{1,17},{2,18},{3,19},{4,68},{5,69},{6,70},{7,71},{8,24},{9,... | collective-permute-start | bytes 1769480 | tf_op jit(solution)/shard_map/ppermute | solution.py:36
  78.7 12.7 %shard_map.147 = (bf16[2,512,256]{2,1,0:T(8,128)(2,1)S(1)}, bf16[2,512,256]{2,1,0:T(8,128)(2,1)}, bf16[2,512,256]{2,1,0:T(8,128)(2,1)}, bf16[2,512,256]{2,1,0:T(8,128)(2,1)}, f32[8,128]{1,0:T(8,128)S(1)}) custom-call(s32[4]{0:T(128)S(1)} %copy-done.21, bf16[512,2048]{1,0:T(8,128)(2,1)S(1)} %copy-done, bf16[8192,256]{1,0:T(8,128)(2,1)} %keys.5, ...), custom_call_target="tpu_custom_call" | custom-call | flops 8589934592 | bytes 16777216 | tf_op jit(solution)/shard_map/pallas_call | solution.py:547
  94.1 3.5 %shard_map.148 = (bf16[4,32,1152]{2,1,0:T(8,128)(2,1)}, bf16[4,32,1152]{2,1,0:T(8,128)(2,1)}, bf16[4,32,1152]{2,1,0:T(8,128)(2,1)}, bf16[4,32,1152]{2,1,0:T(8,128)(2,1)}) custom-call(s32[8,128]{1,0:T(8,128)} %collective-permute-done.4.lists, s32[64]{0:T(128)} %positions.5, s32[4]{0:T(128)} %pad_add_fusion.at, bf16[8,32,1152]{2,1,0:T(8,128)(2,1)} %copy-done.7, ...), custom_call_target="tpu_custom_call" | custom-call | flops 2359 | bytes 4718 | tf_op jit(solution)/shard_map/pallas_call | solution.py:429
  99.1 2.2 %collective-permute-start.18 = (bf16[2,512,256]{2,1,0:T(8,128)(2,1)}, bf16[2,512,256]{2,1,0:T(8,128)(2,1)S(1)}, u32[]{:S(2)}, u32[]{:S(2)}) collective-permute-start(bf16[2,512,256]{2,1,0:T(8,128)(2,1)} %get-tuple-element.60), channel_id=1, source_target_pairs={{0,1},{1,2},{2,3},{3,0},{4,7},{5,4},{6,5},{7,6},{8,9},{9,10},{10,1... | collective-permute-start | bytes 1572872 | tf_op jit(solution)/shard_map/ppermute | solution.py:36
  101.4 1.6 %collective-permute-start.19 = (bf16[2,512,256]{2,1,0:T(8,128)(2,1)}, bf16[2,512,256]{2,1,0:T(8,128)(2,1)}, u32[]{:S(2)}, u32[]{:S(2)}) collective-permute-start(bf16[2,512,256]{2,1,0:T(8,128)(2,1)} %get-tuple-element.61), channel_id=1, source_target_pairs={{0,2},{1,3},{2,0},{3,1},{4,6},{5,7},{6,4},{7,5},{8,10},{9,11},{10,... | collective-permute-start | bytes 1572872 | tf_op jit(solution)/shard_map/ppermute | solution.py:36
  103.0 4.6 %collective-permute-done.22.b3 = bf16[2,512,256]{2,1,0:T(8,128)(2,1)S(1)} collective-permute-done((bf16[2,512,256]{2,1,0:T(8,128)(2,1)}, bf16[2,512,256]{2,1,0:T(8,128)(2,1)S(1)}, u32[]{:S(2)}, u32[]{:S(2)}) %collective-permute-start.22) | collective-permute-done | bytes 524320 | tf_op jit(solution)/shard_map/ppermute | solution.py:36
  108.7 2.5 %collective-permute-start.28 = (bf16[4,32,1152]{2,1,0:T(8,128)(2,1)}, bf16[4,32,1152]{2,1,0:T(8,128)(2,1)S(1)}, u32[]{:S(2)}, u32[]{:S(2)}) collective-permute-start(bf16[4,32,1152]{2,1,0:T(8,128)(2,1)} %get-tuple-element.72), channel_id=1, source_target_pairs={{0,64},{1,65},{2,66},{3,67},{4,20},{5,21},{6,22},{7,23},{8,72},{9,... | collective-permute-start | bytes 884744 | tf_op jit(solution)/shard_map/ppermute | solution.py:36
  111.2 10.6 %shard_map.149 = (bf16[512,2048]{1,0:T(8,128)(2,1)}, f32[8,128]{1,0:T(8,128)}) custom-call(s32[4]{0:T(128)} %pad_add_fusion.at, bf16[2,512,256]{2,1,0:T(8,128)(2,1)} %get-tuple-element.64.b0, bf16[2,512,256]{2,1,0:T(8,128)(2,1)} %copy-done.31, bf16[2,512,256]{2,1,0:T(8,128)(2,1)} %copy-done.30, bf16[2,512,256]{2,1,0:T(8,128)(2,1)} %copy-done.33, ...), custom_call_target="tpu_custom_call" | custom-call | flops 12884901888 | bytes 16777216 | tf_op jit(solution)/shard_map/pallas_call | solution.py:605
  123.8 6.3 %collective-permute-done.19.t3 = bf16[2,512,256]{2,1,0:T(8,128)(2,1)} collective-permute-done((bf16[2,512,256]{2,1,0:T(8,128)(2,1)}, bf16[2,512,256]{2,1,0:T(8,128)(2,1)}, u32[]{:S(2)}, u32[]{:S(2)}) %collective-permute-start.19) | collective-permute-done | bytes 524320 | tf_op jit(solution)/shard_map/ppermute | solution.py:36
  130.2 2.4 %shard_map.150 = (bf16[512,256]{1,0:T(8,128)(2,1)}, bf16[512,256]{1,0:T(8,128)(2,1)}) custom-call(s32[4]{0:T(128)S(1)} %copy-done.22, bf16[64,512]{1,0:T(8,128)(2,1)S(1)} %copy-done.19, bf16[4,32,2304]{2,1,0:T(8,128)(2,1)S(1)} %copy-done.13, f32[2,512,128]{2,1,0:T(8,128)S(1)} %pad_maximum_fusion.tables, bf16[2,512,256]{2,1,0:T(8,128)(2,1)S(1)} %get-tuple-element.58.t0, ...), custom_call_target="tpu_custom_call" | custom-call | bytes 4194 | tf_op jit(solution)/shard_map/pallas_call | solution.py:649
  (133 shorter events, 36.5 us)
Async XLA Ops:
  5.7 55.8 %collective-permute-start.12 = (bf16[2,2048,256]{2,1,0:T(8,128)(2,1)}, bf16[2,2048,256]{2,1,0:T(8,128)(2,1)}, u32[]{:S(2)}, u32[]{:S(2)}) collective-permute-start(bf16[2,2048,256]{2,1,0:T(8,128)(2,1)} %get-tuple-element.40._), channel_id=1, source_target_pairs={{0,1},{1,2},{2,3},{3,0},{4,7},{5,4},{6,5},{7,6},{8,9},{9,10},{10,1... | collective-permute-start | bytes 6291464 | tf_op jit(solution)/shard_map/ppermute | solution.py:36
  14.6 7.8 %collective-permute-start.3 = (bf16[4,32,1280]{2,1,0:T(8,128)(2,1)S(1)}, bf16[4,32,1280]{2,1,0:T(8,128)(2,1)S(1)}, u32[]{:S(2)}, u32[]{:S(2)}) collective-permute-start(bf16[4,32,1280]{2,1,0:T(8,128)(2,1)S(1)} %shard_map.139.m0), channel_id=1, source_target_pairs={{0,64},{1,65},{2,66},{3,67},{4,20},{5,21},{6,22},{7,23},{8,72},{9,... | collective-permute-start | bytes 983048 | tf_op jit(solution)/shard_map/ppermute | solution.py:36
  17.6 8.8 %collective-permute-start.2 = (bf16[4,32,1280]{2,1,0:T(8,128)(2,1)S(1)}, bf16[4,32,1280]{2,1,0:T(8,128)(2,1)S(1)}, u32[]{:S(2)}, u32[]{:S(2)}) collective-permute-start(bf16[4,32,1280]{2,1,0:T(8,128)(2,1)S(1)} %shard_map.139.m0), channel_id=1, source_target_pairs={{0,96},{1,97},{2,98},{3,99},{4,28},{5,29},{6,30},{7,31},{8,104},{9... | collective-permute-start | bytes 983048 | tf_op jit(solution)/shard_map/ppermute | solution.py:36
  18.3 8.0 %collective-permute-start.1 = (bf16[4,32,1280]{2,1,0:T(8,128)(2,1)S(1)}, bf16[4,32,1280]{2,1,0:T(8,128)(2,1)S(1)}, u32[]{:S(2)}, u32[]{:S(2)}) collective-permute-start(bf16[4,32,1280]{2,1,0:T(8,128)(2,1)S(1)} %shard_map.139.m0), channel_id=1, source_target_pairs={{0,32},{1,33},{2,34},{3,35},{4,12},{5,13},{6,14},{7,15},{8,40},{9,... | collective-permute-start | bytes 983048 | tf_op jit(solution)/shard_map/ppermute | solution.py:36
  26.5 35.0 %collective-permute-start.13 = (bf16[2048,256]{1,0:T(8,128)(2,1)}, bf16[2048,256]{1,0:T(8,128)(2,1)}, u32[]{:S(2)}, u32[]{:S(2)}) collective-permute-start(bf16[2048,256]{1,0:T(8,128)(2,1)} %get-tuple-element.51), channel_id=1, source_target_pairs={{0,2},{1,3},{2,0},{3,1},{4,6},{5,7},{6,4},{7,5},{8,10},{9,11},{10,... | collective-permute-start | bytes 3145736 | tf_op jit(solution)/shard_map/ppermute | solution.py:36
  35.4 10.6 %collective-permute-start.5 = (bf16[8,32,1152]{2,1,0:T(8,128)(2,1)}, bf16[8,32,1152]{2,1,0:T(8,128)(2,1)S(1)}, u32[]{:S(2)}, u32[]{:S(2)}) collective-permute-start(bf16[8,32,1152]{2,1,0:T(8,128)(2,1)} %get-tuple-element.44), channel_id=1, source_target_pairs={{0,8},{1,9},{2,10},{3,11},{4,36},{5,37},{6,38},{7,39},{8,16},{9,17... | collective-permute-start | bytes 1769480 | tf_op jit(solution)/shard_map/ppermute | solution.py:36
  36.4 15.3 %collective-permute-start.6 = (bf16[8,32,1152]{2,1,0:T(8,128)(2,1)}, bf16[8,32,1152]{2,1,0:T(8,128)(2,1)}, u32[]{:S(2)}, u32[]{:S(2)}) collective-permute-start(bf16[8,32,1152]{2,1,0:T(8,128)(2,1)} %get-tuple-element.45), channel_id=1, source_target_pairs={{0,24},{1,25},{2,26},{3,27},{4,100},{5,101},{6,102},{7,103},{8,0},... | collective-permute-start | bytes 1769480 | tf_op jit(solution)/shard_map/ppermute | solution.py:36
  38.2 15.0 %collective-permute-start.7 = (bf16[8,32,1152]{2,1,0:T(8,128)(2,1)}, bf16[8,32,1152]{2,1,0:T(8,128)(2,1)}, u32[]{:S(2)}, u32[]{:S(2)}) collective-permute-start(bf16[8,32,1152]{2,1,0:T(8,128)(2,1)} %get-tuple-element.46), channel_id=1, source_target_pairs={{0,16},{1,17},{2,18},{3,19},{4,68},{5,69},{6,70},{7,71},{8,24},{9,... | collective-permute-start | bytes 1769480 | tf_op jit(solution)/shard_map/ppermute | solution.py:36
  61.5 6.8 %collective-permute-start.14 = (bf16[2,2048,256]{2,1,0:T(8,128)(2,1)}, bf16[2,2048,256]{2,1,0:T(8,128)(2,1)S(1)}, u32[]{:S(2)}, u32[]{:S(2)}) collective-permute-start(bf16[2,2048,256]{2,1,0:T(8,128)(2,1)} %collective-permute-done.12.near), channel_id=1, source_target_pairs={{0,4},{1,5},{2,6},{3,7},{4,0},{5,1},{6,2},{7,3},{8,12},{9,13},{10,... | collective-permute-start | bytes 6291464 | tf_op jit(solution)/shard_map/ppermute | solution.py:36
  62.0 6.3 %collective-permute-start.15 = (bf16[2048,256]{1,0:T(8,128)(2,1)}, bf16[2048,256]{1,0:T(8,128)(2,1)S(1)}, u32[]{:S(2)}, u32[]{:S(2)}) collective-permute-start(bf16[2048,256]{1,0:T(8,128)(2,1)} %collective-permute-done.13.far), channel_id=1, source_target_pairs={{0,4},{1,5},{2,6},{3,7},{4,0},{5,1},{6,2},{7,3},{8,12},{9,13},{10,... | collective-permute-start | bytes 3145736 | tf_op jit(solution)/shard_map/ppermute | solution.py:36
  62.1 4.6 %collective-permute-start.11 = (bf16[64,512]{1,0:T(8,128)(2,1)S(1)}, bf16[64,512]{1,0:T(8,128)(2,1)S(1)}, u32[]{:S(2)}, u32[]{:S(2)}) collective-permute-start(bf16[64,512]{1,0:T(8,128)(2,1)S(1)} %get-tuple-element.49.t0), channel_id=1, source_target_pairs={{0,2},{1,3},{2,0},{3,1},{4,6},{5,7},{6,4},{7,5},{8,10},{9,11},{10,... | collective-permute-start | bytes 196616 | tf_op jit(solution)/shard_map/ppermute | solution.py:36
  72.0 20.1 %collective-permute-start.21 = (bf16[2,512,256]{2,1,0:T(8,128)(2,1)}, bf16[2,512,256]{2,1,0:T(8,128)(2,1)S(1)}, u32[]{:S(2)}, u32[]{:S(2)}) collective-permute-start(bf16[2,512,256]{2,1,0:T(8,128)(2,1)} %get-tuple-element.64.b0), channel_id=1, source_target_pairs={{0,3},{1,0},{2,1},{3,2},{4,5},{5,6},{6,7},{7,4},{8,11},{9,8},{10,9... | collective-permute-start | bytes 1572872 | tf_op jit(solution)/shard_map/ppermute | solution.py:36
  72.0 20.1 %collective-permute-start.20 = (bf16[2,512,256]{2,1,0:T(8,128)(2,1)}, bf16[2,512,256]{2,1,0:T(8,128)(2,1)S(1)}, u32[]{:S(2)}, u32[]{:S(2)}) collective-permute-start(bf16[2,512,256]{2,1,0:T(8,128)(2,1)} %get-tuple-element.64.b0), channel_id=1, source_target_pairs={{0,1},{1,2},{2,3},{3,0},{4,7},{5,4},{6,5},{7,6},{8,9},{9,10},{10,1... | collective-permute-start | bytes 1572872 | tf_op jit(solution)/shard_map/ppermute | solution.py:36
  74.8 17.3 %collective-permute-start.25 = (bf16[8,32,1152]{2,1,0:T(8,128)(2,1)S(1)}, bf16[8,32,1152]{2,1,0:T(8,128)(2,1)S(1)}, u32[]{:S(2)}, u32[]{:S(2)}) collective-permute-start(bf16[8,32,1152]{2,1,0:T(8,128)(2,1)S(1)} %shard_map.146._.p0), channel_id=1, source_target_pairs={{0,16},{1,17},{2,18},{3,19},{4,68},{5,69},{6,70},{7,71},{8,24},{9,... | collective-permute-start | bytes 1769480 | tf_op jit(solution)/shard_map/ppermute | solution.py:36
  77.3 14.8 %collective-permute-start.24 = (bf16[8,32,1152]{2,1,0:T(8,128)(2,1)S(1)}, bf16[8,32,1152]{2,1,0:T(8,128)(2,1)S(1)}, u32[]{:S(2)}, u32[]{:S(2)}) collective-permute-start(bf16[8,32,1152]{2,1,0:T(8,128)(2,1)S(1)} %shard_map.146._.p0), channel_id=1, source_target_pairs={{0,24},{1,25},{2,26},{3,27},{4,100},{5,101},{6,102},{7,103},{8,0},... | collective-permute-start | bytes 1769480 | tf_op jit(solution)/shard_map/ppermute | solution.py:36
  78.1 16.0 %collective-permute-start.23 = (bf16[8,32,1152]{2,1,0:T(8,128)(2,1)S(1)}, bf16[8,32,1152]{2,1,0:T(8,128)(2,1)}, u32[]{:S(2)}, u32[]{:S(2)}) collective-permute-start(bf16[8,32,1152]{2,1,0:T(8,128)(2,1)S(1)} %shard_map.146._.p0), channel_id=1, source_target_pairs={{0,8},{1,9},{2,10},{3,11},{4,36},{5,37},{6,38},{7,39},{8,16},{9,17... | collective-permute-start | bytes 1769480 | tf_op jit(solution)/shard_map/ppermute | solution.py:36
  92.1 15.5 %collective-permute-start.22 = (bf16[2,512,256]{2,1,0:T(8,128)(2,1)}, bf16[2,512,256]{2,1,0:T(8,128)(2,1)S(1)}, u32[]{:S(2)}, u32[]{:S(2)}) collective-permute-start(bf16[2,512,256]{2,1,0:T(8,128)(2,1)} %get-tuple-element.64.b0), channel_id=1, source_target_pairs={{0,2},{1,3},{2,0},{3,1},{4,6},{5,7},{6,4},{7,5},{8,10},{9,11},{10,... | collective-permute-start | bytes 1572872 | tf_op jit(solution)/shard_map/ppermute | solution.py:36
  97.6 11.1 %collective-permute-start.26 = (bf16[4,32,1152]{2,1,0:T(8,128)(2,1)}, bf16[4,32,1152]{2,1,0:T(8,128)(2,1)S(1)}, u32[]{:S(2)}, u32[]{:S(2)}) collective-permute-start(bf16[4,32,1152]{2,1,0:T(8,128)(2,1)} %get-tuple-element.70), channel_id=1, source_target_pairs={{0,32},{1,33},{2,34},{3,35},{4,12},{5,13},{6,14},{7,15},{8,40},{9,... | collective-permute-start | bytes 884744 | tf_op jit(solution)/shard_map/ppermute | solution.py:36
  98.7 25.1 %collective-permute-start.17 = (bf16[2,512,256]{2,1,0:T(8,128)(2,1)}, bf16[2,512,256]{2,1,0:T(8,128)(2,1)S(1)}, u32[]{:S(2)}, u32[]{:S(2)}) collective-permute-start(bf16[2,512,256]{2,1,0:T(8,128)(2,1)} %get-tuple-element.59), channel_id=1, source_target_pairs={{0,3},{1,0},{2,1},{3,2},{4,5},{5,6},{6,7},{7,4},{8,11},{9,8},{10,9... | collective-permute-start | bytes 1572872 | tf_op jit(solution)/shard_map/ppermute | solution.py:36
  99.1 24.7 %collective-permute-start.18 = (bf16[2,512,256]{2,1,0:T(8,128)(2,1)}, bf16[2,512,256]{2,1,0:T(8,128)(2,1)S(1)}, u32[]{:S(2)}, u32[]{:S(2)}) collective-permute-start(bf16[2,512,256]{2,1,0:T(8,128)(2,1)} %get-tuple-element.60), channel_id=1, source_target_pairs={{0,1},{1,2},{2,3},{3,0},{4,7},{5,4},{6,5},{7,6},{8,9},{9,10},{10,1... | collective-permute-start | bytes 1572872 | tf_op jit(solution)/shard_map/ppermute | solution.py:36
  101.4 28.8 %collective-permute-start.19 = (bf16[2,512,256]{2,1,0:T(8,128)(2,1)}, bf16[2,512,256]{2,1,0:T(8,128)(2,1)}, u32[]{:S(2)}, u32[]{:S(2)}) collective-permute-start(bf16[2,512,256]{2,1,0:T(8,128)(2,1)} %get-tuple-element.61), channel_id=1, source_target_pairs={{0,2},{1,3},{2,0},{3,1},{4,6},{5,7},{6,4},{7,5},{8,10},{9,11},{10,... | collective-permute-start | bytes 1572872 | tf_op jit(solution)/shard_map/ppermute | solution.py:36
  108.4 13.4 %collective-permute-start.27 = (bf16[4,32,1152]{2,1,0:T(8,128)(2,1)}, bf16[4,32,1152]{2,1,0:T(8,128)(2,1)S(1)}, u32[]{:S(2)}, u32[]{:S(2)}) collective-permute-start(bf16[4,32,1152]{2,1,0:T(8,128)(2,1)} %get-tuple-element.71), channel_id=1, source_target_pairs={{0,96},{1,97},{2,98},{3,99},{4,28},{5,29},{6,30},{7,31},{8,104},{9... | collective-permute-start | bytes 884744 | tf_op jit(solution)/shard_map/ppermute | solution.py:36
  108.7 13.2 %collective-permute-start.28 = (bf16[4,32,1152]{2,1,0:T(8,128)(2,1)}, bf16[4,32,1152]{2,1,0:T(8,128)(2,1)S(1)}, u32[]{:S(2)}, u32[]{:S(2)}) collective-permute-start(bf16[4,32,1152]{2,1,0:T(8,128)(2,1)} %get-tuple-element.72), channel_id=1, source_target_pairs={{0,64},{1,65},{2,66},{3,67},{4,20},{5,21},{6,22},{7,23},{8,72},{9,... | collective-permute-start | bytes 884744 | tf_op jit(solution)/shard_map/ppermute | solution.py:36
  122.6 9.9 %collective-permute-start.29 = (f32[2,32,1152]{2,1,0:T(8,128)S(1)}, f32[2,32,1152]{2,1,0:T(8,128)S(1)}, u32[]{:S(2)}, u32[]{:S(2)}) collective-permute-start(f32[2,32,1152]{2,1,0:T(8,128)S(1)} %shard_map.151), channel_id=1, source_target_pairs={{0,4},{1,5},{2,6},{3,7},{4,0},{5,1},{6,2},{7,3},{8,12},{9,13},{10,... | collective-permute-start | bytes 884744 | tf_op jit(solution)/shard_map/ppermute | solution.py:36
  (40 other events, 359.5 us)

commit v3 on v2

--- a/solution.py
+++ b/solution.py
@@ -406,18 +406,27 @@
 
 
 def collect_kernel(lists, positions, at, p0, p1, p2, p3, *rest):
-    o0, o1, o2, o3, total = rest[-5:]
+    o0, o1, o2, o3, total, held, sems = rest[-7:]
     line, cross, core = at[0], at[1], at[2]
     slots = o0.shape[0]
-    total[...] = jnp.zeros_like(total)
+    found = []
     for i, piece in enumerate((p0, p1, p2, p3)):
         for b in range(piece.shape[0]):
-            on_line, on_cross, local = placed(positions[listed(lists, i, b)], core)
+            on_line, on_cross, local = placed(positions[lists[2 * i + b // 4, b % 4]], core)
+            n = len(found)
+            found.append((on_cross == cross, on_line * slots + local))
 
             @pl.when(on_cross == cross)
             def _():
-                slot = on_line * slots + local
-                total[slot] = total[slot] + piece[b].astype(f32)
+                pltpu.make_async_copy(piece.at[b], held.at[n], sems.at[n]).start()
+
+    total[...] = jnp.zeros_like(total)
+    for n, (here, slot) in enumerate(found):
+
+        @pl.when(here)
+        def _():
+            pltpu.make_async_copy(p0.at[0], held.at[n], sems.at[n]).wait()
+            total[slot] = total[slot] + held[n].astype(f32)
 
     for shift, out in zip((0,) + SHIFTS, (o0, o1, o2, o3)):
         target = (line + shift + SIDE) % SIDE
@@ -425,13 +434,17 @@
 
 
 def collect(lists, positions, at, pieces, slots, after):
-    _, both, wide = pieces[0].shape
+    count, both, wide = pieces[0].shape
     return pl.pallas_call(
         collect_kernel,
         out_shape=[jax.ShapeDtypeStruct((slots, both, wide), bf16)] * 4,
-        in_specs=[SMEM] * 3 + [VMEM] * 4 + [ANY] * len(after),
+        in_specs=[SMEM] * 3 + [ANY] * (4 + len(after)),
         out_specs=[VMEM] * 4,
-        scratch_shapes=[pltpu.VMEM((4 * slots, both, wide), f32)],
+        scratch_shapes=[
+            pltpu.VMEM((4 * slots, both, wide), f32),
+            pltpu.VMEM((4 * count, both, wide), bf16),
+            pltpu.SemaphoreType.DMA((4 * count,)),
+        ],
         compiler_params=params(60),
         cost_estimate=cost(8 * pieces[0].size, 16 * pieces[0].size),
     )(lists, positions, at, *pieces, *after)
@@ -457,7 +470,8 @@
     )(tables, key_grad, value_grad)
 
 
-def send_kernel(at, keys, values, near, far, sems):
+def send_kernel(at, keys, values, near, far, done, sems):
+    done[...] = jnp.zeros_like(done)
     core, z = at[2], at[3]
     width = far.shape[0]
 
@@ -485,9 +499,10 @@
         out_shape=[
             jax.ShapeDtypeStruct((2, rows, kv), bf16),
             jax.ShapeDtypeStruct((rows, kv), bf16),
+            TOKEN,
         ],
         in_specs=[SMEM] + [ANY] * 2,
-        out_specs=[VMEM] * 2,
+        out_specs=[VMEM] * 3,
         scratch_shapes=[pltpu.SemaphoreType.DMA((3,))],
         compiler_params=params(60),
         cost_estimate=cost(0, 12 * rows * kv),
@@ -528,16 +543,20 @@
         i = order[step]
         start_weights(sources[i], own_rows, pl.ds(0, width), weights.at[i], sems.at[i])
 
-    for step in range(3):
+    for step in range(4):
         start(step)
     done[...] = jnp.zeros_like(done)
-    for step, i in enumerate(order):
-        if step + 3 < len(order):
-            start(step + 3)
-        pltpu.make_async_copy(far, weights.at[i], sems.at[i]).wait()
-        (o0, o1, o2, o3)[i % 4][i // 4] = jnp.dot(
-            hidden[...], weights[i], preferred_element_type=f32
-        ).astype(bf16)
+    for k, out in enumerate((o0, o1, o2, o3)):
+        for step in (2 * k + 4, 2 * k + 5):
+            if step < len(order):
+                start(step)
+        for i in (k, 4 + k):
+            pltpu.make_async_copy(far, weights.at[i], sems.at[i]).wait()
+        both = jnp.concatenate([weights[k], weights[4 + k]], axis=1)
+        total = jnp.dot(hidden[...], both, preferred_element_type=f32).astype(bf16)
+        kv = both.shape[1] // 2
+        out[0] = total[:, :kv]
+        out[1] = total[:, kv:]
 
 
 def forward(at, hidden, keys, values, pieces, after):
@@ -729,19 +748,18 @@
     at = jnp.stack([line, cross, core, z])
 
     half = wide // 2
-    sent_near, sent_far = to_send(at, key_weight_frozen, value_weight_frozen)
+    sent_near, sent_far, sent_done = to_send(at, key_weight_frozen, value_weight_frozen)
     mine_half, give_half = split_maps(
         block_adapter_index,
         at,
         adapter_down_maps.reshape(slots_here, both, width),
         adapter_up_maps.reshape(slots_here, both, kv_here),
-        sent_near,
+        sent_done,
     )
     maps_chip = pack([mine_half, to_other_core(give_half)])
     maps_line = [maps_chip] + [along_line(maps_chip, d) for d in SHIFTS]
     lists_here = riding_lists(maps_line)
     lists = to_other_core(lists_here)
-    sent_far, _ = lax.optimization_barrier((sent_far, lists_here))
     segments, _ = lax.optimization_barrier((segment_document_index, maps_chip))
     tables = rope_tables(segments)
     back = turn(tables, key_gradient, value_gradient)
@@ -749,6 +767,7 @@
     received = [along_cross(p, d) for p, d in zip(picked, SHIFTS)]
 
     near = along_z_apart(sent_near, 1)
+    sent_far, _ = lax.optimization_barrier((sent_far, picked[0]))
     far = along_z(sent_far, 2)
     mine_maps, give_maps = resolve(lists, adapter_position, at, maps_line, received)
     into, maps = lora(at, hidden, back, mine_maps, to_other_core(give_maps))
@@ -780,7 +799,7 @@
         at, backs, key_weight_frozen, value_weight_frozen, pieces, sums, maps, line_sums[:1]
     )
     grad_down, grad_up = gather_sums(at, arrived, slots_here, width, (backward_done,))
-    key_out, value_out = finish(at, sums, maps, tables, key_terms, backward_done)
+    key_out, value_out = finish(at, sums, maps, tables, key_terms, grad_up)
     return (
         key_out,
         value_out,

time: 134 us -> 128 us (0.955)
  Pallas kernels: 46.4 us -> 41.2 us
  starting transfers between devices: 38.7 us -> 36.2 us
  waiting for transfers between devices: 36.6 us -> 38.7 us
    pallas_call x1, Pallas kernels: 12.7 us -> 8.04 us  [forward(): pl.pallas_call(forward_kernel, out_shape=[out] * 4 + [TOKEN], in_specs=[S...]
    ppermute x30, starting transfers between devices: 38.7 us -> 36.2 us  [exchange(): return lax.ppermute(array, ('dp', 'tensor'), pairs)]
    ppermute x30, waiting for transfers between devices: 36.6 us -> 38.7 us  [exchange(): return lax.ppermute(array, ('dp', 'tensor'), pairs)]
    unnamed x68 -> x70, local copies, waits for them, and re-layouts: 7.53 us -> 7.05 us
  transfers between devices with their start and end apart: 30 -> 30, of which waited for: 11 -> 11; matrix products, arithmetic and copies ran while one was open for 2% -> 2% of each run, Pallas kernels for 29% -> 25%
where the time goes in v3:
time: 128 us
  Pallas kernels  41.2 us (32%)
  waiting for transfers between devices  38.7 us (30%)
  starting transfers between devices  36.2 us (28%)
  local copies, waits for them, and re-layouts  7.82 us (6%)
  other arithmetic  2.28 us (2%)
  between operations  1.8 us (1%)
    ppermute x30, waiting for transfers between devices, exchange(): return lax.ppermute(array, ('dp', 'tensor'), pairs)  38.7 us
    ppermute x30, starting transfers between devices, exchange(): return lax.ppermute(array, ('dp', 'tensor'), pairs)  36.2 us
    pallas_call x1, Pallas kernels, backward(): pl.pallas_call(backward_kernel, out_shape=[jax.ShapeDtypeStruct((rows, wi...  10.6 us
    pallas_call x1, Pallas kernels, forward(): pl.pallas_call(forward_kernel, out_shape=[out] * 4 + [TOKEN], in_specs=[S...  8.04 us
    unnamed x70, local copies, waits for them, and re-layouts  7.05 us
    pallas_call x1, Pallas kernels, to_send(): pl.pallas_call(send_kernel, out_shape=[jax.ShapeDtypeStruct((2, rows, kv)...  4.37 us
    pallas_call x1, Pallas kernels, collect(): pl.pallas_call(collect_kernel, out_shape=[jax.ShapeDtypeStruct((slots, bo...  3.53 us
    pallas_call x1, Pallas kernels, pick(): pl.pallas_call(pick_kernel, out_shape=[out] * 3, in_specs=[SMEM] * 3 + [A...  3.52 us
  transfers between devices with their start and end apart: 30, of which 11 were waited for; matrix products, arithmetic and copies ran while one was open for 2% of the time, Pallas kernels for 25%

profile of v3, /device:TPU:1, one launch (start us, length us, event | category | flops | bytes accessed | tf_op | source)
XLA Modules:
  0.0 128.0 jit_solution(6053565410280036984)
XLA Ops:
  1.3 4.4 %shard_map.137 = (bf16[2,2048,256]{2,1,0:T(8,128)(2,1)}, bf16[2048,256]{1,0:T(8,128)(2,1)}, f32[8,128]{1,0:T(8,128)}) custom-call(s32[4]{0:T(128)} %pad_add_fusion.at, bf16[8192,256]{1,0:T(8,128)(2,1)} %keys.5, bf16[8192,256]{1,0:T(8,128)(2,1)} %values.5), custom_call_target="tpu_custom_call" | custom-call | bytes 6291 | tf_op jit(solution)/shard_map/pallas_call | solution.py:497
  8.6 3.8 %collective-permute-start.12 = (bf16[2,2048,256]{2,1,0:T(8,128)(2,1)}, bf16[2,2048,256]{2,1,0:T(8,128)(2,1)}, u32[]{:S(2)}, u32[]{:S(2)}) collective-permute-start(bf16[2,2048,256]{2,1,0:T(8,128)(2,1)} %get-tuple-element.51), channel_id=1, source_target_pairs={{0,1},{1,2},{2,3},{3,0},{4,7},{5,4},{6,5},{7,6},{8,9},{9,10},{10,1... | collective-permute-start | bytes 6291464 | tf_op jit(solution)/shard_map/ppermute | solution.py:36
  13.0 3.0 %collective-permute-start.3 = (bf16[4,32,1280]{2,1,0:T(8,128)(2,1)S(1)}, bf16[4,32,1280]{2,1,0:T(8,128)(2,1)S(1)}, u32[]{:S(2)}, u32[]{:S(2)}) collective-permute-start(bf16[4,32,1280]{2,1,0:T(8,128)(2,1)S(1)} %shard_map.139.m0), channel_id=1, source_target_pairs={{0,64},{1,65},{2,66},{3,67},{4,20},{5,21},{6,22},{7,23},{8,72},{9,... | collective-permute-start | bytes 983048 | tf_op jit(solution)/shard_map/ppermute | solution.py:36
  20.5 4.3 %collective-permute-done.2.m2 = bf16[4,32,1280]{2,1,0:T(8,128)(2,1)S(1)} collective-permute-done((bf16[4,32,1280]{2,1,0:T(8,128)(2,1)S(1)}, bf16[4,32,1280]{2,1,0:T(8,128)(2,1)S(1)}, u32[]{:S(2)}, u32[]{:S(2)}) %collective-permute-start.2) | collective-permute-done | bytes 327712 | tf_op jit(solution)/shard_map/ppermute | solution.py:36
  26.7 3.5 %shard_map.142 = (bf16[8,32,1152]{2,1,0:T(8,128)(2,1)}, bf16[8,32,1152]{2,1,0:T(8,128)(2,1)}, bf16[8,32,1152]{2,1,0:T(8,128)(2,1)}) custom-call(s32[8,128]{1,0:T(8,128)} %collective-permute-done.4.lists, s32[64]{0:T(128)} %positions.5, s32[4]{0:T(128)} %pad_add_fusion.at, bf16[4,32,1280]{2,1,0:T(8,128)(2,1)} %copy-done.3, bf16[4,32,1280]{2,1,0:T(8,128)(2,1)} %copy-done.6, ...), custom_call_target="tpu_custom_call" | custom-call | bytes 1310 | tf_op jit(solution)/shard_map/pallas_call | solution.py:259
  32.0 2.1 %collective-permute-start.6 = (bf16[8,32,1152]{2,1,0:T(8,128)(2,1)}, bf16[8,32,1152]{2,1,0:T(8,128)(2,1)S(1)}, u32[]{:S(2)}, u32[]{:S(2)}) collective-permute-start(bf16[8,32,1152]{2,1,0:T(8,128)(2,1)} %get-tuple-element.46), channel_id=1, source_target_pairs={{0,24},{1,25},{2,26},{3,27},{4,100},{5,101},{6,102},{7,103},{8,0},... | collective-permute-start | bytes 1769480 | tf_op jit(solution)/shard_map/ppermute | solution.py:36
  35.2 12.4 %collective-permute-done.6.r2 = bf16[8,32,1152]{2,1,0:T(8,128)(2,1)S(1)} collective-permute-done((bf16[8,32,1152]{2,1,0:T(8,128)(2,1)}, bf16[8,32,1152]{2,1,0:T(8,128)(2,1)S(1)}, u32[]{:S(2)}, u32[]{:S(2)}) %collective-permute-start.6) | collective-permute-done | bytes 589856 | tf_op jit(solution)/shard_map/ppermute | solution.py:36
  47.6 3.7 %collective-permute-done.5.r1 = bf16[8,32,1152]{2,1,0:T(8,128)(2,1)} collective-permute-done((bf16[8,32,1152]{2,1,0:T(8,128)(2,1)}, bf16[8,32,1152]{2,1,0:T(8,128)(2,1)}, u32[]{:S(2)}, u32[]{:S(2)}) %collective-permute-start.5) | collective-permute-done | bytes 589856 | tf_op jit(solution)/shard_map/ppermute | solution.py:36
  51.3 2.8 %shard_map.143 = (bf16[4,32,1152]{2,1,0:T(8,128)(2,1)}, bf16[4,32,1152]{2,1,0:T(8,128)(2,1)}) custom-call(s32[8,128]{1,0:T(8,128)} %collective-permute-done.4.lists, s32[64]{0:T(128)} %positions.5, s32[4]{0:T(128)} %pad_add_fusion.at, bf16[4,32,1280]{2,1,0:T(8,128)(2,1)} %copy-done.3, bf16[4,32,1280]{2,1,0:T(8,128)(2,1)} %copy-done.6, ...), custom_call_target="tpu_custom_call" | custom-call | bytes 589 | tf_op jit(solution)/shard_map/pallas_call | solution.py:301
  54.1 2.8 %collective-permute-start.8 = (bf16[4,32,1152]{2,1,0:T(8,128)(2,1)}, bf16[4,32,1152]{2,1,0:T(8,128)(2,1)S(1)}, u32[]{:S(2)}, u32[]{:S(2)}) collective-permute-start(bf16[4,32,1152]{2,1,0:T(8,128)(2,1)} %get-tuple-element.49), channel_id=1, source_target_pairs={{0,4},{1,5},{2,6},{3,7},{4,0},{5,1},{6,2},{7,3},{8,12},{9,13},{10,... | collective-permute-start | bytes 884744 | tf_op jit(solution)/shard_map/ppermute | solution.py:36
  61.9 2.3 %collective-permute-start.10 = (bf16[64,512]{1,0:T(8,128)(2,1)S(1)}, bf16[64,512]{1,0:T(8,128)(2,1)S(1)}, u32[]{:S(2)}, u32[]{:S(2)}) collective-permute-start(bf16[64,512]{1,0:T(8,128)(2,1)S(1)} %get-tuple-element.50.t0), channel_id=1, source_target_pairs={{0,3},{1,0},{2,1},{3,2},{4,7},{5,4},{6,5},{7,6},{8,11},{9,8},{10,9... | collective-permute-start | bytes 196616 | tf_op jit(solution)/shard_map/ppermute | solution.py:36
  64.1 1.9 %collective-permute-done.11.t3 = bf16[64,512]{1,0:T(8,128)(2,1)S(1)} collective-permute-done((bf16[64,512]{1,0:T(8,128)(2,1)S(1)}, bf16[64,512]{1,0:T(8,128)(2,1)S(1)}, u32[]{:S(2)}, u32[]{:S(2)}) %collective-permute-start.11) | collective-permute-done | bytes 65568 | tf_op jit(solution)/shard_map/ppermute | solution.py:36
  66.0 2.4 %collective-permute-done.9.t1 = bf16[64,512]{1,0:T(8,128)(2,1)S(1)} collective-permute-done((bf16[64,512]{1,0:T(8,128)(2,1)S(1)}, bf16[64,512]{1,0:T(8,128)(2,1)S(1)}, u32[]{:S(2)}, u32[]{:S(2)}) %collective-permute-start.9) | collective-permute-done | bytes 65568 | tf_op jit(solution)/shard_map/ppermute | solution.py:36
  68.5 1.9 %shard_map.145 = (bf16[4,32,1152]{2,1,0:T(8,128)(2,1)S(1)}, bf16[4,32,1152]{2,1,0:T(8,128)(2,1)S(1)}, bf16[64,512]{1,0:T(8,128)(2,1)S(1)}, bf16[2,512,256]{2,1,0:T(8,128)(2,1)}) custom-call(s32[4]{0:T(128)S(1)} %copy-done.21, bf16[512,2048]{1,0:T(8,128)(2,1)S(1)} %copy-done, bf16[2,512,256]{2,1,0:T(8,128)(2,1)S(1)} %copy-done.2, ...), custom_call_target="tpu_custom_call" | custom-call | flops 67108 | bytes 4194 | tf_op jit(solution)/shard_map/pallas_call | solution.py:392
  70.4 2.1 %collective-permute-start.16 = (bf16[4,32,1152]{2,1,0:T(8,128)(2,1)S(1)}, bf16[4,32,1152]{2,1,0:T(8,128)(2,1)S(1)}, u32[]{:S(2)}, u32[]{:S(2)}) collective-permute-start(bf16[4,32,1152]{2,1,0:T(8,128)(2,1)S(1)} %get-tuple-element.58), channel_id=1, source_target_pairs={{0,4},{1,5},{2,6},{3,7},{4,0},{5,1},{6,2},{7,3},{8,12},{9,13},{10,... | collective-permute-start | bytes 884744 | tf_op jit(solution)/shard_map/ppermute | solution.py:36
  72.4 2.7 %collective-permute-start.23 = (bf16[2,512,256]{2,1,0:T(8,128)(2,1)}, bf16[2,512,256]{2,1,0:T(8,128)(2,1)S(1)}, u32[]{:S(2)}, u32[]{:S(2)}) collective-permute-start(bf16[2,512,256]{2,1,0:T(8,128)(2,1)} %get-tuple-element.70.b0), channel_id=1, source_target_pairs={{0,1},{1,2},{2,3},{3,0},{4,7},{5,4},{6,5},{7,6},{8,9},{9,10},{10,1... | collective-permute-start | bytes 1572872 | tf_op jit(solution)/shard_map/ppermute | solution.py:36
  75.3 2.6 %collective-permute-start.22 = (bf16[8,32,1152]{2,1,0:T(8,128)(2,1)S(1)}, bf16[8,32,1152]{2,1,0:T(8,128)(2,1)S(1)}, u32[]{:S(2)}, u32[]{:S(2)}) collective-permute-start(bf16[8,32,1152]{2,1,0:T(8,128)(2,1)S(1)} %shard_map.146._.p0), channel_id=1, source_target_pairs={{0,16},{1,17},{2,18},{3,19},{4,68},{5,69},{6,70},{7,71},{8,24},{9,... | collective-permute-start | bytes 1769480 | tf_op jit(solution)/shard_map/ppermute | solution.py:36
  79.3 8.0 %shard_map.147 = (bf16[2,512,256]{2,1,0:T(8,128)(2,1)S(1)}, bf16[2,512,256]{2,1,0:T(8,128)(2,1)}, bf16[2,512,256]{2,1,0:T(8,128)(2,1)}, bf16[2,512,256]{2,1,0:T(8,128)(2,1)}, f32[8,128]{1,0:T(8,128)S(1)}) custom-call(s32[4]{0:T(128)S(1)} %copy-done.21, bf16[512,2048]{1,0:T(8,128)(2,1)S(1)} %copy-done, bf16[8192,256]{1,0:T(8,128)(2,1)} %keys.5, ...), custom_call_target="tpu_custom_call" | custom-call | flops 8589934592 | bytes 16777216 | tf_op jit(solution)/shard_map/pallas_call | solution.py:566
  88.1 4.1 %collective-permute-done.21.p2 = bf16[8,32,1152]{2,1,0:T(8,128)(2,1)S(1)} collective-permute-done((bf16[8,32,1152]{2,1,0:T(8,128)(2,1)S(1)}, bf16[8,32,1152]{2,1,0:T(8,128)(2,1)S(1)}, u32[]{:S(2)}, u32[]{:S(2)}) %collective-permute-start.21) | collective-permute-done | bytes 589856 | tf_op jit(solution)/shard_map/ppermute | solution.py:36
  93.0 3.5 %shard_map.148 = (bf16[4,32,1152]{2,1,0:T(8,128)(2,1)}, bf16[4,32,1152]{2,1,0:T(8,128)(2,1)}, bf16[4,32,1152]{2,1,0:T(8,128)(2,1)}, bf16[4,32,1152]{2,1,0:T(8,128)(2,1)}) custom-call(s32[8,128]{1,0:T(8,128)} %collective-permute-done.4.lists, s32[64]{0:T(128)} %positions.5, s32[4]{0:T(128)} %pad_add_fusion.at, bf16[8,32,1152]{2,1,0:T(8,128)(2,1)} %copy-done.7, ...), custom_call_target="tpu_custom_call" | custom-call | flops 2359 | bytes 4718 | tf_op jit(solution)/shard_map/pallas_call | solution.py:438
  96.7 2.7 %collective-permute-start.18 = (bf16[2,512,256]{2,1,0:T(8,128)(2,1)}, bf16[2,512,256]{2,1,0:T(8,128)(2,1)S(1)}, u32[]{:S(2)}, u32[]{:S(2)}) collective-permute-start(bf16[2,512,256]{2,1,0:T(8,128)(2,1)} %get-tuple-element.62), channel_id=1, source_target_pairs={{0,1},{1,2},{2,3},{3,0},{4,7},{5,4},{6,5},{7,6},{8,9},{9,10},{10,1... | collective-permute-start | bytes 1572872 | tf_op jit(solution)/shard_map/ppermute | solution.py:36
  99.4 3.9 %collective-permute-done.28.b3 = bf16[2,512,256]{2,1,0:T(8,128)(2,1)S(1)} collective-permute-done((bf16[2,512,256]{2,1,0:T(8,128)(2,1)}, bf16[2,512,256]{2,1,0:T(8,128)(2,1)S(1)}, u32[]{:S(2)}, u32[]{:S(2)}) %collective-permute-start.28) | collective-permute-done | bytes 524320 | tf_op jit(solution)/shard_map/ppermute | solution.py:36
  106.0 10.6 %shard_map.149 = (bf16[512,2048]{1,0:T(8,128)(2,1)}, f32[8,128]{1,0:T(8,128)}) custom-call(s32[4]{0:T(128)} %pad_add_fusion.at, bf16[2,512,256]{2,1,0:T(8,128)(2,1)} %get-tuple-element.70.b0, bf16[2,512,256]{2,1,0:T(8,128)(2,1)} %copy-done.32, bf16[2,512,256]{2,1,0:T(8,128)(2,1)} %copy-done.31, bf16[2,512,256]{2,1,0:T(8,128)(2,1)} %copy-done.34, ...), custom_call_target="tpu_custom_call" | custom-call | flops 12884901888 | bytes 16777216 | tf_op jit(solution)/shard_map/pallas_call | solution.py:624
  123.3 2.1 %collective-permute-done.19.t3 = bf16[2,512,256]{2,1,0:T(8,128)(2,1)S(1)} collective-permute-done((bf16[2,512,256]{2,1,0:T(8,128)(2,1)}, bf16[2,512,256]{2,1,0:T(8,128)(2,1)S(1)}, u32[]{:S(2)}, u32[]{:S(2)}) %collective-permute-start.19) | collective-permute-done | bytes 524320 | tf_op jit(solution)/shard_map/ppermute | solution.py:36
  (135 shorter events, 32.7 us)
Async XLA Ops:
  7.1 5.4 %collective-permute-start = (bf16[2,32,1280]{2,1,0:T(8,128)(2,1)S(1)}, bf16[2,32,1280]{2,1,0:T(8,128)(2,1)S(1)}, u32[]{:S(2)}, u32[]{:S(2)}) collective-permute-start(bf16[2,32,1280]{2,1,0:T(8,128)(2,1)S(1)} %get-tuple-element.43), channel_id=1, source_target_pairs={{0,4},{1,5},{2,6},{3,7},{4,0},{5,1},{6,2},{7,3},{8,12},{9,13},{10,... | collective-permute-start | bytes 491528 | tf_op jit(solution)/shard_map/ppermute | solution.py:36
  8.6 52.2 %collective-permute-start.12 = (bf16[2,2048,256]{2,1,0:T(8,128)(2,1)}, bf16[2,2048,256]{2,1,0:T(8,128)(2,1)}, u32[]{:S(2)}, u32[]{:S(2)}) collective-permute-start(bf16[2,2048,256]{2,1,0:T(8,128)(2,1)} %get-tuple-element.51), channel_id=1, source_target_pairs={{0,1},{1,2},{2,3},{3,0},{4,7},{5,4},{6,5},{7,6},{8,9},{9,10},{10,1... | collective-permute-start | bytes 6291464 | tf_op jit(solution)/shard_map/ppermute | solution.py:36
  13.0 7.5 %collective-permute-start.3 = (bf16[4,32,1280]{2,1,0:T(8,128)(2,1)S(1)}, bf16[4,32,1280]{2,1,0:T(8,128)(2,1)S(1)}, u32[]{:S(2)}, u32[]{:S(2)}) collective-permute-start(bf16[4,32,1280]{2,1,0:T(8,128)(2,1)S(1)} %shard_map.139.m0), channel_id=1, source_target_pairs={{0,64},{1,65},{2,66},{3,67},{4,20},{5,21},{6,22},{7,23},{8,72},{9,... | collective-permute-start | bytes 983048 | tf_op jit(solution)/shard_map/ppermute | solution.py:36
  16.0 8.8 %collective-permute-start.2 = (bf16[4,32,1280]{2,1,0:T(8,128)(2,1)S(1)}, bf16[4,32,1280]{2,1,0:T(8,128)(2,1)S(1)}, u32[]{:S(2)}, u32[]{:S(2)}) collective-permute-start(bf16[4,32,1280]{2,1,0:T(8,128)(2,1)S(1)} %shard_map.139.m0), channel_id=1, source_target_pairs={{0,96},{1,97},{2,98},{3,99},{4,28},{5,29},{6,30},{7,31},{8,104},{9... | collective-permute-start | bytes 983048 | tf_op jit(solution)/shard_map/ppermute | solution.py:36
  16.8 8.0 %collective-permute-start.1 = (bf16[4,32,1280]{2,1,0:T(8,128)(2,1)S(1)}, bf16[4,32,1280]{2,1,0:T(8,128)(2,1)S(1)}, u32[]{:S(2)}, u32[]{:S(2)}) collective-permute-start(bf16[4,32,1280]{2,1,0:T(8,128)(2,1)S(1)} %shard_map.139.m0), channel_id=1, source_target_pairs={{0,32},{1,33},{2,34},{3,35},{4,12},{5,13},{6,14},{7,15},{8,40},{9,... | collective-permute-start | bytes 983048 | tf_op jit(solution)/shard_map/ppermute | solution.py:36
  30.2 30.6 %collective-permute-start.13 = (bf16[2048,256]{1,0:T(8,128)(2,1)}, bf16[2048,256]{1,0:T(8,128)(2,1)}, u32[]{:S(2)}, u32[]{:S(2)}) collective-permute-start(bf16[2048,256]{1,0:T(8,128)(2,1)} %get-tuple-element.53), channel_id=1, source_target_pairs={{0,2},{1,3},{2,0},{3,1},{4,6},{5,7},{6,4},{7,5},{8,10},{9,11},{10,... | collective-permute-start | bytes 3145736 | tf_op jit(solution)/shard_map/ppermute | solution.py:36
  32.0 15.6 %collective-permute-start.6 = (bf16[8,32,1152]{2,1,0:T(8,128)(2,1)}, bf16[8,32,1152]{2,1,0:T(8,128)(2,1)S(1)}, u32[]{:S(2)}, u32[]{:S(2)}) collective-permute-start(bf16[8,32,1152]{2,1,0:T(8,128)(2,1)} %get-tuple-element.46), channel_id=1, source_target_pairs={{0,24},{1,25},{2,26},{3,27},{4,100},{5,101},{6,102},{7,103},{8,0},... | collective-permute-start | bytes 1769480 | tf_op jit(solution)/shard_map/ppermute | solution.py:36
  34.1 13.5 %collective-permute-start.7 = (bf16[8,32,1152]{2,1,0:T(8,128)(2,1)}, bf16[8,32,1152]{2,1,0:T(8,128)(2,1)}, u32[]{:S(2)}, u32[]{:S(2)}) collective-permute-start(bf16[8,32,1152]{2,1,0:T(8,128)(2,1)} %get-tuple-element.47), channel_id=1, source_target_pairs={{0,16},{1,17},{2,18},{3,19},{4,68},{5,69},{6,70},{7,71},{8,24},{9,... | collective-permute-start | bytes 1769480 | tf_op jit(solution)/shard_map/ppermute | solution.py:36
  35.0 16.3 %collective-permute-start.5 = (bf16[8,32,1152]{2,1,0:T(8,128)(2,1)}, bf16[8,32,1152]{2,1,0:T(8,128)(2,1)}, u32[]{:S(2)}, u32[]{:S(2)}) collective-permute-start(bf16[8,32,1152]{2,1,0:T(8,128)(2,1)} %get-tuple-element.45), channel_id=1, source_target_pairs={{0,8},{1,9},{2,10},{3,11},{4,36},{5,37},{6,38},{7,39},{8,16},{9,17... | collective-permute-start | bytes 1769480 | tf_op jit(solution)/shard_map/ppermute | solution.py:36
  60.8 7.6 %collective-permute-start.14 = (bf16[2,2048,256]{2,1,0:T(8,128)(2,1)}, bf16[2,2048,256]{2,1,0:T(8,128)(2,1)S(1)}, u32[]{:S(2)}, u32[]{:S(2)}) collective-permute-start(bf16[2,2048,256]{2,1,0:T(8,128)(2,1)} %collective-permute-done.12.near), channel_id=1, source_target_pairs={{0,4},{1,5},{2,6},{3,7},{4,0},{5,1},{6,2},{7,3},{8,12},{9,13},{10,... | collective-permute-start | bytes 6291464 | tf_op jit(solution)/shard_map/ppermute | solution.py:36
  61.3 7.2 %collective-permute-start.15 = (bf16[2048,256]{1,0:T(8,128)(2,1)}, bf16[2048,256]{1,0:T(8,128)(2,1)S(1)}, u32[]{:S(2)}, u32[]{:S(2)}) collective-permute-start(bf16[2048,256]{1,0:T(8,128)(2,1)} %collective-permute-done.13.far), channel_id=1, source_target_pairs={{0,4},{1,5},{2,6},{3,7},{4,0},{5,1},{6,2},{7,3},{8,12},{9,13},{10,... | collective-permute-start | bytes 3145736 | tf_op jit(solution)/shard_map/ppermute | solution.py:36
  70.4 4.7 %collective-permute-start.16 = (bf16[4,32,1152]{2,1,0:T(8,128)(2,1)S(1)}, bf16[4,32,1152]{2,1,0:T(8,128)(2,1)S(1)}, u32[]{:S(2)}, u32[]{:S(2)}) collective-permute-start(bf16[4,32,1152]{2,1,0:T(8,128)(2,1)S(1)} %get-tuple-element.58), channel_id=1, source_target_pairs={{0,4},{1,5},{2,6},{3,7},{4,0},{5,1},{6,2},{7,3},{8,12},{9,13},{10,... | collective-permute-start | bytes 884744 | tf_op jit(solution)/shard_map/ppermute | solution.py:36
  72.4 15.6 %collective-permute-start.24 = (bf16[2,512,256]{2,1,0:T(8,128)(2,1)}, bf16[2,512,256]{2,1,0:T(8,128)(2,1)S(1)}, u32[]{:S(2)}, u32[]{:S(2)}) collective-permute-start(bf16[2,512,256]{2,1,0:T(8,128)(2,1)} %get-tuple-element.70.b0), channel_id=1, source_target_pairs={{0,3},{1,0},{2,1},{3,2},{4,5},{5,6},{6,7},{7,4},{8,11},{9,8},{10,9... | collective-permute-start | bytes 1572872 | tf_op jit(solution)/shard_map/ppermute | solution.py:36
  72.4 15.6 %collective-permute-start.23 = (bf16[2,512,256]{2,1,0:T(8,128)(2,1)}, bf16[2,512,256]{2,1,0:T(8,128)(2,1)S(1)}, u32[]{:S(2)}, u32[]{:S(2)}) collective-permute-start(bf16[2,512,256]{2,1,0:T(8,128)(2,1)} %get-tuple-element.70.b0), channel_id=1, source_target_pairs={{0,1},{1,2},{2,3},{3,0},{4,7},{5,4},{6,5},{7,6},{8,9},{9,10},{10,1... | collective-permute-start | bytes 1572872 | tf_op jit(solution)/shard_map/ppermute | solution.py:36
  75.3 12.8 %collective-permute-start.22 = (bf16[8,32,1152]{2,1,0:T(8,128)(2,1)S(1)}, bf16[8,32,1152]{2,1,0:T(8,128)(2,1)S(1)}, u32[]{:S(2)}, u32[]{:S(2)}) collective-permute-start(bf16[8,32,1152]{2,1,0:T(8,128)(2,1)S(1)} %shard_map.146._.p0), channel_id=1, source_target_pairs={{0,16},{1,17},{2,18},{3,19},{4,68},{5,69},{6,70},{7,71},{8,24},{9,... | collective-permute-start | bytes 1769480 | tf_op jit(solution)/shard_map/ppermute | solution.py:36
  77.9 14.3 %collective-permute-start.21 = (bf16[8,32,1152]{2,1,0:T(8,128)(2,1)S(1)}, bf16[8,32,1152]{2,1,0:T(8,128)(2,1)S(1)}, u32[]{:S(2)}, u32[]{:S(2)}) collective-permute-start(bf16[8,32,1152]{2,1,0:T(8,128)(2,1)S(1)} %shard_map.146._.p0), channel_id=1, source_target_pairs={{0,24},{1,25},{2,26},{3,27},{4,100},{5,101},{6,102},{7,103},{8,0},... | collective-permute-start | bytes 1769480 | tf_op jit(solution)/shard_map/ppermute | solution.py:36
  78.8 14.3 %collective-permute-start.20 = (bf16[8,32,1152]{2,1,0:T(8,128)(2,1)S(1)}, bf16[8,32,1152]{2,1,0:T(8,128)(2,1)}, u32[]{:S(2)}, u32[]{:S(2)}) collective-permute-start(bf16[8,32,1152]{2,1,0:T(8,128)(2,1)S(1)} %shard_map.146._.p0), channel_id=1, source_target_pairs={{0,8},{1,9},{2,10},{3,11},{4,36},{5,37},{6,38},{7,39},{8,16},{9,17... | collective-permute-start | bytes 1769480 | tf_op jit(solution)/shard_map/ppermute | solution.py:36
  88.0 15.3 %collective-permute-start.28 = (bf16[2,512,256]{2,1,0:T(8,128)(2,1)}, bf16[2,512,256]{2,1,0:T(8,128)(2,1)S(1)}, u32[]{:S(2)}, u32[]{:S(2)}) collective-permute-start(bf16[2,512,256]{2,1,0:T(8,128)(2,1)} %get-tuple-element.70.b0), channel_id=1, source_target_pairs={{0,2},{1,3},{2,0},{3,1},{4,6},{5,7},{6,4},{7,5},{8,10},{9,11},{10,... | collective-permute-start | bytes 1572872 | tf_op jit(solution)/shard_map/ppermute | solution.py:36
  96.6 8.9 %collective-permute-start.25 = (bf16[4,32,1152]{2,1,0:T(8,128)(2,1)}, bf16[4,32,1152]{2,1,0:T(8,128)(2,1)S(1)}, u32[]{:S(2)}, u32[]{:S(2)}) collective-permute-start(bf16[4,32,1152]{2,1,0:T(8,128)(2,1)} %get-tuple-element.67), channel_id=1, source_target_pairs={{0,32},{1,33},{2,34},{3,35},{4,12},{5,13},{6,14},{7,15},{8,40},{9,... | collective-permute-start | bytes 884744 | tf_op jit(solution)/shard_map/ppermute | solution.py:36
  96.7 25.4 %collective-permute-start.17 = (bf16[2,512,256]{2,1,0:T(8,128)(2,1)}, bf16[2,512,256]{2,1,0:T(8,128)(2,1)S(1)}, u32[]{:S(2)}, u32[]{:S(2)}) collective-permute-start(bf16[2,512,256]{2,1,0:T(8,128)(2,1)} %get-tuple-element.61), channel_id=1, source_target_pairs={{0,3},{1,0},{2,1},{3,2},{4,5},{5,6},{6,7},{7,4},{8,11},{9,8},{10,9... | collective-permute-start | bytes 1572872 | tf_op jit(solution)/shard_map/ppermute | solution.py:36
  96.7 26.5 %collective-permute-start.18 = (bf16[2,512,256]{2,1,0:T(8,128)(2,1)}, bf16[2,512,256]{2,1,0:T(8,128)(2,1)S(1)}, u32[]{:S(2)}, u32[]{:S(2)}) collective-permute-start(bf16[2,512,256]{2,1,0:T(8,128)(2,1)} %get-tuple-element.62), channel_id=1, source_target_pairs={{0,1},{1,2},{2,3},{3,0},{4,7},{5,4},{6,5},{7,6},{8,9},{9,10},{10,1... | collective-permute-start | bytes 1572872 | tf_op jit(solution)/shard_map/ppermute | solution.py:36
  99.4 25.9 %collective-permute-start.19 = (bf16[2,512,256]{2,1,0:T(8,128)(2,1)}, bf16[2,512,256]{2,1,0:T(8,128)(2,1)S(1)}, u32[]{:S(2)}, u32[]{:S(2)}) collective-permute-start(bf16[2,512,256]{2,1,0:T(8,128)(2,1)} %get-tuple-element.63), channel_id=1, source_target_pairs={{0,2},{1,3},{2,0},{3,1},{4,6},{5,7},{6,4},{7,5},{8,10},{9,11},{10,... | collective-permute-start | bytes 1572872 | tf_op jit(solution)/shard_map/ppermute | solution.py:36
  104.2 12.5 %collective-permute-start.26 = (bf16[4,32,1152]{2,1,0:T(8,128)(2,1)}, bf16[4,32,1152]{2,1,0:T(8,128)(2,1)S(1)}, u32[]{:S(2)}, u32[]{:S(2)}) collective-permute-start(bf16[4,32,1152]{2,1,0:T(8,128)(2,1)} %get-tuple-element.68), channel_id=1, source_target_pairs={{0,96},{1,97},{2,98},{3,99},{4,28},{5,29},{6,30},{7,31},{8,104},{9... | collective-permute-start | bytes 884744 | tf_op jit(solution)/shard_map/ppermute | solution.py:36
  105.5 11.2 %collective-permute-start.27 = (bf16[4,32,1152]{2,1,0:T(8,128)(2,1)}, bf16[4,32,1152]{2,1,0:T(8,128)(2,1)S(1)}, u32[]{:S(2)}, u32[]{:S(2)}) collective-permute-start(bf16[4,32,1152]{2,1,0:T(8,128)(2,1)} %get-tuple-element.69), channel_id=1, source_target_pairs={{0,64},{1,65},{2,66},{3,67},{4,20},{5,21},{6,22},{7,23},{8,72},{9,... | collective-permute-start | bytes 884744 | tf_op jit(solution)/shard_map/ppermute | solution.py:36
  (41 other events, 329.5 us)

commit v4 on v3

--- a/solution.py
+++ b/solution.py
@@ -767,7 +767,7 @@
     received = [along_cross(p, d) for p, d in zip(picked, SHIFTS)]
 
     near = along_z_apart(sent_near, 1)
-    sent_far, _ = lax.optimization_barrier((sent_far, picked[0]))
+    sent_far, _ = lax.optimization_barrier((sent_far, lists_here))
     far = along_z(sent_far, 2)
     mine_maps, give_maps = resolve(lists, adapter_position, at, maps_line, received)
     into, maps = lora(at, hidden, back, mine_maps, to_other_core(give_maps))

time: 128 us -> 127 us (level)
  waiting for transfers between devices: 38.7 us -> 34.2 us
  starting transfers between devices: 36.2 us -> 39.7 us
    ppermute x30, waiting for transfers between devices: 38.7 us -> 34.2 us  [exchange(): return lax.ppermute(array, ('dp', 'tensor'), pairs)]
    ppermute x30, starting transfers between devices: 36.2 us -> 39.7 us  [exchange(): return lax.ppermute(array, ('dp', 'tensor'), pairs)]
  transfers between devices with their start and end apart: 30 -> 30, of which waited for: 11 -> 13; matrix products, arithmetic and copies ran while one was open for 2% -> 2% of each run, Pallas kernels for 25% -> 26%
where the time goes in v4:
time: 127 us; the launch traced here: 126 us
  Pallas kernels  41.2 us (32%)
  starting transfers between devices  39.7 us (31%)
  waiting for transfers between devices  34.2 us (27%)
  local copies, waits for them, and re-layouts  7.24 us (6%)
  other arithmetic  2.27 us (2%)
  between operations  1.77 us (1%)
    ppermute x30, starting transfers between devices, exchange(): return lax.ppermute(array, ('dp', 'tensor'), pairs)  39.7 us
    ppermute x30, waiting for transfers between devices, exchange(): return lax.ppermute(array, ('dp', 'tensor'), pairs)  34.2 us
    pallas_call x1, Pallas kernels, backward(): pl.pallas_call(backward_kernel, out_shape=[jax.ShapeDtypeStruct((rows, wi...  10.6 us
    pallas_call x1, Pallas kernels, forward(): pl.pallas_call(forward_kernel, out_shape=[out] * 4 + [TOKEN], in_specs=[S...  8.04 us
    unnamed x70, local copies, waits for them, and re-layouts  6.46 us
    pallas_call x1, Pallas kernels, to_send(): pl.pallas_call(send_kernel, out_shape=[jax.ShapeDtypeStruct((2, rows, kv)...  4.37 us
    pallas_call x1, Pallas kernels, pick(): pl.pallas_call(pick_kernel, out_shape=[out] * 3, in_specs=[SMEM] * 3 + [A...  3.54 us
    pallas_call x1, Pallas kernels, collect(): pl.pallas_call(collect_kernel, out_shape=[jax.ShapeDtypeStruct((slots, bo...  3.48 us
  transfers between devices with their start and end apart: 30, of which 13 were waited for; matrix products, arithmetic and copies ran while one was open for 2% of the time, Pallas kernels for 26%

profile of v4, /device:TPU:1, one launch (start us, length us, event | category | flops | bytes accessed | tf_op | source)
XLA Modules:
  0.0 126.3 jit_solution(9605440349335557729)
XLA Ops:
  1.3 4.4 %shard_map.137 = (bf16[2,2048,256]{2,1,0:T(8,128)(2,1)}, bf16[2048,256]{1,0:T(8,128)(2,1)}, f32[8,128]{1,0:T(8,128)}) custom-call(s32[4]{0:T(128)} %pad_add_fusion.at, bf16[8192,256]{1,0:T(8,128)(2,1)} %keys.5, bf16[8192,256]{1,0:T(8,128)(2,1)} %values.5), custom_call_target="tpu_custom_call" | custom-call | bytes 6291 | tf_op jit(solution)/shard_map/pallas_call | solution.py:497
  8.6 3.8 %collective-permute-start.12 = (bf16[2,2048,256]{2,1,0:T(8,128)(2,1)}, bf16[2,2048,256]{2,1,0:T(8,128)(2,1)}, u32[]{:S(2)}, u32[]{:S(2)}) collective-permute-start(bf16[2,2048,256]{2,1,0:T(8,128)(2,1)} %get-tuple-element.51), channel_id=1, source_target_pairs={{0,1},{1,2},{2,3},{3,0},{4,7},{5,4},{6,5},{7,6},{8,9},{9,10},{10,1... | collective-permute-start | bytes 6291464 | tf_op jit(solution)/shard_map/ppermute | solution.py:36
  13.0 3.0 %collective-permute-start.3 = (bf16[4,32,1280]{2,1,0:T(8,128)(2,1)S(1)}, bf16[4,32,1280]{2,1,0:T(8,128)(2,1)S(1)}, u32[]{:S(2)}, u32[]{:S(2)}) collective-permute-start(bf16[4,32,1280]{2,1,0:T(8,128)(2,1)S(1)} %shard_map.139.m0), channel_id=1, source_target_pairs={{0,64},{1,65},{2,66},{3,67},{4,20},{5,21},{6,22},{7,23},{8,72},{9,... | collective-permute-start | bytes 983048 | tf_op jit(solution)/shard_map/ppermute | solution.py:36
  20.5 4.3 %collective-permute-done.2.m2 = bf16[4,32,1280]{2,1,0:T(8,128)(2,1)S(1)} collective-permute-done((bf16[4,32,1280]{2,1,0:T(8,128)(2,1)S(1)}, bf16[4,32,1280]{2,1,0:T(8,128)(2,1)S(1)}, u32[]{:S(2)}, u32[]{:S(2)}) %collective-permute-start.2) | collective-permute-done | bytes 327712 | tf_op jit(solution)/shard_map/ppermute | solution.py:36
  26.8 1.9 %collective-permute-start.4 = (s32[8,128]{1,0:T(8,128)S(1)}, s32[8,128]{1,0:T(8,128)}, u32[]{:S(2)}, u32[]{:S(2)}) collective-permute-start(s32[8,128]{1,0:T(8,128)S(1)} %shard_map.141), channel_id=1, source_target_pairs={{0,4},{1,5},{2,6},{3,7},{4,0},{5,1},{6,2},{7,3},{8,12},{9,13},{10,... | collective-permute-start | bytes 12296 | tf_op jit(solution)/shard_map/ppermute | solution.py:36
  29.7 3.5 %shard_map.142 = (bf16[8,32,1152]{2,1,0:T(8,128)(2,1)}, bf16[8,32,1152]{2,1,0:T(8,128)(2,1)}, bf16[8,32,1152]{2,1,0:T(8,128)(2,1)}) custom-call(s32[8,128]{1,0:T(8,128)} %collective-permute-done.4.lists, s32[64]{0:T(128)} %positions.5, s32[4]{0:T(128)} %pad_add_fusion.at, bf16[4,32,1280]{2,1,0:T(8,128)(2,1)} %copy-done.3, bf16[4,32,1280]{2,1,0:T(8,128)(2,1)} %copy-done.6, ...), custom_call_target="tpu_custom_call" | custom-call | bytes 1310 | tf_op jit(solution)/shard_map/pallas_call | solution.py:259
  34.1 1.9 %collective-permute-start.6 = (bf16[8,32,1152]{2,1,0:T(8,128)(2,1)}, bf16[8,32,1152]{2,1,0:T(8,128)(2,1)}, u32[]{:S(2)}, u32[]{:S(2)}) collective-permute-start(bf16[8,32,1152]{2,1,0:T(8,128)(2,1)} %get-tuple-element.46), channel_id=1, source_target_pairs={{0,24},{1,25},{2,26},{3,27},{4,100},{5,101},{6,102},{7,103},{8,0},... | collective-permute-start | bytes 1769480 | tf_op jit(solution)/shard_map/ppermute | solution.py:36
  37.3 6.6 %collective-permute-done.5.r1 = bf16[8,32,1152]{2,1,0:T(8,128)(2,1)S(1)} collective-permute-done((bf16[8,32,1152]{2,1,0:T(8,128)(2,1)}, bf16[8,32,1152]{2,1,0:T(8,128)(2,1)S(1)}, u32[]{:S(2)}, u32[]{:S(2)}) %collective-permute-start.5) | collective-permute-done | bytes 589856 | tf_op jit(solution)/shard_map/ppermute | solution.py:36
  43.9 5.6 %collective-permute-done.6.r2 = bf16[8,32,1152]{2,1,0:T(8,128)(2,1)} collective-permute-done((bf16[8,32,1152]{2,1,0:T(8,128)(2,1)}, bf16[8,32,1152]{2,1,0:T(8,128)(2,1)}, u32[]{:S(2)}, u32[]{:S(2)}) %collective-permute-start.6) | collective-permute-done | bytes 589856 | tf_op jit(solution)/shard_map/ppermute | solution.py:36
  50.8 2.8 %shard_map.143 = (bf16[4,32,1152]{2,1,0:T(8,128)(2,1)}, bf16[4,32,1152]{2,1,0:T(8,128)(2,1)}) custom-call(s32[8,128]{1,0:T(8,128)} %collective-permute-done.4.lists, s32[64]{0:T(128)} %positions.5, s32[4]{0:T(128)} %pad_add_fusion.at, bf16[4,32,1280]{2,1,0:T(8,128)(2,1)} %copy-done.3, bf16[4,32,1280]{2,1,0:T(8,128)(2,1)} %copy-done.6, ...), custom_call_target="tpu_custom_call" | custom-call | bytes 589 | tf_op jit(solution)/shard_map/pallas_call | solution.py:301
  59.3 1.8 %collective-permute-start.14 = (bf16[2,2048,256]{2,1,0:T(8,128)(2,1)}, bf16[2,2048,256]{2,1,0:T(8,128)(2,1)S(1)}, u32[]{:S(2)}, u32[]{:S(2)}) collective-permute-start(bf16[2,2048,256]{2,1,0:T(8,128)(2,1)} %collective-permute-done.12.near), channel_id=1, source_target_pairs={{0,4},{1,5},{2,6},{3,7},{4,0},{5,1},{6,2},{7,3},{8,12},{9,13},{10,... | collective-permute-start | bytes 6291464 | tf_op jit(solution)/shard_map/ppermute | solution.py:36
  62.7 3.0 %collective-permute-done.11.t3 = bf16[64,512]{1,0:T(8,128)(2,1)S(1)} collective-permute-done((bf16[64,512]{1,0:T(8,128)(2,1)S(1)}, bf16[64,512]{1,0:T(8,128)(2,1)S(1)}, u32[]{:S(2)}, u32[]{:S(2)}) %collective-permute-start.11) | collective-permute-done | bytes 65568 | tf_op jit(solution)/shard_map/ppermute | solution.py:36
  67.4 1.9 %shard_map.145 = (bf16[4,32,1152]{2,1,0:T(8,128)(2,1)S(1)}, bf16[4,32,1152]{2,1,0:T(8,128)(2,1)S(1)}, bf16[64,512]{1,0:T(8,128)(2,1)S(1)}, bf16[2,512,256]{2,1,0:T(8,128)(2,1)}) custom-call(s32[4]{0:T(128)S(1)} %copy-done.21, bf16[512,2048]{1,0:T(8,128)(2,1)S(1)} %copy-done, bf16[2,512,256]{2,1,0:T(8,128)(2,1)S(1)} %copy-done.2, ...), custom_call_target="tpu_custom_call" | custom-call | flops 67108 | bytes 4194 | tf_op jit(solution)/shard_map/pallas_call | solution.py:392
  70.9 2.7 %collective-permute-start.23 = (bf16[2,512,256]{2,1,0:T(8,128)(2,1)}, bf16[2,512,256]{2,1,0:T(8,128)(2,1)S(1)}, u32[]{:S(2)}, u32[]{:S(2)}) collective-permute-start(bf16[2,512,256]{2,1,0:T(8,128)(2,1)} %get-tuple-element.70.b0), channel_id=1, source_target_pairs={{0,1},{1,2},{2,3},{3,0},{4,7},{5,4},{6,5},{7,6},{8,9},{9,10},{10,1... | collective-permute-start | bytes 1572872 | tf_op jit(solution)/shard_map/ppermute | solution.py:36
  73.8 2.5 %collective-permute-start.22 = (bf16[8,32,1152]{2,1,0:T(8,128)(2,1)S(1)}, bf16[8,32,1152]{2,1,0:T(8,128)(2,1)S(1)}, u32[]{:S(2)}, u32[]{:S(2)}) collective-permute-start(bf16[8,32,1152]{2,1,0:T(8,128)(2,1)S(1)} %shard_map.146._.p0), channel_id=1, source_target_pairs={{0,16},{1,17},{2,18},{3,19},{4,68},{5,69},{6,70},{7,71},{8,24},{9,... | collective-permute-start | bytes 1769480 | tf_op jit(solution)/shard_map/ppermute | solution.py:36
  77.7 8.0 %shard_map.147 = (bf16[2,512,256]{2,1,0:T(8,128)(2,1)S(1)}, bf16[2,512,256]{2,1,0:T(8,128)(2,1)}, bf16[2,512,256]{2,1,0:T(8,128)(2,1)}, bf16[2,512,256]{2,1,0:T(8,128)(2,1)}, f32[8,128]{1,0:T(8,128)S(1)}) custom-call(s32[4]{0:T(128)S(1)} %copy-done.21, bf16[512,2048]{1,0:T(8,128)(2,1)S(1)} %copy-done, bf16[8192,256]{1,0:T(8,128)(2,1)} %keys.5, ...), custom_call_target="tpu_custom_call" | custom-call | flops 8589934592 | bytes 16777216 | tf_op jit(solution)/shard_map/pallas_call | solution.py:566
  86.4 4.2 %collective-permute-done.21.p2 = bf16[8,32,1152]{2,1,0:T(8,128)(2,1)S(1)} collective-permute-done((bf16[8,32,1152]{2,1,0:T(8,128)(2,1)S(1)}, bf16[8,32,1152]{2,1,0:T(8,128)(2,1)S(1)}, u32[]{:S(2)}, u32[]{:S(2)}) %collective-permute-start.21) | collective-permute-done | bytes 589856 | tf_op jit(solution)/shard_map/ppermute | solution.py:36
  91.5 3.5 %shard_map.148 = (bf16[4,32,1152]{2,1,0:T(8,128)(2,1)}, bf16[4,32,1152]{2,1,0:T(8,128)(2,1)}, bf16[4,32,1152]{2,1,0:T(8,128)(2,1)}, bf16[4,32,1152]{2,1,0:T(8,128)(2,1)}) custom-call(s32[8,128]{1,0:T(8,128)} %collective-permute-done.4.lists, s32[64]{0:T(128)} %positions.5, s32[4]{0:T(128)} %pad_add_fusion.at, bf16[8,32,1152]{2,1,0:T(8,128)(2,1)} %copy-done.7, ...), custom_call_target="tpu_custom_call" | custom-call | flops 2359 | bytes 4718 | tf_op jit(solution)/shard_map/pallas_call | solution.py:438
  96.3 2.7 %collective-permute-start.18 = (bf16[2,512,256]{2,1,0:T(8,128)(2,1)}, bf16[2,512,256]{2,1,0:T(8,128)(2,1)S(1)}, u32[]{:S(2)}, u32[]{:S(2)}) collective-permute-start(bf16[2,512,256]{2,1,0:T(8,128)(2,1)} %get-tuple-element.62), channel_id=1, source_target_pairs={{0,1},{1,2},{2,3},{3,0},{4,7},{5,4},{6,5},{7,6},{8,9},{9,10},{10,1... | collective-permute-start | bytes 1572872 | tf_op jit(solution)/shard_map/ppermute | solution.py:36
  99.0 2.2 %collective-permute-done.28.b3 = bf16[2,512,256]{2,1,0:T(8,128)(2,1)S(1)} collective-permute-done((bf16[2,512,256]{2,1,0:T(8,128)(2,1)}, bf16[2,512,256]{2,1,0:T(8,128)(2,1)S(1)}, u32[]{:S(2)}, u32[]{:S(2)}) %collective-permute-start.28) | collective-permute-done | bytes 524320 | tf_op jit(solution)/shard_map/ppermute | solution.py:36
  102.0 3.3 %collective-permute-start.26 = (bf16[4,32,1152]{2,1,0:T(8,128)(2,1)}, bf16[4,32,1152]{2,1,0:T(8,128)(2,1)S(1)}, u32[]{:S(2)}, u32[]{:S(2)}) collective-permute-start(bf16[4,32,1152]{2,1,0:T(8,128)(2,1)} %get-tuple-element.68), channel_id=1, source_target_pairs={{0,96},{1,97},{2,98},{3,99},{4,28},{5,29},{6,30},{7,31},{8,104},{9... | collective-permute-start | bytes 884744 | tf_op jit(solution)/shard_map/ppermute | solution.py:36
  106.0 10.6 %shard_map.149 = (bf16[512,2048]{1,0:T(8,128)(2,1)}, f32[8,128]{1,0:T(8,128)}) custom-call(s32[4]{0:T(128)} %pad_add_fusion.at, bf16[2,512,256]{2,1,0:T(8,128)(2,1)} %get-tuple-element.70.b0, bf16[2,512,256]{2,1,0:T(8,128)(2,1)} %copy-done.32, bf16[2,512,256]{2,1,0:T(8,128)(2,1)} %copy-done.31, bf16[2,512,256]{2,1,0:T(8,128)(2,1)} %copy-done.34, ...), custom_call_target="tpu_custom_call" | custom-call | flops 12884901888 | bytes 16777216 | tf_op jit(solution)/shard_map/pallas_call | solution.py:624
  117.5 1.9 %collective-permute-start.29 = (f32[2,32,1152]{2,1,0:T(8,128)S(1)}, f32[2,32,1152]{2,1,0:T(8,128)S(1)}, u32[]{:S(2)}, u32[]{:S(2)}) collective-permute-start(f32[2,32,1152]{2,1,0:T(8,128)S(1)} %shard_map.150), channel_id=1, source_target_pairs={{0,4},{1,5},{2,6},{3,7},{4,0},{5,1},{6,2},{7,3},{8,12},{9,13},{10,... | collective-permute-start | bytes 884744 | tf_op jit(solution)/shard_map/ppermute | solution.py:36
  124.5 1.8 %shard_map.152 = (bf16[512,256]{1,0:T(8,128)(2,1)}, bf16[512,256]{1,0:T(8,128)(2,1)}) custom-call(s32[4]{0:T(128)S(1)} %copy-done.22, bf16[64,512]{1,0:T(8,128)(2,1)S(1)} %copy-done.18, bf16[4,32,2304]{2,1,0:T(8,128)(2,1)S(1)} %copy-done.12, f32[2,512,128]{2,1,0:T(8,128)S(1)} %pad_maximum_fusion.tables, bf16[2,512,256]{2,1,0:T(8,128)(2,1)S(1)} %get-tuple-element.60.t0, ...), custom_call_target="tpu_custom_call" | custom-call | bytes 4194 | tf_op jit(solution)/shard_map/pallas_call | solution.py:668
  (135 shorter events, 36.7 us)
Async XLA Ops:
  7.1 5.4 %collective-permute-start = (bf16[2,32,1280]{2,1,0:T(8,128)(2,1)S(1)}, bf16[2,32,1280]{2,1,0:T(8,128)(2,1)S(1)}, u32[]{:S(2)}, u32[]{:S(2)}) collective-permute-start(bf16[2,32,1280]{2,1,0:T(8,128)(2,1)S(1)} %get-tuple-element.43), channel_id=1, source_target_pairs={{0,4},{1,5},{2,6},{3,7},{4,0},{5,1},{6,2},{7,3},{8,12},{9,13},{10,... | collective-permute-start | bytes 491528 | tf_op jit(solution)/shard_map/ppermute | solution.py:36
  8.6 50.7 %collective-permute-start.12 = (bf16[2,2048,256]{2,1,0:T(8,128)(2,1)}, bf16[2,2048,256]{2,1,0:T(8,128)(2,1)}, u32[]{:S(2)}, u32[]{:S(2)}) collective-permute-start(bf16[2,2048,256]{2,1,0:T(8,128)(2,1)} %get-tuple-element.51), channel_id=1, source_target_pairs={{0,1},{1,2},{2,3},{3,0},{4,7},{5,4},{6,5},{7,6},{8,9},{9,10},{10,1... | collective-permute-start | bytes 6291464 | tf_op jit(solution)/shard_map/ppermute | solution.py:36
  13.0 7.5 %collective-permute-start.3 = (bf16[4,32,1280]{2,1,0:T(8,128)(2,1)S(1)}, bf16[4,32,1280]{2,1,0:T(8,128)(2,1)S(1)}, u32[]{:S(2)}, u32[]{:S(2)}) collective-permute-start(bf16[4,32,1280]{2,1,0:T(8,128)(2,1)S(1)} %shard_map.139.m0), channel_id=1, source_target_pairs={{0,64},{1,65},{2,66},{3,67},{4,20},{5,21},{6,22},{7,23},{8,72},{9,... | collective-permute-start | bytes 983048 | tf_op jit(solution)/shard_map/ppermute | solution.py:36
  16.0 8.8 %collective-permute-start.2 = (bf16[4,32,1280]{2,1,0:T(8,128)(2,1)S(1)}, bf16[4,32,1280]{2,1,0:T(8,128)(2,1)S(1)}, u32[]{:S(2)}, u32[]{:S(2)}) collective-permute-start(bf16[4,32,1280]{2,1,0:T(8,128)(2,1)S(1)} %shard_map.139.m0), channel_id=1, source_target_pairs={{0,96},{1,97},{2,98},{3,99},{4,28},{5,29},{6,30},{7,31},{8,104},{9... | collective-permute-start | bytes 983048 | tf_op jit(solution)/shard_map/ppermute | solution.py:36
  16.8 8.0 %collective-permute-start.1 = (bf16[4,32,1280]{2,1,0:T(8,128)(2,1)S(1)}, bf16[4,32,1280]{2,1,0:T(8,128)(2,1)S(1)}, u32[]{:S(2)}, u32[]{:S(2)}) collective-permute-start(bf16[4,32,1280]{2,1,0:T(8,128)(2,1)S(1)} %shard_map.139.m0), channel_id=1, source_target_pairs={{0,32},{1,33},{2,34},{3,35},{4,12},{5,13},{6,14},{7,15},{8,40},{9,... | collective-permute-start | bytes 983048 | tf_op jit(solution)/shard_map/ppermute | solution.py:36
  24.9 34.4 %collective-permute-start.13 = (bf16[2048,256]{1,0:T(8,128)(2,1)}, bf16[2048,256]{1,0:T(8,128)(2,1)}, u32[]{:S(2)}, u32[]{:S(2)}) collective-permute-start(bf16[2048,256]{1,0:T(8,128)(2,1)} %get-tuple-element.53), channel_id=1, source_target_pairs={{0,2},{1,3},{2,0},{3,1},{4,6},{5,7},{6,4},{7,5},{8,10},{9,11},{10,... | collective-permute-start | bytes 3145736 | tf_op jit(solution)/shard_map/ppermute | solution.py:36
  33.3 10.6 %collective-permute-start.5 = (bf16[8,32,1152]{2,1,0:T(8,128)(2,1)}, bf16[8,32,1152]{2,1,0:T(8,128)(2,1)S(1)}, u32[]{:S(2)}, u32[]{:S(2)}) collective-permute-start(bf16[8,32,1152]{2,1,0:T(8,128)(2,1)} %get-tuple-element.45), channel_id=1, source_target_pairs={{0,8},{1,9},{2,10},{3,11},{4,36},{5,37},{6,38},{7,39},{8,16},{9,17... | collective-permute-start | bytes 1769480 | tf_op jit(solution)/shard_map/ppermute | solution.py:36
  34.1 15.4 %collective-permute-start.6 = (bf16[8,32,1152]{2,1,0:T(8,128)(2,1)}, bf16[8,32,1152]{2,1,0:T(8,128)(2,1)}, u32[]{:S(2)}, u32[]{:S(2)}) collective-permute-start(bf16[8,32,1152]{2,1,0:T(8,128)(2,1)} %get-tuple-element.46), channel_id=1, source_target_pairs={{0,24},{1,25},{2,26},{3,27},{4,100},{5,101},{6,102},{7,103},{8,0},... | collective-permute-start | bytes 1769480 | tf_op jit(solution)/shard_map/ppermute | solution.py:36
  36.0 14.8 %collective-permute-start.7 = (bf16[8,32,1152]{2,1,0:T(8,128)(2,1)}, bf16[8,32,1152]{2,1,0:T(8,128)(2,1)}, u32[]{:S(2)}, u32[]{:S(2)}) collective-permute-start(bf16[8,32,1152]{2,1,0:T(8,128)(2,1)} %get-tuple-element.47), channel_id=1, source_target_pairs={{0,16},{1,17},{2,18},{3,19},{4,68},{5,69},{6,70},{7,71},{8,24},{9,... | collective-permute-start | bytes 1769480 | tf_op jit(solution)/shard_map/ppermute | solution.py:36
  59.3 8.1 %collective-permute-start.14 = (bf16[2,2048,256]{2,1,0:T(8,128)(2,1)}, bf16[2,2048,256]{2,1,0:T(8,128)(2,1)S(1)}, u32[]{:S(2)}, u32[]{:S(2)}) collective-permute-start(bf16[2,2048,256]{2,1,0:T(8,128)(2,1)} %collective-permute-done.12.near), channel_id=1, source_target_pairs={{0,4},{1,5},{2,6},{3,7},{4,0},{5,1},{6,2},{7,3},{8,12},{9,13},{10,... | collective-permute-start | bytes 6291464 | tf_op jit(solution)/shard_map/ppermute | solution.py:36
  61.1 6.3 %collective-permute-start.15 = (bf16[2048,256]{1,0:T(8,128)(2,1)}, bf16[2048,256]{1,0:T(8,128)(2,1)S(1)}, u32[]{:S(2)}, u32[]{:S(2)}) collective-permute-start(bf16[2048,256]{1,0:T(8,128)(2,1)} %collective-permute-done.13.far), channel_id=1, source_target_pairs={{0,4},{1,5},{2,6},{3,7},{4,0},{5,1},{6,2},{7,3},{8,12},{9,13},{10,... | collective-permute-start | bytes 3145736 | tf_op jit(solution)/shard_map/ppermute | solution.py:36
  61.2 4.9 %collective-permute-start.10 = (bf16[64,512]{1,0:T(8,128)(2,1)S(1)}, bf16[64,512]{1,0:T(8,128)(2,1)S(1)}, u32[]{:S(2)}, u32[]{:S(2)}) collective-permute-start(bf16[64,512]{1,0:T(8,128)(2,1)S(1)} %get-tuple-element.50.t0), channel_id=1, source_target_pairs={{0,3},{1,0},{2,1},{3,2},{4,7},{5,4},{6,5},{7,6},{8,11},{9,8},{10,9... | collective-permute-start | bytes 196616 | tf_op jit(solution)/shard_map/ppermute | solution.py:36
  70.9 15.5 %collective-permute-start.24 = (bf16[2,512,256]{2,1,0:T(8,128)(2,1)}, bf16[2,512,256]{2,1,0:T(8,128)(2,1)S(1)}, u32[]{:S(2)}, u32[]{:S(2)}) collective-permute-start(bf16[2,512,256]{2,1,0:T(8,128)(2,1)} %get-tuple-element.70.b0), channel_id=1, source_target_pairs={{0,3},{1,0},{2,1},{3,2},{4,5},{5,6},{6,7},{7,4},{8,11},{9,8},{10,9... | collective-permute-start | bytes 1572872 | tf_op jit(solution)/shard_map/ppermute | solution.py:36
  70.9 15.5 %collective-permute-start.23 = (bf16[2,512,256]{2,1,0:T(8,128)(2,1)}, bf16[2,512,256]{2,1,0:T(8,128)(2,1)S(1)}, u32[]{:S(2)}, u32[]{:S(2)}) collective-permute-start(bf16[2,512,256]{2,1,0:T(8,128)(2,1)} %get-tuple-element.70.b0), channel_id=1, source_target_pairs={{0,1},{1,2},{2,3},{3,0},{4,7},{5,4},{6,5},{7,6},{8,9},{9,10},{10,1... | collective-permute-start | bytes 1572872 | tf_op jit(solution)/shard_map/ppermute | solution.py:36
  73.8 12.7 %collective-permute-start.22 = (bf16[8,32,1152]{2,1,0:T(8,128)(2,1)S(1)}, bf16[8,32,1152]{2,1,0:T(8,128)(2,1)S(1)}, u32[]{:S(2)}, u32[]{:S(2)}) collective-permute-start(bf16[8,32,1152]{2,1,0:T(8,128)(2,1)S(1)} %shard_map.146._.p0), channel_id=1, source_target_pairs={{0,16},{1,17},{2,18},{3,19},{4,68},{5,69},{6,70},{7,71},{8,24},{9,... | collective-permute-start | bytes 1769480 | tf_op jit(solution)/shard_map/ppermute | solution.py:36
  76.3 14.3 %collective-permute-start.21 = (bf16[8,32,1152]{2,1,0:T(8,128)(2,1)S(1)}, bf16[8,32,1152]{2,1,0:T(8,128)(2,1)S(1)}, u32[]{:S(2)}, u32[]{:S(2)}) collective-permute-start(bf16[8,32,1152]{2,1,0:T(8,128)(2,1)S(1)} %shard_map.146._.p0), channel_id=1, source_target_pairs={{0,24},{1,25},{2,26},{3,27},{4,100},{5,101},{6,102},{7,103},{8,0},... | collective-permute-start | bytes 1769480 | tf_op jit(solution)/shard_map/ppermute | solution.py:36
  77.1 14.4 %collective-permute-start.20 = (bf16[8,32,1152]{2,1,0:T(8,128)(2,1)S(1)}, bf16[8,32,1152]{2,1,0:T(8,128)(2,1)}, u32[]{:S(2)}, u32[]{:S(2)}) collective-permute-start(bf16[8,32,1152]{2,1,0:T(8,128)(2,1)S(1)} %shard_map.146._.p0), channel_id=1, source_target_pairs={{0,8},{1,9},{2,10},{3,11},{4,36},{5,37},{6,38},{7,39},{8,16},{9,17... | collective-permute-start | bytes 1769480 | tf_op jit(solution)/shard_map/ppermute | solution.py:36
  86.4 14.8 %collective-permute-start.28 = (bf16[2,512,256]{2,1,0:T(8,128)(2,1)}, bf16[2,512,256]{2,1,0:T(8,128)(2,1)S(1)}, u32[]{:S(2)}, u32[]{:S(2)}) collective-permute-start(bf16[2,512,256]{2,1,0:T(8,128)(2,1)} %get-tuple-element.70.b0), channel_id=1, source_target_pairs={{0,2},{1,3},{2,0},{3,1},{4,6},{5,7},{6,4},{7,5},{8,10},{9,11},{10,... | collective-permute-start | bytes 1572872 | tf_op jit(solution)/shard_map/ppermute | solution.py:36
  95.0 10.4 %collective-permute-start.25 = (bf16[4,32,1152]{2,1,0:T(8,128)(2,1)}, bf16[4,32,1152]{2,1,0:T(8,128)(2,1)S(1)}, u32[]{:S(2)}, u32[]{:S(2)}) collective-permute-start(bf16[4,32,1152]{2,1,0:T(8,128)(2,1)} %get-tuple-element.67), channel_id=1, source_target_pairs={{0,32},{1,33},{2,34},{3,35},{4,12},{5,13},{6,14},{7,15},{8,40},{9,... | collective-permute-start | bytes 884744 | tf_op jit(solution)/shard_map/ppermute | solution.py:36
  96.3 25.8 %collective-permute-start.17 = (bf16[2,512,256]{2,1,0:T(8,128)(2,1)}, bf16[2,512,256]{2,1,0:T(8,128)(2,1)S(1)}, u32[]{:S(2)}, u32[]{:S(2)}) collective-permute-start(bf16[2,512,256]{2,1,0:T(8,128)(2,1)} %get-tuple-element.61), channel_id=1, source_target_pairs={{0,3},{1,0},{2,1},{3,2},{4,5},{5,6},{6,7},{7,4},{8,11},{9,8},{10,9... | collective-permute-start | bytes 1572872 | tf_op jit(solution)/shard_map/ppermute | solution.py:36
  96.3 25.8 %collective-permute-start.18 = (bf16[2,512,256]{2,1,0:T(8,128)(2,1)}, bf16[2,512,256]{2,1,0:T(8,128)(2,1)S(1)}, u32[]{:S(2)}, u32[]{:S(2)}) collective-permute-start(bf16[2,512,256]{2,1,0:T(8,128)(2,1)} %get-tuple-element.62), channel_id=1, source_target_pairs={{0,1},{1,2},{2,3},{3,0},{4,7},{5,4},{6,5},{7,6},{8,9},{9,10},{10,1... | collective-permute-start | bytes 1572872 | tf_op jit(solution)/shard_map/ppermute | solution.py:36
  99.0 24.7 %collective-permute-start.19 = (bf16[2,512,256]{2,1,0:T(8,128)(2,1)}, bf16[2,512,256]{2,1,0:T(8,128)(2,1)S(1)}, u32[]{:S(2)}, u32[]{:S(2)}) collective-permute-start(bf16[2,512,256]{2,1,0:T(8,128)(2,1)} %get-tuple-element.63), channel_id=1, source_target_pairs={{0,2},{1,3},{2,0},{3,1},{4,6},{5,7},{6,4},{7,5},{8,10},{9,11},{10,... | collective-permute-start | bytes 1572872 | tf_op jit(solution)/shard_map/ppermute | solution.py:36
  102.0 14.6 %collective-permute-start.26 = (bf16[4,32,1152]{2,1,0:T(8,128)(2,1)}, bf16[4,32,1152]{2,1,0:T(8,128)(2,1)S(1)}, u32[]{:S(2)}, u32[]{:S(2)}) collective-permute-start(bf16[4,32,1152]{2,1,0:T(8,128)(2,1)} %get-tuple-element.68), channel_id=1, source_target_pairs={{0,96},{1,97},{2,98},{3,99},{4,28},{5,29},{6,30},{7,31},{8,104},{9... | collective-permute-start | bytes 884744 | tf_op jit(solution)/shard_map/ppermute | solution.py:36
  105.3 11.3 %collective-permute-start.27 = (bf16[4,32,1152]{2,1,0:T(8,128)(2,1)}, bf16[4,32,1152]{2,1,0:T(8,128)(2,1)S(1)}, u32[]{:S(2)}, u32[]{:S(2)}) collective-permute-start(bf16[4,32,1152]{2,1,0:T(8,128)(2,1)} %get-tuple-element.69), channel_id=1, source_target_pairs={{0,64},{1,65},{2,66},{3,67},{4,20},{5,21},{6,22},{7,23},{8,72},{9,... | collective-permute-start | bytes 884744 | tf_op jit(solution)/shard_map/ppermute | solution.py:36
  (41 other events, 332.0 us)

commit v5 on v4

--- a/solution.py
+++ b/solution.py
@@ -139,14 +139,14 @@
     )(*pieces, *after)
 
 
-def halves_kernel(index, at, down, up, _, mine, give, riding, sems):
+def halves_kernel(index, positions, at, down, up, _, mine, give, riding, sems):
     core = at[2]
     slots, both, width = down.shape
     wide = mine.shape[2] - HEAD
     lane = lax.broadcasted_iota(jnp.int32, riding.shape, 2)
     value = jnp.zeros(riding.shape, f32)
     for b in range(index.shape[0]):
-        value = jnp.where(lane == b, index[b].astype(f32), value)
+        value = jnp.where(lane == b, positions[index[b]].astype(f32), value)
     riding[...] = value.astype(bf16)
     ends = [
         pltpu.make_async_copy(riding, out.at[:, :, pl.ds(wide, HEAD)], sems.at[i])
@@ -180,19 +180,19 @@
         copy.wait()
 
 
-def split_maps(index, at, down, up, after):
+def split_maps(index, positions, at, down, up, after):
     slots, both, width = down.shape
     wide = (width + up.shape[2]) // 2
     out = jax.ShapeDtypeStruct((slots, both, wide + HEAD), bf16)
     return pl.pallas_call(
         halves_kernel,
         out_shape=[out] * 2,
-        in_specs=[SMEM] * 2 + [ANY] * 3,
+        in_specs=[SMEM] * 3 + [ANY] * 3,
         out_specs=[VMEM] * 2,
         scratch_shapes=[pltpu.VMEM((slots, both, HEAD), bf16), pltpu.SemaphoreType.DMA((5,))],
         compiler_params=params(16),
         cost_estimate=cost(0, 4 * down.size),
-    )(index, at, down, up, after)
+    )(index, positions, at, down, up, after)
 
 
 def lists_kernel(m0, m1, m2, m3, out, rows, sems):
@@ -228,49 +228,61 @@
     return lists[2 * piece + b // 4, b % 4]
 
 
-def pick_kernel(lists, positions, at, m0, m1, m2, m3, *rest):
-    o1, o2, o3, sems = rest[-4:]
+def pick_kernel(lists, at, m0, m1, m2, m3, *rest):
+    o1, o2, o3, held, sems = rest[-5:]
     line, cross, core = at[0], at[1], at[2]
     count, _, wide = o1.shape
     found = []
     for i, (row, out) in enumerate(((2, o1), (1, o2), (3, o3))):
         for b in range(count):
-            on_line, on_cross, local = placed(positions[listed(lists, row, b)], core)
+            n = len(found)
+            on_line, on_cross, local = placed(listed(lists, row, b), core)
             piece = jnp.where(on_cross == cross, piece_from(line, on_line), SIDE)
-            found.append((piece, out.at[b], sems.at[i * count + b]))
+            found.append((piece < SIDE, out.at[b]))
             for k, source in enumerate((m0, m1, m2, m3)):
 
                 @pl.when(piece == k)
                 def _():
                     pltpu.make_async_copy(
-                        source.at[local, :, pl.ds(0, wide)], out.at[b], sems.at[i * count + b]
+                        source.at[local, :, pl.ds(0, wide)], held.at[n], sems.at[0, n]
                     ).start()
 
-    for piece, target, sem in found:
-
-        @pl.when(piece < SIDE)
+    for n, (here, target) in enumerate(found):
+
+        @pl.when(here)
         def _():
-            pltpu.make_async_copy(m0.at[0, :, pl.ds(0, wide)], target, sem).wait()
-
-
-def pick(lists, positions, at, pieces, wide, blocks, after):
+            pltpu.make_async_copy(m0.at[0, :, pl.ds(0, wide)], held.at[n], sems.at[0, n]).wait()
+            pltpu.make_async_copy(held.at[n], target, sems.at[1, n]).start()
+
+    for n, (here, target) in enumerate(found):
+
+        @pl.when(here)
+        def _():
+            pltpu.make_async_copy(held.at[n], target, sems.at[1, n]).wait()
+
+
+def pick(lists, at, pieces, wide, blocks, after):
     count = 2 * blocks
-    out = jax.ShapeDtypeStruct((count, pieces[0].shape[1], wide), bf16)
+    both = pieces[0].shape[1]
+    out = jax.ShapeDtypeStruct((count, both, wide), bf16)
     return pl.pallas_call(
         pick_kernel,
         out_shape=[out] * 3,
-        in_specs=[SMEM] * 3 + [ANY] * (4 + len(after)),
-        out_specs=[VMEM] * 3,
-        scratch_shapes=[pltpu.SemaphoreType.DMA((3 * count,))],
-        compiler_params=params(60),
+        in_specs=[SMEM] * 2 + [ANY] * (4 + len(after)),
+        out_specs=[ANY] * 3,
+        scratch_shapes=[
+            pltpu.VMEM((3 * count, both, wide), bf16),
+            pltpu.SemaphoreType.DMA((2, 3 * count)),
+        ],
+        compiler_params=params(63),
         cost_estimate=cost(0, 8 * pieces[0].size),
-    )(lists, positions, at, *pieces, *after)
-
-
-def start_block(lists, positions, at, line_pieces, cross_pieces, b, target, sem):
+    )(lists, at, *pieces, *after)
+
+
+def start_block(lists, at, line_pieces, cross_pieces, b, target, sem):
     line, cross, core = at[0], at[1], at[2]
     wide = cross_pieces[0].shape[2]
-    on_line, on_cross, local = placed(positions[listed(lists, 0, b)], core)
+    on_line, on_cross, local = placed(listed(lists, 0, b), core)
     piece = piece_from(line, on_line)
     sender = piece_from(cross, on_cross)
     for k, source in enumerate(line_pieces):
@@ -286,27 +298,27 @@
             pltpu.make_async_copy(source.at[b], target, sem).start()
 
 
-def resolve_kernel(lists, positions, at, m0, m1, m2, m3, r1, r2, r3, mine, give, sems):
+def resolve_kernel(lists, at, m0, m1, m2, m3, r1, r2, r3, mine, give, sems):
     blocks = mine.shape[0]
     targets = [give.at[b] for b in range(blocks)] + [mine.at[b] for b in range(blocks)]
     for b, target in enumerate(targets):
-        start_block(lists, positions, at, (m0, m1, m2, m3), (r1, r2, r3), b, target, sems.at[b])
+        start_block(lists, at, (m0, m1, m2, m3), (r1, r2, r3), b, target, sems.at[b])
     for b, target in enumerate(targets):
         pltpu.make_async_copy(r1.at[0], target, sems.at[b]).wait()
 
 
-def resolve(lists, positions, at, pieces, received):
+def resolve(lists, at, pieces, received):
     count, both, wide = received[0].shape
     out = jax.ShapeDtypeStruct((count // 2, both, wide), bf16)
     return pl.pallas_call(
         resolve_kernel,
         out_shape=[out] * 2,
-        in_specs=[SMEM] * 3 + [ANY] * 7,
+        in_specs=[SMEM] * 2 + [ANY] * 7,
         out_specs=[VMEM] * 2,
         scratch_shapes=[pltpu.SemaphoreType.DMA((count,))],
         compiler_params=params(60),
         cost_estimate=cost(0, 2 * received[0].size),
-    )(lists, positions, at, *pieces, *received)
+    )(lists, at, *pieces, *received)
 
 
 def lora_kernel(at, hidden, back, mine, other, out, maps):
@@ -405,14 +417,14 @@
     )(at, hidden, back, *pieces, *after)
 
 
-def collect_kernel(lists, positions, at, p0, p1, p2, p3, *rest):
+def collect_kernel(lists, at, p0, p1, p2, p3, *rest):
     o0, o1, o2, o3, total, held, sems = rest[-7:]
     line, cross, core = at[0], at[1], at[2]
     slots = o0.shape[0]
     found = []
     for i, piece in enumerate((p0, p1, p2, p3)):
         for b in range(piece.shape[0]):
-            on_line, on_cross, local = placed(positions[lists[2 * i + b // 4, b % 4]], core)
+            on_line, on_cross, local = placed(listed(lists, i, b), core)
             n = len(found)
             found.append((on_cross == cross, on_line * slots + local))
 
@@ -433,12 +445,12 @@
         out[...] = total[pl.ds(target * slots, slots)].astype(bf16)
 
 
-def collect(lists, positions, at, pieces, slots, after):
+def collect(lists, at, pieces, slots, after):
     count, both, wide = pieces[0].shape
     return pl.pallas_call(
         collect_kernel,
         out_shape=[jax.ShapeDtypeStruct((slots, both, wide), bf16)] * 4,
-        in_specs=[SMEM] * 3 + [ANY] * (4 + len(after)),
+        in_specs=[SMEM] * 2 + [ANY] * (4 + len(after)),
         out_specs=[VMEM] * 4,
         scratch_shapes=[
             pltpu.VMEM((4 * slots, both, wide), f32),
@@ -447,7 +459,7 @@
         ],
         compiler_params=params(60),
         cost_estimate=cost(8 * pieces[0].size, 16 * pieces[0].size),
-    )(lists, positions, at, *pieces, *after)
+    )(lists, at, *pieces, *after)
 
 
 def turn_kernel(tables, key_grad, value_grad, back):
@@ -470,22 +482,35 @@
     )(tables, key_grad, value_grad)
 
 
-def send_kernel(at, keys, values, near, far, done, sems):
-    done[...] = jnp.zeros_like(done)
+def send_kernel(at, keys, values, near, far, done, held, sems):
     core, z = at[2], at[3]
     width = far.shape[0]
+    size = held.shape[1]
+    parts = width // size
+    done[...] = jnp.zeros_like(done)
 
     def copies(mine, theirs, shift):
-        rows = pl.ds(pl.multiple_of(((z + shift + SIDE) % SIDE) * width, 256), width)
-        across = pl.ds(pl.multiple_of(((z + 2) % SIDE) * width, 256), width)
-        found = [
-            pltpu.make_async_copy(mine.at[rows], near.at[0], sems.at[0]),
-            pltpu.make_async_copy(theirs.at[rows], near.at[1], sems.at[1]),
-            pltpu.make_async_copy(mine.at[across], far, sems.at[2]),
-        ]
-        for copy in found:
+        rows = ((z + shift + SIDE) % SIDE) * width
+        across = ((z + 2) % SIDE) * width
+        loads, saves = [], []
+        for source, start, target in (
+            (mine, rows, near.at[0]), (theirs, rows, near.at[1]), (mine, across, far)
+        ):
+            for i in range(parts):
+                n = len(loads)
+                here = pl.ds(pl.multiple_of(start + i * size, 256), size)
+                loads.append(pltpu.make_async_copy(source.at[here], held.at[n], sems.at[0, n]))
+                saves.append(
+                    pltpu.make_async_copy(
+                        held.at[n], target.at[pl.ds(i * size, size)], sems.at[1, n]
+                    )
+                )
+        for copy in loads:
             copy.start()
-        for copy in found:
+        for load, save in zip(loads, saves):
+            load.wait()
+            save.start()
+        for copy in saves:
             copy.wait()
 
     pl.when(core == 0)(lambda: copies(keys, values, 1))
@@ -494,6 +519,7 @@
 
 def to_send(at, keys, values):
     rows, kv = keys.shape[0] // SIDE, keys.shape[1]
+    size = rows // 4
     return pl.pallas_call(
         send_kernel,
         out_shape=[
@@ -502,9 +528,9 @@
             TOKEN,
         ],
         in_specs=[SMEM] + [ANY] * 2,
-        out_specs=[VMEM] * 3,
-        scratch_shapes=[pltpu.SemaphoreType.DMA((3,))],
-        compiler_params=params(60),
+        out_specs=[ANY] * 2 + [VMEM],
+        scratch_shapes=[pltpu.VMEM((12, size, kv), bf16), pltpu.SemaphoreType.DMA((2, 12))],
+        compiler_params=params(63),
         cost_estimate=cost(0, 12 * rows * kv),
     )(at, keys, values)
 
@@ -751,6 +777,7 @@
     sent_near, sent_far, sent_done = to_send(at, key_weight_frozen, value_weight_frozen)
     mine_half, give_half = split_maps(
         block_adapter_index,
+        adapter_position,
         at,
         adapter_down_maps.reshape(slots_here, both, width),
         adapter_up_maps.reshape(slots_here, both, kv_here),
@@ -763,13 +790,13 @@
     segments, _ = lax.optimization_barrier((segment_document_index, maps_chip))
     tables = rope_tables(segments)
     back = turn(tables, key_gradient, value_gradient)
-    picked = pick(lists, adapter_position, at, maps_line, half, blocks, (back,))
+    picked = pick(lists, at, maps_line, half, blocks, (back,))
     received = [along_cross(p, d) for p, d in zip(picked, SHIFTS)]
 
     near = along_z_apart(sent_near, 1)
     sent_far, _ = lax.optimization_barrier((sent_far, lists_here))
     far = along_z(sent_far, 2)
-    mine_maps, give_maps = resolve(lists, adapter_position, at, maps_line, received)
+    mine_maps, give_maps = resolve(lists, at, maps_line, received)
     into, maps = lora(at, hidden, back, mine_maps, to_other_core(give_maps))
     near, far, _ = lax.optimization_barrier((near, far, into))
     pieces = [near, to_other_core(near), far, to_other_core(far)]
@@ -786,7 +813,7 @@
     back_later, _ = lax.optimization_barrier((back, forward_done))
     backs = [back, along_z_apart(back, 1), along_z_apart(back, -1), along_z(back_later, 2)]
     line_sums = collect(
-        lists, adapter_position, at, part_from, 2 * slots_here, [forward_done] + backs[1:3]
+        lists, at, part_from, 2 * slots_here, [forward_done] + backs[1:3]
     )
     arrived = [line_sums[0]] + [along_line(s, d) for s, d in zip(line_sums[1:], SHIFTS)]
     key_terms = [
@@ -796,7 +823,8 @@
         along_z(partial[3], 2),
     ]
     hidden_gradient, backward_done = backward(
-        at, backs, key_weight_frozen, value_weight_frozen, pieces, sums, maps, line_sums[:1]
+        at, backs, key_weight_frozen, value_weight_frozen, pieces, sums, maps,
+        line_sums[:1],
     )
     grad_down, grad_up = gather_sums(at, arrived, slots_here, width, (backward_done,))
     key_out, value_out = finish(at, sums, maps, tables, key_terms, grad_up)

time: 127 us -> 128 us (level)
  waiting for transfers between devices: 34.2 us -> 36 us
    ppermute x30, waiting for transfers between devices: 34.2 us -> 36 us  [exchange(): return lax.ppermute(array, ('dp', 'tensor'), pairs)]
    unnamed x70 -> x76, local copies, waits for them, and re-layouts: 6.46 us -> 6.8 us
  transfers between devices with their start and end apart: 30 -> 30, of which waited for: 13 -> 14; matrix products, arithmetic and copies ran while one was open for 2% -> 2% of each run, Pallas kernels for 26% -> 25%
where the time goes in v5:
time: 128 us; the launch traced here: 127 us
  Pallas kernels  40.5 us (32%)
  starting transfers between devices  38.9 us (30%)
  waiting for transfers between devices  36 us (28%)
  local copies, waits for them, and re-layouts  7.57 us (6%)
  other arithmetic  2.36 us (2%)
  between operations  1.81 us (1%)
    ppermute x30, starting transfers between devices, exchange(): return lax.ppermute(array, ('dp', 'tensor'), pairs)  38.9 us
    ppermute x30, waiting for transfers between devices, exchange(): return lax.ppermute(array, ('dp', 'tensor'), pairs)  36 us
    pallas_call x1, Pallas kernels, backward(): pl.pallas_call(backward_kernel, out_shape=[jax.ShapeDtypeStruct((rows, wi...  10.6 us
    pallas_call x1, Pallas kernels, forward(): pl.pallas_call(forward_kernel, out_shape=[out] * 4 + [TOKEN], in_specs=[S...  8.03 us
    unnamed x76, local copies, waits for them, and re-layouts  6.8 us
    pallas_call x1, Pallas kernels, to_send(): pl.pallas_call(send_kernel, out_shape=[jax.ShapeDtypeStruct((2, rows, kv)...  4.2 us
    pallas_call x1, Pallas kernels, collect(): pl.pallas_call(collect_kernel, out_shape=[jax.ShapeDtypeStruct((slots, bo...  3.34 us
    pallas_call x1, Pallas kernels, pick(): pl.pallas_call(pick_kernel, out_shape=[out] * 3, in_specs=[SMEM] * 2 + [A...  3.11 us
  transfers between devices with their start and end apart: 30, of which 14 were waited for; matrix products, arithmetic and copies ran while one was open for 2% of the time, Pallas kernels for 25%

profile of v5, /device:TPU:1, one launch (start us, length us, event | category | flops | bytes accessed | tf_op | source)
XLA Modules:
  0.0 127.1 jit_solution(7900024719891854580)
XLA Ops:
  1.4 4.2 %shard_map.137 = (bf16[2,2048,256]{2,1,0:T(8,128)(2,1)}, bf16[2048,256]{1,0:T(8,128)(2,1)}, f32[8,128]{1,0:T(8,128)}) custom-call(s32[4]{0:T(128)} %pad_add_fusion.at, bf16[8192,256]{1,0:T(8,128)(2,1)} %keys.5, bf16[8192,256]{1,0:T(8,128)(2,1)} %values.5), custom_call_target="tpu_custom_call" | custom-call | bytes 6291 | tf_op jit(solution)/shard_map/pallas_call | solution.py:523
  8.6 3.8 %collective-permute-start.12 = (bf16[2,2048,256]{2,1,0:T(8,128)(2,1)}, bf16[2,2048,256]{2,1,0:T(8,128)(2,1)}, u32[]{:S(2)}, u32[]{:S(2)}) collective-permute-start(bf16[2,2048,256]{2,1,0:T(8,128)(2,1)} %get-tuple-element.51), channel_id=1, source_target_pairs={{0,1},{1,2},{2,3},{3,0},{4,7},{5,4},{6,5},{7,6},{8,9},{9,10},{10,1... | collective-permute-start | bytes 6291464 | tf_op jit(solution)/shard_map/ppermute | solution.py:36
  13.0 3.0 %collective-permute-start.3 = (bf16[4,32,1280]{2,1,0:T(8,128)(2,1)S(1)}, bf16[4,32,1280]{2,1,0:T(8,128)(2,1)S(1)}, u32[]{:S(2)}, u32[]{:S(2)}) collective-permute-start(bf16[4,32,1280]{2,1,0:T(8,128)(2,1)S(1)} %shard_map.139.m0), channel_id=1, source_target_pairs={{0,64},{1,65},{2,66},{3,67},{4,20},{5,21},{6,22},{7,23},{8,72},{9,... | collective-permute-start | bytes 983048 | tf_op jit(solution)/shard_map/ppermute | solution.py:36
  20.5 4.3 %collective-permute-done.2.m2 = bf16[4,32,1280]{2,1,0:T(8,128)(2,1)S(1)} collective-permute-done((bf16[4,32,1280]{2,1,0:T(8,128)(2,1)S(1)}, bf16[4,32,1280]{2,1,0:T(8,128)(2,1)S(1)}, u32[]{:S(2)}, u32[]{:S(2)}) %collective-permute-start.2) | collective-permute-done | bytes 327712 | tf_op jit(solution)/shard_map/ppermute | solution.py:36
  26.7 1.9 %collective-permute-start.4 = (s32[8,128]{1,0:T(8,128)S(1)}, s32[8,128]{1,0:T(8,128)S(1)}, u32[]{:S(2)}, u32[]{:S(2)}) collective-permute-start(s32[8,128]{1,0:T(8,128)S(1)} %shard_map.141), channel_id=1, source_target_pairs={{0,4},{1,5},{2,6},{3,7},{4,0},{5,1},{6,2},{7,3},{8,12},{9,13},{10,... | collective-permute-start | bytes 12296 | tf_op jit(solution)/shard_map/ppermute | solution.py:36
  30.8 3.1 %shard_map.142 = (bf16[8,32,1152]{2,1,0:T(8,128)(2,1)}, bf16[8,32,1152]{2,1,0:T(8,128)(2,1)}, bf16[8,32,1152]{2,1,0:T(8,128)(2,1)}) custom-call(s32[8,128]{1,0:T(8,128)} %copy-done.36, s32[4]{0:T(128)} %pad_add_fusion.at, bf16[4,32,1280]{2,1,0:T(8,128)(2,1)} %copy-done.3, bf16[4,32,1280]{2,1,0:T(8,128)(2,1)} %copy-done.8, bf16[4,32,1280]{2,1,0:T(8,128)(2,1)} %copy-done.7, ...), custom_call_target="tpu_custom_call" | custom-call | bytes 1310 | tf_op jit(solution)/shard_map/pallas_call | solution.py:268
  38.0 6.5 %collective-permute-done.5.r1 = bf16[8,32,1152]{2,1,0:T(8,128)(2,1)S(1)} collective-permute-done((bf16[8,32,1152]{2,1,0:T(8,128)(2,1)}, bf16[8,32,1152]{2,1,0:T(8,128)(2,1)S(1)}, u32[]{:S(2)}, u32[]{:S(2)}) %collective-permute-start.5) | collective-permute-done | bytes 589856 | tf_op jit(solution)/shard_map/ppermute | solution.py:36
  44.5 5.7 %collective-permute-done.6.r2 = bf16[8,32,1152]{2,1,0:T(8,128)(2,1)} collective-permute-done((bf16[8,32,1152]{2,1,0:T(8,128)(2,1)}, bf16[8,32,1152]{2,1,0:T(8,128)(2,1)}, u32[]{:S(2)}, u32[]{:S(2)}) %collective-permute-start.6) | collective-permute-done | bytes 589856 | tf_op jit(solution)/shard_map/ppermute | solution.py:36
  51.5 2.8 %shard_map.143 = (bf16[4,32,1152]{2,1,0:T(8,128)(2,1)}, bf16[4,32,1152]{2,1,0:T(8,128)(2,1)}) custom-call(s32[8,128]{1,0:T(8,128)} %copy-done.36, s32[4]{0:T(128)} %pad_add_fusion.at, bf16[4,32,1280]{2,1,0:T(8,128)(2,1)} %copy-done.3, bf16[4,32,1280]{2,1,0:T(8,128)(2,1)} %copy-done.8, bf16[4,32,1280]{2,1,0:T(8,128)(2,1)} %copy-done.7, ...), custom_call_target="tpu_custom_call" | custom-call | bytes 589 | tf_op jit(solution)/shard_map/pallas_call | solution.py:313
  61.2 2.0 %collective-permute-start.10 = (bf16[64,512]{1,0:T(8,128)(2,1)S(1)}, bf16[64,512]{1,0:T(8,128)(2,1)S(1)}, u32[]{:S(2)}, u32[]{:S(2)}) collective-permute-start(bf16[64,512]{1,0:T(8,128)(2,1)S(1)} %get-tuple-element.50.t0), channel_id=1, source_target_pairs={{0,3},{1,0},{2,1},{3,2},{4,7},{5,4},{6,5},{7,6},{8,11},{9,8},{10,9... | collective-permute-start | bytes 196616 | tf_op jit(solution)/shard_map/ppermute | solution.py:36
  63.2 2.5 %collective-permute-done.11.t3 = bf16[64,512]{1,0:T(8,128)(2,1)S(1)} collective-permute-done((bf16[64,512]{1,0:T(8,128)(2,1)S(1)}, bf16[64,512]{1,0:T(8,128)(2,1)S(1)}, u32[]{:S(2)}, u32[]{:S(2)}) %collective-permute-start.11) | collective-permute-done | bytes 65568 | tf_op jit(solution)/shard_map/ppermute | solution.py:36
  67.6 1.9 %shard_map.145 = (bf16[4,32,1152]{2,1,0:T(8,128)(2,1)S(1)}, bf16[4,32,1152]{2,1,0:T(8,128)(2,1)S(1)}, bf16[64,512]{1,0:T(8,128)(2,1)S(1)}, bf16[2,512,256]{2,1,0:T(8,128)(2,1)}) custom-call(s32[4]{0:T(128)S(1)} %copy-done.23, bf16[512,2048]{1,0:T(8,128)(2,1)S(1)} %copy-done, bf16[2,512,256]{2,1,0:T(8,128)(2,1)S(1)} %copy-done.2, ...), custom_call_target="tpu_custom_call" | custom-call | flops 67108 | bytes 4194 | tf_op jit(solution)/shard_map/pallas_call | solution.py:404
  69.5 2.0 %collective-permute-start.16 = (bf16[4,32,1152]{2,1,0:T(8,128)(2,1)S(1)}, bf16[4,32,1152]{2,1,0:T(8,128)(2,1)S(1)}, u32[]{:S(2)}, u32[]{:S(2)}) collective-permute-start(bf16[4,32,1152]{2,1,0:T(8,128)(2,1)S(1)} %get-tuple-element.58), channel_id=1, source_target_pairs={{0,4},{1,5},{2,6},{3,7},{4,0},{5,1},{6,2},{7,3},{8,12},{9,13},{10,... | collective-permute-start | bytes 884744 | tf_op jit(solution)/shard_map/ppermute | solution.py:36
  71.5 2.7 %collective-permute-start.23 = (bf16[2,512,256]{2,1,0:T(8,128)(2,1)}, bf16[2,512,256]{2,1,0:T(8,128)(2,1)S(1)}, u32[]{:S(2)}, u32[]{:S(2)}) collective-permute-start(bf16[2,512,256]{2,1,0:T(8,128)(2,1)} %get-tuple-element.70.b0), channel_id=1, source_target_pairs={{0,1},{1,2},{2,3},{3,0},{4,7},{5,4},{6,5},{7,6},{8,9},{9,10},{10,1... | collective-permute-start | bytes 1572872 | tf_op jit(solution)/shard_map/ppermute | solution.py:36
  74.3 2.3 %collective-permute-start.22 = (bf16[8,32,1152]{2,1,0:T(8,128)(2,1)S(1)}, bf16[8,32,1152]{2,1,0:T(8,128)(2,1)S(1)}, u32[]{:S(2)}, u32[]{:S(2)}) collective-permute-start(bf16[8,32,1152]{2,1,0:T(8,128)(2,1)S(1)} %shard_map.146._.p0), channel_id=1, source_target_pairs={{0,16},{1,17},{2,18},{3,19},{4,68},{5,69},{6,70},{7,71},{8,24},{9,... | collective-permute-start | bytes 1769480 | tf_op jit(solution)/shard_map/ppermute | solution.py:36
  78.1 8.0 %shard_map.147 = (bf16[2,512,256]{2,1,0:T(8,128)(2,1)S(1)}, bf16[2,512,256]{2,1,0:T(8,128)(2,1)}, bf16[2,512,256]{2,1,0:T(8,128)(2,1)}, bf16[2,512,256]{2,1,0:T(8,128)(2,1)}, f32[8,128]{1,0:T(8,128)S(1)}) custom-call(s32[4]{0:T(128)S(1)} %copy-done.23, bf16[512,2048]{1,0:T(8,128)(2,1)S(1)} %copy-done, bf16[8192,256]{1,0:T(8,128)(2,1)} %keys.5, ...), custom_call_target="tpu_custom_call" | custom-call | flops 8589934592 | bytes 16777216 | tf_op jit(solution)/shard_map/pallas_call | solution.py:592
  86.8 4.3 %collective-permute-done.21.p2 = bf16[8,32,1152]{2,1,0:T(8,128)(2,1)S(1)} collective-permute-done((bf16[8,32,1152]{2,1,0:T(8,128)(2,1)S(1)}, bf16[8,32,1152]{2,1,0:T(8,128)(2,1)S(1)}, u32[]{:S(2)}, u32[]{:S(2)}) %collective-permute-start.21) | collective-permute-done | bytes 589856 | tf_op jit(solution)/shard_map/ppermute | solution.py:36
  92.0 3.3 %shard_map.148 = (bf16[4,32,1152]{2,1,0:T(8,128)(2,1)}, bf16[4,32,1152]{2,1,0:T(8,128)(2,1)}, bf16[4,32,1152]{2,1,0:T(8,128)(2,1)}, bf16[4,32,1152]{2,1,0:T(8,128)(2,1)}) custom-call(s32[8,128]{1,0:T(8,128)} %copy-done.36, s32[4]{0:T(128)} %pad_add_fusion.at, bf16[8,32,1152]{2,1,0:T(8,128)(2,1)} %copy-done.9, ...), custom_call_target="tpu_custom_call" | custom-call | flops 2359 | bytes 4718 | tf_op jit(solution)/shard_map/pallas_call | solution.py:450
  96.6 2.7 %collective-permute-start.18 = (bf16[2,512,256]{2,1,0:T(8,128)(2,1)}, bf16[2,512,256]{2,1,0:T(8,128)(2,1)S(1)}, u32[]{:S(2)}, u32[]{:S(2)}) collective-permute-start(bf16[2,512,256]{2,1,0:T(8,128)(2,1)} %get-tuple-element.62), channel_id=1, source_target_pairs={{0,1},{1,2},{2,3},{3,0},{4,7},{5,4},{6,5},{7,6},{8,9},{9,10},{10,1... | collective-permute-start | bytes 1572872 | tf_op jit(solution)/shard_map/ppermute | solution.py:36
  99.3 2.7 %collective-permute-done.28.b3 = bf16[2,512,256]{2,1,0:T(8,128)(2,1)} collective-permute-done((bf16[2,512,256]{2,1,0:T(8,128)(2,1)}, bf16[2,512,256]{2,1,0:T(8,128)(2,1)}, u32[]{:S(2)}, u32[]{:S(2)}) %collective-permute-start.28) | collective-permute-done | bytes 524320 | tf_op jit(solution)/shard_map/ppermute | solution.py:36
  102.1 1.9 %collective-permute-start.26 = (bf16[4,32,1152]{2,1,0:T(8,128)(2,1)}, bf16[4,32,1152]{2,1,0:T(8,128)(2,1)S(1)}, u32[]{:S(2)}, u32[]{:S(2)}) collective-permute-start(bf16[4,32,1152]{2,1,0:T(8,128)(2,1)} %get-tuple-element.68), channel_id=1, source_target_pairs={{0,96},{1,97},{2,98},{3,99},{4,28},{5,29},{6,30},{7,31},{8,104},{9... | collective-permute-start | bytes 884744 | tf_op jit(solution)/shard_map/ppermute | solution.py:36
  105.1 10.6 %shard_map.149 = (bf16[512,2048]{1,0:T(8,128)(2,1)}, f32[8,128]{1,0:T(8,128)}) custom-call(s32[4]{0:T(128)} %pad_add_fusion.at, bf16[2,512,256]{2,1,0:T(8,128)(2,1)} %get-tuple-element.70.b0, bf16[2,512,256]{2,1,0:T(8,128)(2,1)} %copy-done.35, bf16[2,512,256]{2,1,0:T(8,128)(2,1)} %copy-done.34, bf16[2,512,256]{2,1,0:T(8,128)(2,1)} %collective-permute-done.28.b3, ...), custom_call_target="tpu_custom_call" | custom-call | flops 12884901888 | bytes 16777216 | tf_op jit(solution)/shard_map/pallas_call | solution.py:650
  116.7 1.9 %collective-permute-start.29 = (f32[2,32,1152]{2,1,0:T(8,128)S(1)}, f32[2,32,1152]{2,1,0:T(8,128)S(1)}, u32[]{:S(2)}, u32[]{:S(2)}) collective-permute-start(f32[2,32,1152]{2,1,0:T(8,128)S(1)} %shard_map.150), channel_id=1, source_target_pairs={{0,4},{1,5},{2,6},{3,7},{4,0},{5,1},{6,2},{7,3},{8,12},{9,13},{10,... | collective-permute-start | bytes 884744 | tf_op jit(solution)/shard_map/ppermute | solution.py:36
  122.2 2.3 %collective-permute-done.19.t3 = bf16[2,512,256]{2,1,0:T(8,128)(2,1)S(1)} collective-permute-done((bf16[2,512,256]{2,1,0:T(8,128)(2,1)}, bf16[2,512,256]{2,1,0:T(8,128)(2,1)S(1)}, u32[]{:S(2)}, u32[]{:S(2)}) %collective-permute-start.19) | collective-permute-done | bytes 524320 | tf_op jit(solution)/shard_map/ppermute | solution.py:36
  (141 shorter events, 38.9 us)
Async XLA Ops:
  7.1 5.4 %collective-permute-start = (bf16[2,32,1280]{2,1,0:T(8,128)(2,1)S(1)}, bf16[2,32,1280]{2,1,0:T(8,128)(2,1)S(1)}, u32[]{:S(2)}, u32[]{:S(2)}) collective-permute-start(bf16[2,32,1280]{2,1,0:T(8,128)(2,1)S(1)} %get-tuple-element.43), channel_id=1, source_target_pairs={{0,4},{1,5},{2,6},{3,7},{4,0},{5,1},{6,2},{7,3},{8,12},{9,13},{10,... | collective-permute-start | bytes 491528 | tf_op jit(solution)/shard_map/ppermute | solution.py:36
  8.6 51.3 %collective-permute-start.12 = (bf16[2,2048,256]{2,1,0:T(8,128)(2,1)}, bf16[2,2048,256]{2,1,0:T(8,128)(2,1)}, u32[]{:S(2)}, u32[]{:S(2)}) collective-permute-start(bf16[2,2048,256]{2,1,0:T(8,128)(2,1)} %get-tuple-element.51), channel_id=1, source_target_pairs={{0,1},{1,2},{2,3},{3,0},{4,7},{5,4},{6,5},{7,6},{8,9},{9,10},{10,1... | collective-permute-start | bytes 6291464 | tf_op jit(solution)/shard_map/ppermute | solution.py:36
  13.0 7.5 %collective-permute-start.3 = (bf16[4,32,1280]{2,1,0:T(8,128)(2,1)S(1)}, bf16[4,32,1280]{2,1,0:T(8,128)(2,1)S(1)}, u32[]{:S(2)}, u32[]{:S(2)}) collective-permute-start(bf16[4,32,1280]{2,1,0:T(8,128)(2,1)S(1)} %shard_map.139.m0), channel_id=1, source_target_pairs={{0,64},{1,65},{2,66},{3,67},{4,20},{5,21},{6,22},{7,23},{8,72},{9,... | collective-permute-start | bytes 983048 | tf_op jit(solution)/shard_map/ppermute | solution.py:36
  16.0 8.8 %collective-permute-start.2 = (bf16[4,32,1280]{2,1,0:T(8,128)(2,1)S(1)}, bf16[4,32,1280]{2,1,0:T(8,128)(2,1)S(1)}, u32[]{:S(2)}, u32[]{:S(2)}) collective-permute-start(bf16[4,32,1280]{2,1,0:T(8,128)(2,1)S(1)} %shard_map.139.m0), channel_id=1, source_target_pairs={{0,96},{1,97},{2,98},{3,99},{4,28},{5,29},{6,30},{7,31},{8,104},{9... | collective-permute-start | bytes 983048 | tf_op jit(solution)/shard_map/ppermute | solution.py:36
  16.7 8.0 %collective-permute-start.1 = (bf16[4,32,1280]{2,1,0:T(8,128)(2,1)S(1)}, bf16[4,32,1280]{2,1,0:T(8,128)(2,1)S(1)}, u32[]{:S(2)}, u32[]{:S(2)}) collective-permute-start(bf16[4,32,1280]{2,1,0:T(8,128)(2,1)S(1)} %shard_map.139.m0), channel_id=1, source_target_pairs={{0,32},{1,33},{2,34},{3,35},{4,12},{5,13},{6,14},{7,15},{8,40},{9,... | collective-permute-start | bytes 983048 | tf_op jit(solution)/shard_map/ppermute | solution.py:36
  24.9 35.0 %collective-permute-start.13 = (bf16[2048,256]{1,0:T(8,128)(2,1)}, bf16[2048,256]{1,0:T(8,128)(2,1)}, u32[]{:S(2)}, u32[]{:S(2)}) collective-permute-start(bf16[2048,256]{1,0:T(8,128)(2,1)} %get-tuple-element.53), channel_id=1, source_target_pairs={{0,2},{1,3},{2,0},{3,1},{4,6},{5,7},{6,4},{7,5},{8,10},{9,11},{10,... | collective-permute-start | bytes 3145736 | tf_op jit(solution)/shard_map/ppermute | solution.py:36
  34.0 10.5 %collective-permute-start.5 = (bf16[8,32,1152]{2,1,0:T(8,128)(2,1)}, bf16[8,32,1152]{2,1,0:T(8,128)(2,1)S(1)}, u32[]{:S(2)}, u32[]{:S(2)}) collective-permute-start(bf16[8,32,1152]{2,1,0:T(8,128)(2,1)} %get-tuple-element.45), channel_id=1, source_target_pairs={{0,8},{1,9},{2,10},{3,11},{4,36},{5,37},{6,38},{7,39},{8,16},{9,17... | collective-permute-start | bytes 1769480 | tf_op jit(solution)/shard_map/ppermute | solution.py:36
  35.0 15.2 %collective-permute-start.6 = (bf16[8,32,1152]{2,1,0:T(8,128)(2,1)}, bf16[8,32,1152]{2,1,0:T(8,128)(2,1)}, u32[]{:S(2)}, u32[]{:S(2)}) collective-permute-start(bf16[8,32,1152]{2,1,0:T(8,128)(2,1)} %get-tuple-element.46), channel_id=1, source_target_pairs={{0,24},{1,25},{2,26},{3,27},{4,100},{5,101},{6,102},{7,103},{8,0},... | collective-permute-start | bytes 1769480 | tf_op jit(solution)/shard_map/ppermute | solution.py:36
  36.7 14.8 %collective-permute-start.7 = (bf16[8,32,1152]{2,1,0:T(8,128)(2,1)}, bf16[8,32,1152]{2,1,0:T(8,128)(2,1)}, u32[]{:S(2)}, u32[]{:S(2)}) collective-permute-start(bf16[8,32,1152]{2,1,0:T(8,128)(2,1)} %get-tuple-element.47), channel_id=1, source_target_pairs={{0,16},{1,17},{2,18},{3,19},{4,68},{5,69},{6,70},{7,71},{8,24},{9,... | collective-permute-start | bytes 1769480 | tf_op jit(solution)/shard_map/ppermute | solution.py:36
  59.9 7.7 %collective-permute-start.14 = (bf16[2,2048,256]{2,1,0:T(8,128)(2,1)}, bf16[2,2048,256]{2,1,0:T(8,128)(2,1)S(1)}, u32[]{:S(2)}, u32[]{:S(2)}) collective-permute-start(bf16[2,2048,256]{2,1,0:T(8,128)(2,1)} %collective-permute-done.12.near), channel_id=1, source_target_pairs={{0,4},{1,5},{2,6},{3,7},{4,0},{5,1},{6,2},{7,3},{8,12},{9,13},{10,... | collective-permute-start | bytes 6291464 | tf_op jit(solution)/shard_map/ppermute | solution.py:36
  61.1 6.5 %collective-permute-start.15 = (bf16[2048,256]{1,0:T(8,128)(2,1)}, bf16[2048,256]{1,0:T(8,128)(2,1)S(1)}, u32[]{:S(2)}, u32[]{:S(2)}) collective-permute-start(bf16[2048,256]{1,0:T(8,128)(2,1)} %collective-permute-done.13.far), channel_id=1, source_target_pairs={{0,4},{1,5},{2,6},{3,7},{4,0},{5,1},{6,2},{7,3},{8,12},{9,13},{10,... | collective-permute-start | bytes 3145736 | tf_op jit(solution)/shard_map/ppermute | solution.py:36
  61.2 4.9 %collective-permute-start.10 = (bf16[64,512]{1,0:T(8,128)(2,1)S(1)}, bf16[64,512]{1,0:T(8,128)(2,1)S(1)}, u32[]{:S(2)}, u32[]{:S(2)}) collective-permute-start(bf16[64,512]{1,0:T(8,128)(2,1)S(1)} %get-tuple-element.50.t0), channel_id=1, source_target_pairs={{0,3},{1,0},{2,1},{3,2},{4,7},{5,4},{6,5},{7,6},{8,11},{9,8},{10,9... | collective-permute-start | bytes 196616 | tf_op jit(solution)/shard_map/ppermute | solution.py:36
  71.5 15.2 %collective-permute-start.24 = (bf16[2,512,256]{2,1,0:T(8,128)(2,1)}, bf16[2,512,256]{2,1,0:T(8,128)(2,1)S(1)}, u32[]{:S(2)}, u32[]{:S(2)}) collective-permute-start(bf16[2,512,256]{2,1,0:T(8,128)(2,1)} %get-tuple-element.70.b0), channel_id=1, source_target_pairs={{0,3},{1,0},{2,1},{3,2},{4,5},{5,6},{6,7},{7,4},{8,11},{9,8},{10,9... | collective-permute-start | bytes 1572872 | tf_op jit(solution)/shard_map/ppermute | solution.py:36
  71.5 15.2 %collective-permute-start.23 = (bf16[2,512,256]{2,1,0:T(8,128)(2,1)}, bf16[2,512,256]{2,1,0:T(8,128)(2,1)S(1)}, u32[]{:S(2)}, u32[]{:S(2)}) collective-permute-start(bf16[2,512,256]{2,1,0:T(8,128)(2,1)} %get-tuple-element.70.b0), channel_id=1, source_target_pairs={{0,1},{1,2},{2,3},{3,0},{4,7},{5,4},{6,5},{7,6},{8,9},{9,10},{10,1... | collective-permute-start | bytes 1572872 | tf_op jit(solution)/shard_map/ppermute | solution.py:36
  74.3 12.4 %collective-permute-start.22 = (bf16[8,32,1152]{2,1,0:T(8,128)(2,1)S(1)}, bf16[8,32,1152]{2,1,0:T(8,128)(2,1)S(1)}, u32[]{:S(2)}, u32[]{:S(2)}) collective-permute-start(bf16[8,32,1152]{2,1,0:T(8,128)(2,1)S(1)} %shard_map.146._.p0), channel_id=1, source_target_pairs={{0,16},{1,17},{2,18},{3,19},{4,68},{5,69},{6,70},{7,71},{8,24},{9,... | collective-permute-start | bytes 1769480 | tf_op jit(solution)/shard_map/ppermute | solution.py:36
  76.6 14.5 %collective-permute-start.21 = (bf16[8,32,1152]{2,1,0:T(8,128)(2,1)S(1)}, bf16[8,32,1152]{2,1,0:T(8,128)(2,1)S(1)}, u32[]{:S(2)}, u32[]{:S(2)}) collective-permute-start(bf16[8,32,1152]{2,1,0:T(8,128)(2,1)S(1)} %shard_map.146._.p0), channel_id=1, source_target_pairs={{0,24},{1,25},{2,26},{3,27},{4,100},{5,101},{6,102},{7,103},{8,0},... | collective-permute-start | bytes 1769480 | tf_op jit(solution)/shard_map/ppermute | solution.py:36
  77.6 14.4 %collective-permute-start.20 = (bf16[8,32,1152]{2,1,0:T(8,128)(2,1)S(1)}, bf16[8,32,1152]{2,1,0:T(8,128)(2,1)}, u32[]{:S(2)}, u32[]{:S(2)}) collective-permute-start(bf16[8,32,1152]{2,1,0:T(8,128)(2,1)S(1)} %shard_map.146._.p0), channel_id=1, source_target_pairs={{0,8},{1,9},{2,10},{3,11},{4,36},{5,37},{6,38},{7,39},{8,16},{9,17... | collective-permute-start | bytes 1769480 | tf_op jit(solution)/shard_map/ppermute | solution.py:36
  86.7 15.3 %collective-permute-start.28 = (bf16[2,512,256]{2,1,0:T(8,128)(2,1)}, bf16[2,512,256]{2,1,0:T(8,128)(2,1)}, u32[]{:S(2)}, u32[]{:S(2)}) collective-permute-start(bf16[2,512,256]{2,1,0:T(8,128)(2,1)} %get-tuple-element.70.b0), channel_id=1, source_target_pairs={{0,2},{1,3},{2,0},{3,1},{4,6},{5,7},{6,4},{7,5},{8,10},{9,11},{10,... | collective-permute-start | bytes 1572872 | tf_op jit(solution)/shard_map/ppermute | solution.py:36
  95.4 8.6 %collective-permute-start.25 = (bf16[4,32,1152]{2,1,0:T(8,128)(2,1)}, bf16[4,32,1152]{2,1,0:T(8,128)(2,1)S(1)}, u32[]{:S(2)}, u32[]{:S(2)}) collective-permute-start(bf16[4,32,1152]{2,1,0:T(8,128)(2,1)} %get-tuple-element.67), channel_id=1, source_target_pairs={{0,32},{1,33},{2,34},{3,35},{4,12},{5,13},{6,14},{7,15},{8,40},{9,... | collective-permute-start | bytes 884744 | tf_op jit(solution)/shard_map/ppermute | solution.py:36
  96.6 24.6 %collective-permute-start.17 = (bf16[2,512,256]{2,1,0:T(8,128)(2,1)}, bf16[2,512,256]{2,1,0:T(8,128)(2,1)S(1)}, u32[]{:S(2)}, u32[]{:S(2)}) collective-permute-start(bf16[2,512,256]{2,1,0:T(8,128)(2,1)} %get-tuple-element.61), channel_id=1, source_target_pairs={{0,3},{1,0},{2,1},{3,2},{4,5},{5,6},{6,7},{7,4},{8,11},{9,8},{10,9... | collective-permute-start | bytes 1572872 | tf_op jit(solution)/shard_map/ppermute | solution.py:36
  96.6 25.5 %collective-permute-start.18 = (bf16[2,512,256]{2,1,0:T(8,128)(2,1)}, bf16[2,512,256]{2,1,0:T(8,128)(2,1)S(1)}, u32[]{:S(2)}, u32[]{:S(2)}) collective-permute-start(bf16[2,512,256]{2,1,0:T(8,128)(2,1)} %get-tuple-element.62), channel_id=1, source_target_pairs={{0,1},{1,2},{2,3},{3,0},{4,7},{5,4},{6,5},{7,6},{8,9},{9,10},{10,1... | collective-permute-start | bytes 1572872 | tf_op jit(solution)/shard_map/ppermute | solution.py:36
  99.3 25.1 %collective-permute-start.19 = (bf16[2,512,256]{2,1,0:T(8,128)(2,1)}, bf16[2,512,256]{2,1,0:T(8,128)(2,1)S(1)}, u32[]{:S(2)}, u32[]{:S(2)}) collective-permute-start(bf16[2,512,256]{2,1,0:T(8,128)(2,1)} %get-tuple-element.63), channel_id=1, source_target_pairs={{0,2},{1,3},{2,0},{3,1},{4,6},{5,7},{6,4},{7,5},{8,10},{9,11},{10,... | collective-permute-start | bytes 1572872 | tf_op jit(solution)/shard_map/ppermute | solution.py:36
  102.1 13.7 %collective-permute-start.26 = (bf16[4,32,1152]{2,1,0:T(8,128)(2,1)}, bf16[4,32,1152]{2,1,0:T(8,128)(2,1)S(1)}, u32[]{:S(2)}, u32[]{:S(2)}) collective-permute-start(bf16[4,32,1152]{2,1,0:T(8,128)(2,1)} %get-tuple-element.68), channel_id=1, source_target_pairs={{0,96},{1,97},{2,98},{3,99},{4,28},{5,29},{6,30},{7,31},{8,104},{9... | collective-permute-start | bytes 884744 | tf_op jit(solution)/shard_map/ppermute | solution.py:36
  103.9 11.9 %collective-permute-start.27 = (bf16[4,32,1152]{2,1,0:T(8,128)(2,1)}, bf16[4,32,1152]{2,1,0:T(8,128)(2,1)S(1)}, u32[]{:S(2)}, u32[]{:S(2)}) collective-permute-start(bf16[4,32,1152]{2,1,0:T(8,128)(2,1)} %get-tuple-element.69), channel_id=1, source_target_pairs={{0,64},{1,65},{2,66},{3,67},{4,20},{5,21},{6,22},{7,23},{8,72},{9,... | collective-permute-start | bytes 884744 | tf_op jit(solution)/shard_map/ppermute | solution.py:36
  (44 other events, 346.3 us)
